TPU v7x, 256 devices: a whole 4x4x8 slice. The times are simulated.
256 devices in a mesh: dom: 32 (over y, x, z_hi), band: 8 (over z_lo, core).
Axes of the slice: x: 4, y: 4, z: 8 (z_hi: 2, z_lo: 4; z = z_hi * 4 + z_lo), core: 2. Of those that a mesh axis runs over, the one named last changes fastest.
Arguments:
- wavefunctions: bfloat16 [65536, 1024], P('dom', 'band'), may hold values from -4 to 4
- mass_scale: float32 [65536], P('dom'), may hold values from 0.7 to 1.4
- cell_matrices: bfloat16 [256, 512, 512], P('dom')
- connectivity: int32 [256, 512], P('dom'), may hold values from 0 to 2303, as said below
- face_index: int32 [8192], P('dom'), may hold values from 0 to 2047, as said below
Outputs:
- rotated: float32 [65536, 1024], P('dom', 'band')
Inputs may be any that keep to these rules, and one draw needn't show every extreme that they name: `connectivity`: local numbers of each cell's 512 nodes within its domain: below 2048 the domain's own nodes, from 2048 on the entries of the next domain's face list in order; every local number appears in its domain, and a number may repeat. `face_index`: local numbers of 256 own nodes of each domain, in the order that the previous domain uses; a number may repeat.
All inputs are finite; a program needn't handle non-finite values.
Results may differ from a plain program's by a relative error of at most 0.011.
Values may be sent and summed in bfloat16 or wider, within the bound.
No kernel may reach another device: no remote copies, remote signals or barrier semaphores. Data moves between devices by JAX's collectives and lax.ppermute only.
A program may use at most 64 MiB of HBM per device.

v0:
```python
import functools

import jax
import jax.numpy as jnp
from jax import lax
from jax.sharding import Mesh
from jax.sharding import PartitionSpec as P

STATES = 1024
DEGREE = 3
NS_ITERS = 2
DOM = ("dom_0", "dom_1", "dom_2")
BAND = ("band_0", "band_1")
DOM_BAND = ("dom_0", "dom_1", "dom_2", "band_0", "band_1")


filter_center = 5.0
filter_half = 5.0


def passed_along(value, axis, steps):
    count = lax.axis_size(axis)
    initial, last = (max(0, -steps), min(count, count - steps))
    return lax.ppermute(value, axis, [(source, source + steps) for source in range(initial, last)])


def split_up(array, dim, peers):
    lengths = array.shape
    pieces = array.reshape(*lengths[:dim], peers, lengths[dim] // peers, *lengths[dim + 1 :])
    return jnp.moveaxis(pieces, dim, 0)


def sent_and_summed(array, axis, dim):
    pieces = split_up(array, dim, lax.axis_size(axis))
    arrived = lax.all_to_all(pieces, axis, split_axis=0, concat_axis=0, tiled=True)
    return arrived.sum(axis=0)


def by_axis(array, axes):
    return functools.reduce(lax.psum, axes, array)


def in_one_piece(arrays, axis, dim, along):
    both = jnp.concatenate(arrays, axis=along)
    filled, at, finished = (lax.all_gather(both, axis, axis=dim, tiled=True), 0, [])
    for a in arrays:
        finished.append(lax.slice_in_dim(filled, at, at + a.shape[along], axis=along))
        at += a.shape[along]
    return tuple(finished)


def copy_for_each(array, axis):
    copies = jnp.broadcast_to(array, (lax.axis_size(axis), *array.shape))
    return lax.all_to_all(copies, axis, split_axis=0, concat_axis=0, tiled=True)


def laid_out(pieces, dim):
    lengths = list(pieces.shape[1:])
    lengths[dim] *= pieces.shape[0]
    return jnp.moveaxis(pieces, 0, dim).reshape(lengths)


def gathered_copies(array, axis, dim):
    pieces = copy_for_each(array, axis)
    return laid_out(pieces, dim)


def apply_hamiltonian(vectors, mass_scale, cell_matrices, connectivity, face_index):
    own_nodes, band_width = vectors.shape
    scaled = (mass_scale[:, None] * vectors).astype(jnp.bfloat16)
    face_rows = jnp.take(scaled, face_index, axis=0)
    received = passed_along(face_rows, DOM, -1)
    extended = jnp.concatenate([scaled, received], axis=0)
    gathered = jnp.take(extended, connectivity, axis=0)
    products = jnp.einsum(
        "cij,cjs->cis", cell_matrices, gathered, preferred_element_type=jnp.float32
    )
    assembled = jnp.zeros((extended.shape[0], band_width), jnp.float32)
    assembled = assembled.at[connectivity.reshape(-1)].add(products.reshape(-1, band_width))
    returned = passed_along(assembled[own_nodes:], DOM, 1)
    summed = assembled[:own_nodes].at[face_index].add(returned)
    return mass_scale[:, None] * summed


def on_device(wavefunctions, mass_scale, cell_matrices, connectivity, face_index):
    highest = lax.Precision.HIGHEST

    def hamiltonian(vectors):
        return apply_hamiltonian(vectors, mass_scale, cell_matrices, connectivity, face_index)

    previous = wavefunctions.astype(jnp.float32)
    current = (hamiltonian(previous) - filter_center * previous) / filter_half
    for sweep_index in range(DEGREE - 1):
        following = 2.0 * (hamiltonian(current) - filter_center * current) / filter_half - previous
        previous, current = (current, following)
    own_nodes, band_width = current.shape
    rounded = current.astype(jnp.bfloat16)
    contract_rows = (((0,), (0,)), ((), ()))
    partial_margin = lax.dot_general(
        lax.all_gather(rounded, BAND, axis=1, tiled=True),
        rounded,
        contract_rows,
        preferred_element_type=jnp.float32,
    )
    domains = lax.axis_size(DOM)
    tile_rows = STATES // domains
    dom_position = lax.axis_index(DOM)
    margin_tile = sent_and_summed(partial_margin, DOM, 0)
    margin_tile = margin_tile / (own_nodes * domains)
    row_ids = dom_position * tile_rows + lax.broadcasted_iota(jnp.int32, (tile_rows, band_width), 0)
    col_ids = lax.axis_index(BAND) * band_width + lax.broadcasted_iota(
        jnp.int32, (tile_rows, band_width), 1
    )
    identity = (row_ids == col_ids).astype(jnp.float32)
    trace_part = jnp.sum(margin_tile * identity)
    mean_eigen = by_axis(trace_part, DOM_BAND) / STATES
    current_y = margin_tile / mean_eigen
    current_z = identity
    for ns_index in range(NS_ITERS):
        z_panel, y_panel = tuple(
            (
                part.astype(jnp.float32)
                for part in in_one_piece(
                    (current_z.astype(jnp.bfloat16), current_y.astype(jnp.bfloat16)), BAND, 1, 0
                )
            )
        )
        product = jnp.dot(
            z_panel,
            gathered_copies(current_y, DOM, 0),
            precision=highest,
            preferred_element_type=jnp.float32,
        )
        correction = 1.5 * identity - 0.5 * product
        segment = gathered_copies(correction, DOM, 0)
        new_y = jnp.dot(y_panel, segment, precision=highest, preferred_element_type=jnp.float32)
        new_z = jnp.dot(z_panel, segment, precision=highest, preferred_element_type=jnp.float32)
        current_y = new_y
        current_z = new_z
    inverse_root = current_z / jnp.sqrt(mean_eigen)
    root_columns = gathered_copies(inverse_root, DOM, 0)
    return jnp.dot(
        lax.all_gather(current, BAND, axis=1, tiled=True),
        root_columns,
        precision=highest,
        preferred_element_type=jnp.float32,
    )


def solution(mesh):
    finer = Mesh(
        mesh.devices.reshape(4, 4, 2, 4, 2), ("dom_0", "dom_1", "dom_2", "band_0", "band_1")
    )
    placed = (P(DOM, BAND), P(DOM), P(DOM, None, None), P(DOM, None), P(DOM))
    return jax.shard_map(
        on_device, mesh=finer, in_specs=placed, out_specs=P(DOM, BAND), check_vma=False
    )
```

profile of v0, /device:TPU:1, one launch (start us, length us, event | category | flops | bytes accessed | tf_op | source)
XLA Modules:
  0.0 527.7 jit_solution(1182816498723439362)
XLA Ops:
  7.9 1.4 fusion.2
  13.8 7.9 %collective-permute-done = bf16[256,128]{1,0:T(8,128)(2,1)S(1)} collective-permute-done((bf16[256,128]{1,0:T(8,128)(2,1)S(1)}, bf16[256,128]{1,0:T(8,128)(2,1)S(1)}, u32[]{:S(2)}, u32[]{:S(2)}) %collective-permute-start) | collective-permute-done | bytes 65568 | tf_op jit(solution)/shard_map/ppermute | solution.py:24
  21.7 12.1 %gather_fusion.1 = bf16[4096,128]{1,0:T(8,128)(2,1)S(1)} fusion(bf16[2304,128]{1,0:T(8,128)(2,1)S(1)} %pad_maximum_fusion, s32[4096]{0:T(1024)S(1)} %broadcast_clamp_fusion), kind=kCustom, calls=%fused_computation.1.clone | custom fusion | bytes 2113536 | tf_op jit(solution)/shard_map/jit(_take)/gather | solution.py:74
  34.4 3.7 convolution_bitcast_fusion.2
  38.1 1.9 copy.10
  39.9 22.9 %scatter_custom_fusion = f32[2304,128]{1,0:T(8,128)S(1)} fusion(s32[4096]{0:T(1024)S(1)} %bitcast.53, f32[4096,128]{1,0:T(8,128)} %bitcast.45, f32[]{:T(128)} %constant.35.clone.1), kind=kCustom, calls=%fused_computation.42 | custom fusion | flops 524288 | bytes 1180160 | tf_op jit(solution)/shard_map/scatter-add | solution.py:79
  62.9 8.2 %collective-permute-start.1 = (f32[256,128]{1,0:T(8,128)S(1)}, f32[256,128]{1,0:T(8,128)S(1)}, u32[]{:S(2)}, u32[]{:S(2)}) collective-permute-start(f32[256,128]{1,0:T(8,128)S(1)} %slice.49), channel_id=1, source_target_pairs={{0,8},{8,16},{16,24},{24,32},{32,40},{40,48},{48,56},{56,64},{64,7... | collective-permute-start | bytes 393224 | tf_op jit(solution)/shard_map/ppermute | solution.py:24
  71.2 2.1 collective-permute-done.1
  73.3 2.3 scatter_fusion
  77.3 1.3 collective-permute-start.2
  78.6 8.2 %collective-permute-done.2 = bf16[256,128]{1,0:T(8,128)(2,1)S(1)} collective-permute-done((bf16[256,128]{1,0:T(8,128)(2,1)S(1)}, bf16[256,128]{1,0:T(8,128)(2,1)S(1)}, u32[]{:S(2)}, u32[]{:S(2)}) %collective-permute-start.2) | collective-permute-done | bytes 65568 | tf_op jit(solution)/shard_map/ppermute | solution.py:24
  86.8 12.1 %gather_fusion.3 = bf16[4096,128]{1,0:T(8,128)(2,1)S(1)} fusion(bf16[2304,128]{1,0:T(8,128)(2,1)S(1)} %pad_maximum_fusion.1, s32[4096]{0:T(1024)S(1)} %broadcast_clamp_fusion), kind=kCustom, calls=%fused_computation.4.clone | custom fusion | bytes 2113536 | tf_op jit(solution)/shard_map/jit(_take)/gather | solution.py:74
  99.0 1.3 copy.11
  100.3 4.0 convolution_bitcast_fusion.1
  104.3 1.9 copy.12
  106.1 22.9 %scatter_custom_fusion.2 = f32[2304,128]{1,0:T(8,128)S(1)} fusion(s32[4096]{0:T(1024)S(1)} %bitcast.54, f32[4096,128]{1,0:T(8,128)} %bitcast.46, f32[]{:T(128)} %constant.35.clone.1), kind=kCustom, calls=%fused_computation.40 | custom fusion | flops 524288 | bytes 1180160 | tf_op jit(solution)/shard_map/scatter-add | solution.py:79
  130.1 8.3 %collective-permute-start.3 = (f32[256,128]{1,0:T(8,128)S(1)}, f32[256,128]{1,0:T(8,128)S(1)}, u32[]{:S(2)}, u32[]{:S(2)}) collective-permute-start(f32[256,128]{1,0:T(8,128)S(1)} %slice.51), channel_id=1, source_target_pairs={{0,8},{8,16},{16,24},{24,32},{32,40},{40,48},{48,56},{56,64},{64,7... | collective-permute-start | bytes 393224 | tf_op jit(solution)/shard_map/ppermute | solution.py:24
  138.5 1.3 slice.50
  140.4 2.5 scatter_fusion.1
  144.3 1.3 collective-permute-start.4
  145.6 8.1 %collective-permute-done.4 = bf16[256,128]{1,0:T(8,128)(2,1)S(1)} collective-permute-done((bf16[256,128]{1,0:T(8,128)(2,1)S(1)}, bf16[256,128]{1,0:T(8,128)(2,1)S(1)}, u32[]{:S(2)}, u32[]{:S(2)}) %collective-permute-start.4) | collective-permute-done | bytes 65568 | tf_op jit(solution)/shard_map/ppermute | solution.py:24
  153.7 15.0 %gather_fusion.5 = bf16[4096,128]{1,0:T(8,128)(2,1)} fusion(bf16[2304,128]{1,0:T(8,128)(2,1)S(1)} %pad_maximum_fusion.2, s32[4096]{0:T(1024)S(1)} %broadcast_clamp_fusion), kind=kCustom, calls=%fused_computation.5.clone | custom fusion | bytes 2113536 | tf_op jit(solution)/shard_map/jit(_take)/gather | solution.py:74
  168.8 1.5 copy.13
  170.3 5.0 convolution_bitcast_fusion
  175.3 2.9 copy.14
  178.2 22.9 %scatter_custom_fusion.4 = f32[2304,128]{1,0:T(8,128)S(1)} fusion(s32[4096]{0:T(1024)S(1)} %bitcast.55, f32[4096,128]{1,0:T(8,128)} %bitcast.44, f32[]{:T(128)} %constant.35.clone.1), kind=kCustom, calls=%fused_computation.38 | custom fusion | flops 524288 | bytes 1180160 | tf_op jit(solution)/shard_map/scatter-add | solution.py:79
  202.1 8.2 %collective-permute-start.5 = (f32[256,128]{1,0:T(8,128)S(1)}, f32[256,128]{1,0:T(8,128)S(1)}, u32[]{:S(2)}, u32[]{:S(2)}) collective-permute-start(f32[256,128]{1,0:T(8,128)S(1)} %slice.53), channel_id=1, source_target_pairs={{0,8},{8,16},{16,24},{24,32},{32,40},{40,48},{48,56},{56,64},{64,7... | collective-permute-start | bytes 393224 | tf_op jit(solution)/shard_map/ppermute | solution.py:24
  210.3 1.3 slice.52
  212.2 2.3 scatter_fusion.2
  214.6 2.8 fusion.32
  218.1 73.2 %all-gather.5.cloned.1.call-done = bf16[2048,1024]{1,0:T(8,128)(2,1)} async-done(((bf16[2048,128]{1,0:T(8,128)(2,1)}), bf16[2048,1024]{1,0:T(8,128)(2,1)}) %all-gather.5.cloned.1.call-update) | async-done | bytes 4194320 | tf_op jit(solution)/shard_map/all_gather | solution.py:100
  291.4 4.4 fusion.34
  295.8 10.0 %all-to-all-start = ((f32[32,32,128]{2,1,0:T(8,128)}), f32[32,32,128]{2,1,0:T(8,128)S(1)}, u32[]{:S(2)}, u32[]{:S(2)}) async-start(f32[32,32,128]{2,1,0:T(8,128)} %bitcast.10), calls=%async_computation | async-start | bytes 1048576 | tf_op jit(solution)/shard_map/all_to_all | solution.py:35
  305.8 27.0 %all-to-all-done = f32[32,32,128]{2,1,0:T(8,128)S(1)} async-done(((f32[32,32,128]{2,1,0:T(8,128)}), f32[32,32,128]{2,1,0:T(8,128)S(1)}, u32[]{:S(2)}, u32[]{:S(2)}) %all-to-all-start) | async-done | bytes 524320 | tf_op jit(solution)/shard_map/all_to_all | solution.py:35
  333.5 7.9 %psum.35 = f32[]{:T(128)} all-reduce(f32[]{:T(128)} %fusion.26), channel_id=1, replica_groups=mesh['dom_0'=4,'dom_1'=4,'dom_2'=2,'band_0'=4,'band_1'=2] {'dom_0'}, use_global_device_ids=true, to_apply=%region_8.11 | all-reduce | flops 1 | bytes 8 | tf_op jit(solution)/shard_map/psum | solution.py:40
  341.4 8.0 %psum.36 = f32[]{:T(128)} all-reduce(f32[]{:T(128)} %psum.35), channel_id=1, replica_groups=mesh['dom_0'=4,'dom_1'=4,'dom_2'=2,'band_0'=4,'band_1'=2] {'dom_1'}, use_global_device_ids=true, to_apply=%region_9.12 | all-reduce | flops 1 | bytes 8 | tf_op jit(solution)/shard_map/psum | solution.py:40
  349.4 8.3 %psum.37 = f32[]{:T(128)} all-reduce(f32[]{:T(128)} %psum.36), channel_id=1, replica_groups=mesh['dom_0'=4,'dom_1'=4,'dom_2'=2,'band_0'=4,'band_1'=2] {'dom_2'}, use_global_device_ids=true, to_apply=%region_10.13 | all-reduce | flops 1 | bytes 8 | tf_op jit(solution)/shard_map/psum | solution.py:40
  357.8 7.8 %psum.38 = f32[]{:T(128)} all-reduce(f32[]{:T(128)} %psum.37), channel_id=1, replica_groups=mesh['dom_0'=4,'dom_1'=4,'dom_2'=2,'band_0'=4,'band_1'=2] {'band_0'}, use_global_device_ids=true, to_apply=%region_11.14 | all-reduce | flops 1 | bytes 8 | tf_op jit(solution)/shard_map/psum | solution.py:40
  365.6 10.0 %psum.39 = f32[]{:T(128)} all-reduce(f32[]{:T(128)} %psum.38), channel_id=1, replica_groups=mesh['dom_0'=4,'dom_1'=4,'dom_2'=2,'band_0'=4,'band_1'=2] {'band_1'}, use_global_device_ids=true, to_apply=%region_12.15 | all-reduce | flops 1 | bytes 8 | tf_op jit(solution)/shard_map/psum | solution.py:40
  377.1 3.9 all-to-all-start.1
  381.1 25.9 %all_gather.14 = bf16[64,1024]{1,0:T(8,128)(2,1)S(1)} all-gather(bf16[64,128]{1,0:T(8,128)(2,1)S(1)} %pad_maximum_fusion.3), channel_id=1, replica_groups=mesh['dom_0'=4,'dom_1'=4,'dom_2'=2,'band_0'=4,'band_1'=2] {'band_0','ban..., dimensions={1}, use_global_device_ids=true | all-gather | bytes 147456 | tf_op jit(solution)/shard_map/all_gather | solution.py:45
  407.8 28.0 %all_to_all.30 = f32[32,32,128]{2,1,0:T(8,128)S(1)} all-to-all(f32[32,32,128]{2,1,0:T(8,128)S(1)} %broadcast_in_dim.49), channel_id=1, replica_groups=mesh['dom_0'=4,'dom_1'=4,'dom_2'=2,'band_0'=4,'band_1'=2] {'dom_0','dom_..., dimensions={0} | all-to-all | bytes 1048576 | tf_op jit(solution)/shard_map/all_to_all | solution.py:54
  437.1 3.9 all-to-all-start.3
  441.3 22.3 %all_gather.15 = bf16[64,1024]{1,0:T(8,128)(2,1)S(1)} all-gather(bf16[64,128]{1,0:T(8,128)(2,1)S(1)} %pad_maximum_fusion.4), channel_id=1, replica_groups=mesh['dom_0'=4,'dom_1'=4,'dom_2'=2,'band_0'=4,'band_1'=2] {'band_0','ban..., dimensions={1}, use_global_device_ids=true | all-gather | bytes 147456 | tf_op jit(solution)/shard_map/all_gather | solution.py:45
  464.8 10.3 %all-to-all-start.4 = ((f32[32,32,128]{2,1,0:T(8,128)}), f32[32,32,128]{2,1,0:T(8,128)S(1)}, u32[]{:S(2)}, u32[]{:S(2)}) async-start(f32[32,32,128]{2,1,0:T(8,128)} %broadcast_in_dim.51), calls=%async_computation.4 | async-start | bytes 1048576 | tf_op jit(solution)/shard_map/all_to_all | solution.py:54
  475.2 17.9 %all-to-all-done.4 = f32[32,32,128]{2,1,0:T(8,128)S(1)} async-done(((f32[32,32,128]{2,1,0:T(8,128)}), f32[32,32,128]{2,1,0:T(8,128)S(1)}, u32[]{:S(2)}, u32[]{:S(2)}) %all-to-all-start.4) | async-done | bytes 524320 | tf_op jit(solution)/shard_map/all_to_all | solution.py:54
  493.5 17.6 %all_to_all.31 = f32[32,32,128]{2,1,0:T(8,128)S(1)} all-to-all(f32[32,32,128]{2,1,0:T(8,128)S(1)} %broadcast_in_dim.52), channel_id=1, replica_groups=mesh['dom_0'=4,'dom_1'=4,'dom_2'=2,'band_0'=4,'band_1'=2] {'dom_0','dom_..., dimensions={0} | all-to-all | bytes 1048576 | tf_op jit(solution)/shard_map/all_to_all | solution.py:54
  511.0 9.8 %fusion.35 = f32[2048,128]{1,0:T(8,128)} fusion(f32[2048,1024]{1,0:T(8,128)} %all-gather.3.cloned.1.call-done, f32[1024,128]{1,0:T(8,128)S(1)} %bitcast.43), kind=kOutput, calls=%fused_computation.82 | convolution fusion | flops 3221225472 | bytes 9961472 | tf_op jit(solution)/shard_map/dot_general | solution.py:142
  (64 shorter events, 19.2 us)
Async XLA Ops:
  6.5 284.8 %all-gather.5.cloned.1.call-start = ((), (), s32[]{:S(2)}) async-start(), calls=%async_computation.7 | async-start | bytes 4718592 | tf_op jit(solution)/shard_map/all_gather | solution.py:100
  10.3 11.4 %collective-permute-start = (bf16[256,128]{1,0:T(8,128)(2,1)S(1)}, bf16[256,128]{1,0:T(8,128)(2,1)S(1)}, u32[]{:S(2)}, u32[]{:S(2)}) collective-permute-start(bf16[256,128]{1,0:T(8,128)(2,1)S(1)} %broadcast_select_fusion.2), channel_id=1, source_target_pairs={{8,0},{16,8},{24,16},{32,24},{40,32},{48,40},{56,48},{64,56},{72,6... | collective-permute-start | bytes 196616 | tf_op jit(solution)/shard_map/ppermute | solution.py:24
  38.0 33.0 %copy-start.4 = (f32[2048]{0:T(1024)S(1)}, f32[2048]{0:T(1024)}, u32[]{:S(2)}) copy-start(f32[2048]{0:T(1024)} %param.10) | copy-start | bytes 24580
  62.9 10.4 %collective-permute-start.1 = (f32[256,128]{1,0:T(8,128)S(1)}, f32[256,128]{1,0:T(8,128)S(1)}, u32[]{:S(2)}, u32[]{:S(2)}) collective-permute-start(f32[256,128]{1,0:T(8,128)S(1)} %slice.49), channel_id=1, source_target_pairs={{0,8},{8,16},{16,24},{24,32},{32,40},{40,48},{48,56},{56,64},{64,7... | collective-permute-start | bytes 393224 | tf_op jit(solution)/shard_map/ppermute | solution.py:24
  71.1 4.5 copy-start
  77.3 9.4 %collective-permute-start.2 = (bf16[256,128]{1,0:T(8,128)(2,1)S(1)}, bf16[256,128]{1,0:T(8,128)(2,1)S(1)}, u32[]{:S(2)}, u32[]{:S(2)}) collective-permute-start(bf16[256,128]{1,0:T(8,128)(2,1)S(1)} %broadcast_select_fusion.1), channel_id=1, source_target_pairs={{8,0},{16,8},{24,16},{32,24},{40,32},{48,40},{56,48},{64,56},{72,6... | collective-permute-start | bytes 196616 | tf_op jit(solution)/shard_map/ppermute | solution.py:24
  129.1 1.0 copy-start.3
  130.1 12.8 %copy-start.1 = (bf16[2048,128]{1,0:T(8,128)(2,1)S(1)}, bf16[2048,128]{1,0:T(8,128)(2,1)}, u32[]{:S(2)}) copy-start(bf16[2048,128]{1,0:T(8,128)(2,1)} %param.9) | copy-start | bytes 1572868
  130.1 10.3 %collective-permute-start.3 = (f32[256,128]{1,0:T(8,128)S(1)}, f32[256,128]{1,0:T(8,128)S(1)}, u32[]{:S(2)}, u32[]{:S(2)}) collective-permute-start(f32[256,128]{1,0:T(8,128)S(1)} %slice.51), channel_id=1, source_target_pairs={{0,8},{8,16},{16,24},{24,32},{32,40},{40,48},{48,56},{56,64},{64,7... | collective-permute-start | bytes 393224 | tf_op jit(solution)/shard_map/ppermute | solution.py:24
  144.3 9.4 %collective-permute-start.4 = (bf16[256,128]{1,0:T(8,128)(2,1)S(1)}, bf16[256,128]{1,0:T(8,128)(2,1)S(1)}, u32[]{:S(2)}, u32[]{:S(2)}) collective-permute-start(bf16[256,128]{1,0:T(8,128)(2,1)S(1)} %broadcast_select_fusion), channel_id=1, source_target_pairs={{8,0},{16,8},{24,16},{32,24},{40,32},{48,40},{56,48},{64,56},{72,6... | collective-permute-start | bytes 196616 | tf_op jit(solution)/shard_map/ppermute | solution.py:24
  201.1 1.0 copy-start.2
  202.1 10.1 %collective-permute-start.5 = (f32[256,128]{1,0:T(8,128)S(1)}, f32[256,128]{1,0:T(8,128)S(1)}, u32[]{:S(2)}, u32[]{:S(2)}) collective-permute-start(f32[256,128]{1,0:T(8,128)S(1)} %slice.53), channel_id=1, source_target_pairs={{0,8},{8,16},{16,24},{24,32},{32,40},{40,48},{48,56},{56,64},{64,7... | collective-permute-start | bytes 393224 | tf_op jit(solution)/shard_map/ppermute | solution.py:24
  217.4 293.7 %all-gather.3.cloned.1.call-start = ((), (), s32[]{:S(2)}) async-start(), calls=%async_computation.6 | async-start | bytes 9437184 | tf_op jit(solution)/shard_map/all_gather | solution.py:143
  295.8 37.0 %all-to-all-start = ((f32[32,32,128]{2,1,0:T(8,128)}), f32[32,32,128]{2,1,0:T(8,128)S(1)}, u32[]{:S(2)}, u32[]{:S(2)}) async-start(f32[32,32,128]{2,1,0:T(8,128)} %bitcast.10), calls=%async_computation | async-start | bytes 1048576 | tf_op jit(solution)/shard_map/all_to_all | solution.py:35
  377.1 30.4 %all-to-all-start.1 = ((f32[32,32,128]{2,1,0:T(8,128)}), f32[32,32,128]{2,1,0:T(8,128)S(1)}, u32[]{:S(2)}, u32[]{:S(2)}) async-start(f32[32,32,128]{2,1,0:T(8,128)} %broadcast_in_dim.48), calls=%async_computation.1 | async-start | bytes 1048576 | tf_op jit(solution)/shard_map/all_to_all | solution.py:54
  437.1 26.6 %all-to-all-start.3 = ((f32[32,32,128]{2,1,0:T(8,128)}), f32[32,32,128]{2,1,0:T(8,128)S(1)}, u32[]{:S(2)}, u32[]{:S(2)}) async-start(f32[32,32,128]{2,1,0:T(8,128)} %broadcast_in_dim.50), calls=%async_computation.3 | async-start | bytes 1048576 | tf_op jit(solution)/shard_map/all_to_all | solution.py:54
  464.8 28.3 %all-to-all-start.4 = ((f32[32,32,128]{2,1,0:T(8,128)}), f32[32,32,128]{2,1,0:T(8,128)S(1)}, u32[]{:S(2)}, u32[]{:S(2)}) async-start(f32[32,32,128]{2,1,0:T(8,128)} %broadcast_in_dim.51), calls=%async_computation.4 | async-start | bytes 1048576 | tf_op jit(solution)/shard_map/all_to_all | solution.py:54
Sparse Core Ops, SparseCore 0:
  217.5 73.8 all-gather.4
  293.1 115.6 all-gather.2
where the time goes:
time: 535 us; the launch traced here: 528 us
  waiting for transfers between devices  147 us (27%)
  blocking collectives  136 us (25%)
  other arithmetic  85.3 us (16%)
  local copies, waits for them, and re-layouts  60.1 us (11%)
  starting transfers between devices  56.7 us (11%)
  matrix products  28.4 us (5%)
  between operations  14.5 us (3%)
    all_gather x1, waiting for transfers between devices, on_device(): lax.all_gather(rounded, BAND, axis=1, tiled=True)  73.2 us
    scatter-add x3, other arithmetic, apply_hamiltonian(): assembled.at[connectivity.reshape(-1)].add(products.reshape(-1, band_width))  68.8 us
    all_gather x2, blocking collectives, in_one_piece(): lax.all_gather(both, axis, axis=dim, tiled=True)  48.3 us
    all_to_all x2, blocking collectives, copy_for_each(): return lax.all_to_all(copies, axis, split_axis=0, concat_axis=0, tiled=True)  45.6 us
    gather x6, local copies, waits for them, and re-layouts, apply_hamiltonian(): gathered = jnp.take(extended, connectivity, axis=0)  42.6 us
    psum x5, blocking collectives, by_axis(): return functools.reduce(lax.psum, axes, array)  42.1 us
    ppermute x6, starting transfers between devices, passed_along(): lax.ppermute(value, axis, [(source, source + steps) for source in range(i...  28.6 us
    ppermute x6, waiting for transfers between devices, passed_along(): lax.ppermute(value, axis, [(source, source + steps) for source in range(i...  27.5 us
  transfers between devices with their start and end apart: 12, of which 10 were waited for; matrix products, arithmetic and copies ran while one was open for 3% of the time, Pallas kernels for 0%

commit v1 on v0

v1 whole, which is shorter than its diff:
```python
import functools

import jax
import jax.numpy as jnp
from jax import lax
from jax.experimental import pallas as pl
from jax.experimental.pallas import tpu as pltpu
from jax.sharding import Mesh
from jax.sharding import PartitionSpec as P

STATES = 1024
DEGREE = 3
CENTER = 5.0
HALF = 5.0
DOM = ("dom_0", "dom_1", "dom_2")
BAND = ("band_0", "band_1")
PLANE = ("dom_0", "dom_1")
COLUMN = ("dom_2", "band_0")
CORE = ("band_1",)
F32 = jnp.float32
BF16 = jnp.bfloat16
IN_VMEM = pl.BlockSpec(memory_space=pltpu.VMEM)
IN_SMEM = pl.BlockSpec(memory_space=pltpu.SMEM)
IN_ANY = pl.BlockSpec(memory_space=pl.ANY)


def shape(dims, dtype):
    return jax.ShapeDtypeStruct(dims, dtype)


def call(body, name, ins, outs, scratch=(), flops=0, moved=0, vmem=32):
    return pl.pallas_call(
        body,
        in_specs=ins,
        out_specs=jax.tree.map(lambda _: IN_VMEM, outs),
        out_shape=outs,
        scratch_shapes=list(scratch),
        compiler_params=pltpu.CompilerParams(vmem_limit_bytes=vmem * 2**20),
        cost_estimate=pl.CostEstimate(flops=flops, bytes_accessed=moved, transcendentals=0),
        name=name,
    )


def dot(a, b):
    return jnp.dot(a, b, preferred_element_type=F32)


def halves(a, axis=1):
    high = a.astype(BF16)
    return jnp.concatenate([high, (a - high.astype(F32)).astype(BF16)], axis)


def one_hot(hit):
    return jnp.where(hit, 1.0, 0.0).astype(BF16)


def scale_rows(own, width, values, mass_ref, face_ref, scaled_ref, rows_ref, picked):
    scaled_ref[:own, :] = (mass_ref[...] * values).astype(BF16).astype(F32)
    scaled_ref[own:, :] = jnp.zeros((scaled_ref.shape[0] - own, width), F32)

    def take(i, carry):
        rows = [scaled_ref[pl.ds(face_ref[0, i * 8 + u], 1), :] for u in range(8)]
        picked[pl.ds(pl.multiple_of(i * 8, 8), 8), :] = jnp.concatenate(rows, 0)
        return carry

    lax.fori_loop(0, picked.shape[0] // 8, take, 0)
    rows_ref[...] = picked[...].astype(BF16)


def start_body(face_ref, wave_ref, mass_ref, scaled_ref, rows_ref, picked):
    own, width = wave_ref.shape
    scale_rows(
        own, width, wave_ref[...].astype(F32), mass_ref, face_ref, scaled_ref, rows_ref, picked
    )


def face_hits(links_ref, own, face, cell, nodes):
    links = links_ref[:1, cell * nodes : (cell + 1) * nodes]
    return one_hot(links == lax.broadcasted_iota(jnp.int32, (face, nodes), 0) + own)


def face_matrix_body(own, face, links_ref, cells_ref, spread_ref, block_ref):
    cells, nodes, _ = cells_ref.shape
    total = jnp.zeros((face, 2 * face), F32)
    for cell in range(cells):
        hits = face_hits(links_ref, own, face, cell, nodes)
        columns = lax.dot_general(
            cells_ref[cell], hits, (((1,), (1,)), ((), ())), preferred_element_type=F32
        )
        both = halves(columns)
        spread_ref[cell * nodes : (cell + 1) * nodes, :] = both
        total = total + dot(hits, both)
    block_ref[...] = total[:, :face] + total[:, face:]


def local_body(own, face, index_ref, links_ref, scaled_ref, cells_ref, products_ref, sent_ref, held):
    cells, nodes, _ = cells_ref.shape
    width = scaled_ref.shape[1]

    def take(i, carry):
        for cell in range(cells):
            rows = [scaled_ref[pl.ds(index_ref[cell, i * 8 + u], 1), :] for u in range(8)]
            held[pl.ds(pl.multiple_of(cell * nodes + i * 8, 8), 8), :] = jnp.concatenate(rows, 0)
        return carry

    lax.fori_loop(0, nodes // 8, take, 0)
    total = jnp.zeros((face, 2 * width), F32)
    for cell in range(cells):
        part = slice(cell * nodes, (cell + 1) * nodes)
        product = dot(cells_ref[cell], held[part, :].astype(BF16))
        products_ref[part, :] = product
        total = total + dot(face_hits(links_ref, own, face, cell, nodes), halves(product))
    sent_ref[...] = total[:, :width] + total[:, width:]


def assemble_body(index_ref, products_ref, spread_ref, rows_ref, summed_ref, whole, *totals):
    cells, nodes = index_ref.shape
    own = summed_ref.shape[0]
    rows = rows_ref[...]
    twice = jnp.concatenate([rows, rows], 0)
    for cell in range(cells):
        part = slice(cell * nodes, (cell + 1) * nodes)
        whole[part, :] = products_ref[part, :] + dot(spread_ref[part, :], twice)
    for total in totals:
        total[...] = jnp.zeros_like(total)

    def add(i, carry):
        for u in range(4):
            j = i * 4 + u
            at = [pl.ds(index_ref[cell, j], 1) for cell in range(cells)]
            sums = [
                totals[cell][at[cell], :] + whole[pl.ds(cell * nodes + j, 1), :]
                for cell in range(cells)
            ]
            for cell in range(cells):
                totals[cell][at[cell], :] = sums[cell]
        return carry

    lax.fori_loop(0, nodes // 4, add, 0)

    def collect(i, carry):
        part = pl.ds(pl.multiple_of(i * 64, 64), 64)
        summed = totals[0][part, :]
        for total in totals[1:]:
            summed = summed + total[part, :]
        summed_ref[part, :] = summed
        return carry

    lax.fori_loop(0, own // 64, collect, 0)


def applied(faces_ref, summed_ref, arrived_ref, block_ref, rows_ref, mass_ref):
    own, width = summed_ref.shape
    face = rows_ref.shape[0]
    rows = rows_ref[...]
    contribution = arrived_ref[...] + dot(halves(block_ref[...]), jnp.concatenate([rows, rows], 0))
    hits = one_hot(lax.broadcasted_iota(jnp.int32, (own, face), 0) == faces_ref[:1, :])
    added = dot(hits, halves(contribution))
    return mass_ref[...] * (summed_ref[...] + (added[:, :width] + added[:, width:]))


def first_body(
    face_ref, faces_ref, summed_ref, arrived_ref, block_ref, rows_ref, mass_ref, wave_ref,
    current_ref, scaled_ref, sent_ref, picked,
):
    own, width = summed_ref.shape
    image = applied(faces_ref, summed_ref, arrived_ref, block_ref, rows_ref, mass_ref)
    current_ref[...] = (image - CENTER * wave_ref[...].astype(F32)) / HALF
    scale_rows(own, width, current_ref[...], mass_ref, face_ref, scaled_ref, sent_ref, picked)


def next_body(
    face_ref, faces_ref, summed_ref, arrived_ref, block_ref, rows_ref, mass_ref, previous_ref,
    current_ref, following_ref, scaled_ref, sent_ref, picked,
):
    own, width = summed_ref.shape
    image = applied(faces_ref, summed_ref, arrived_ref, block_ref, rows_ref, mass_ref)
    following_ref[...] = 2.0 * (image - CENTER * current_ref[...]) / HALF - previous_ref[
        ...
    ].astype(F32)
    scale_rows(own, width, following_ref[...], mass_ref, face_ref, scaled_ref, sent_ref, picked)


def last_body(
    faces_ref, summed_ref, arrived_ref, block_ref, rows_ref, mass_ref, previous_ref, current_ref,
    rounded_ref,
):
    image = applied(faces_ref, summed_ref, arrived_ref, block_ref, rows_ref, mass_ref)
    rounded_ref[...] = (
        2.0 * (image - CENTER * current_ref[...]) / HALF - previous_ref[...].astype(F32)
    ).astype(BF16)


def gram_body(rows_ref, blocks_ref):
    groups = rows_ref.shape[0]
    width = rows_ref.shape[2]
    every = jnp.concatenate([rows_ref[g] for g in range(groups)], 1)
    at = 0
    for g in range(groups):
        panel = lax.dot_general(
            rows_ref[g], every[:, g * width :], (((0,), (0,)), ((), ())),
            preferred_element_type=F32,
        )
        for h in range(groups - g):
            blocks_ref[at] = panel[:, h * width : (h + 1) * width].astype(BF16)
            at += 1


def rotate_body(nodes, band_ref, blocks_ref, every_ref, rotated_ref, gram, rows, sem):
    copy = pltpu.make_async_copy(every_ref, rows, sem)
    copy.start()
    states = gram.shape[0]
    width = rotated_ref.shape[1]
    groups = states // width
    same = lax.broadcasted_iota(jnp.int32, (width, width), 0) == lax.broadcasted_iota(
        jnp.int32, (width, width), 1
    )
    diagonal = jnp.zeros((width, width), F32)
    at = 0
    for g in range(groups):
        for h in range(g, groups):
            block = blocks_ref[at].astype(F32)
            at += 1
            gram[g * width : (g + 1) * width, h * width : (h + 1) * width] = block.astype(BF16)
            if h == g:
                diagonal = diagonal + jnp.where(same, block, 0.0)
            else:
                gram[h * width : (h + 1) * width, g * width : (g + 1) * width] = block.T.astype(
                    BF16
                )
    trace = jnp.sum(jnp.sum(diagonal, axis=0, keepdims=True), axis=1, keepdims=True)
    unit = states / trace
    first = pl.multiple_of(band_ref[0] * width, width)
    unity = (
        lax.broadcasted_iota(jnp.int32, (states, width), 0)
        == lax.broadcasted_iota(jnp.int32, (states, width), 1) + first
    ).astype(F32)

    def times_y(v):
        both = dot(gram[...], halves(v))
        return (both[:, :width] + both[:, width:]) * unit

    once = 1.5 * unity - 0.5 * (gram[:, pl.ds(first, width)].astype(F32) * unit)
    right = 1.5 * once - 0.5 * times_y(once)
    middle = times_y(right)
    product = 1.5 * middle - 0.5 * times_y(middle)
    root = 1.5 * once - 0.5 * product
    mean_eigen = trace / (states * nodes)
    both = halves(root / jnp.sqrt(mean_eigen))
    copy.wait()
    own = rotated_ref.shape[0]
    total = jnp.zeros((own, 2 * width), F32)
    for g in range(groups):
        total = total + dot(
            rows[g * own : (g + 1) * own, :], both[g * width : (g + 1) * width, :]
        )
    rotated_ref[...] = total[:, :width] + total[:, width:]


def passed_along(value, steps):
    count = lax.axis_size(DOM)
    initial, last = max(0, -steps), min(count, count - steps)
    return lax.ppermute(value, DOM, [(source, source + steps) for source in range(initial, last)])


def exchanged(pieces, axes):
    return lax.all_to_all(pieces, axes, split_axis=0, concat_axis=0, tiled=True)


def sum_of_share(array, axes):
    peers = lax.axis_size(axes)
    pieces = array.reshape(peers, array.shape[0] // peers, array.shape[1])
    return exchanged(pieces, axes).astype(F32).sum(axis=0).astype(BF16)


def shares_of_all(array, axes):
    peers = lax.axis_size(axes)
    arrived = exchanged(jnp.broadcast_to(array, (peers, *array.shape)), axes)
    return arrived.reshape(peers * array.shape[0], array.shape[1])


def on_device(wavefunctions, mass_scale, cell_matrices, connectivity, face_index):
    own, width = wavefunctions.shape
    face = face_index.shape[0]
    cells, cell_nodes = connectivity.shape
    extent = own + face
    entries = cells * cell_nodes
    domains = lax.axis_size(DOM)
    bands = lax.axis_size(BAND)

    mass = jnp.broadcast_to(mass_scale[:, None], (own, width))
    links = jnp.broadcast_to(connectivity.reshape(1, entries), (8, entries))
    faces = jnp.broadcast_to(face_index.reshape(1, face), (8, face))
    face_list = face_index.reshape(1, face)

    picked = pltpu.VMEM((face, width), F32)
    scaled_shape = shape((extent, width), F32)
    rows_shape = shape((face, width), BF16)
    wide = shape((own, width), F32)
    start = call(
        start_body, "scaled_start", [IN_SMEM] + [IN_VMEM] * 2, [scaled_shape, rows_shape], [picked],
        10**6, 3 * 2**20,
    )
    face_matrix = call(
        functools.partial(face_matrix_body, own, face), "face_matrix", [IN_VMEM] * 2,
        [shape((entries, 2 * face), BF16), shape((face, face), F32)],
        [], 3 * 10**9, 8 * 2**20,
    )
    local = call(
        functools.partial(local_body, own, face), "local_products", [IN_SMEM] + [IN_VMEM] * 3,
        [shape((entries, width), F32), shape((face, width), F32)],
        [pltpu.VMEM((entries, width), F32)], 5 * 10**9, 16 * 2**20,
    )
    assemble = call(
        assemble_body, "assembled", [IN_SMEM] + [IN_VMEM] * 3, wide,
        [pltpu.VMEM((entries, width), F32)] + [pltpu.VMEM((extent, width), F32)] * cells,
        5 * 10**9, 16 * 2**20,
    )

    scaled, rows = start(face_list, wavefunctions, mass)
    spread, block = face_matrix(links, cell_matrices)
    block = passed_along(block, 1)
    previous, current = None, wavefunctions
    for sweep in range(DEGREE):
        received = passed_along(rows, -1)
        products, sent = local(connectivity, links, scaled, cell_matrices)
        arrived = passed_along(sent, 1)
        summed = assemble(connectivity, products, spread, received)
        parts = (summed, arrived, block, rows, mass)
        if sweep == DEGREE - 1:
            rounded = call(
                last_body, "filtered", [IN_VMEM] * 8, shape((own, width), BF16), [],
                10**9, 6 * 2**20,
            )(faces, *parts, previous, current)
        elif sweep == 0:
            following, scaled, rows = call(
                first_body, "first_step", [IN_SMEM] + [IN_VMEM] * 7,
                [wide, scaled_shape, rows_shape], [picked], 10**9, 6 * 2**20,
            )(face_list, faces, *parts, current)
            previous, current = current, following
        else:
            following, scaled, rows = call(
                next_body, "next_step", [IN_SMEM] + [IN_VMEM] * 8,
                [wide, scaled_shape, rows_shape], [picked], 10**9, 6 * 2**20,
            )(face_list, faces, *parts, previous, current)
            previous, current = current, following

    every = lax.all_gather(rounded, BAND, axis=0, tiled=True)
    nodes_rows = exchanged(rounded.reshape(bands, own // bands, width), BAND)
    pairs = bands * (bands + 1) // 2
    gram = call(
        gram_body, "gram", [IN_VMEM], shape((pairs, width, width), BF16), [], 10**9, 2 * 2**20,
    )(nodes_rows)
    gram = gram.reshape(pairs * width, width)
    for axes in (CORE, PLANE, COLUMN):
        gram = sum_of_share(gram, axes)
    for axes in (COLUMN, PLANE, CORE):
        gram = shares_of_all(gram, axes)
    band = lax.axis_index(BAND).astype(jnp.int32).reshape(1)
    return call(
        functools.partial(rotate_body, own * domains), "rotated", [IN_SMEM, IN_VMEM, IN_ANY], wide,
        [
            pltpu.VMEM((bands * width, bands * width), BF16),
            pltpu.VMEM((bands * own, width), BF16),
            pltpu.SemaphoreType.DMA,
        ],
        3 * 10**9, 8 * 2**20,
    )(band, gram.reshape(pairs, width, width), every)


def solution(mesh):
    finer = Mesh(
        mesh.devices.reshape(4, 4, 2, 4, 2), ("dom_0", "dom_1", "dom_2", "band_0", "band_1")
    )
    placed = (P(DOM, BAND), P(DOM), P(DOM, None, None), P(DOM, None), P(DOM))
    return jax.shard_map(
        on_device, mesh=finer, in_specs=placed, out_specs=P(DOM, BAND), check_vma=False
    )
```

time: 535 us -> 235 us (0.44); the launches traced: 528 us -> 234 us
  waiting for transfers between devices: 147 us -> 9.59 us
  other arithmetic: 85.3 us -> 0.69 us
  Pallas kernels: 0 us -> 69.4 us
  local copies, waits for them, and re-layouts: 60.1 us -> 7.18 us
  blocking collectives: 136 us -> 91.4 us
  matrix products: 28.4 us -> 0 us
  starting transfers between devices: 56.7 us -> 42.1 us
    scatter-add x6 -> x0, other arithmetic: 75.9 us -> none  [the longest x3 68.8 us: apply_hamiltonian(): assembled.at[connectivity.reshape(-1)].add(products.reshape(-1, band_width))]
    all_gather x2 -> x1, waiting for transfers between devices: 73.2 us -> 0.01 us  [on_device(): every = lax.all_gather(rounded, BAND, axis=0, tiled=True)]
    pallas_call x0 -> x13, Pallas kernels: none -> 69.4 us  [the longest x3 26.5 us: on_device(): products, sent = local(connectivity, links, scaled, cell_matrices)]
    all_gather x2 -> x0, blocking collectives: 48.3 us -> none  [in_one_piece(): lax.all_gather(both, axis, axis=dim, tiled=True)]
    all_to_all x2 -> x6, blocking collectives: 45.6 us -> 91.4 us  [exchanged(): return lax.all_to_all(pieces, axes, split_axis=0, concat_axis=0, tiled=True)]
    gather x9 -> x0, local copies, waits for them, and re-layouts: 45.2 us -> none  [the longest x6 42.6 us: apply_hamiltonian(): gathered = jnp.take(extended, connectivity, axis=0)]
    psum x5 -> x0, blocking collectives: 42.1 us -> none  [by_axis(): return functools.reduce(lax.psum, axes, array)]
    all_to_all x4 -> x1, waiting for transfers between devices: 45.4 us -> 9.55 us  [exchanged(): return lax.all_to_all(pieces, axes, split_axis=0, concat_axis=0, tiled=True)]
  transfers between devices with their start and end apart: 12 -> 9, of which waited for: 10 -> 1; matrix products, arithmetic and copies ran while one was open for 3% -> 1% of each run, Pallas kernels for 0% -> 24%
where the time goes in v1:
time: 235 us; the launch traced here: 234 us
  blocking collectives  91.4 us (39%)
  Pallas kernels  69.4 us (30%)
  starting transfers between devices  42.1 us (18%)
  between operations  13.7 us (6%)
  waiting for transfers between devices  9.59 us (4%)
  local copies, waits for them, and re-layouts  7.18 us (3%)
    all_to_all x6, blocking collectives, exchanged(): return lax.all_to_all(pieces, axes, split_axis=0, concat_axis=0, tiled=True)  91.4 us
    ppermute x7, starting transfers between devices, passed_along(): lax.ppermute(value, DOM, [(source, source + steps) for source in range(in...  38.3 us
    pallas_call x3, Pallas kernels, on_device(): products, sent = local(connectivity, links, scaled, cell_matrices)  26.5 us
    pallas_call x3, Pallas kernels, on_device(): summed = assemble(connectivity, products, spread, received)  25.5 us
    all_to_all x1, waiting for transfers between devices, exchanged(): return lax.all_to_all(pieces, axes, split_axis=0, concat_axis=0, tiled=True)  9.55 us
    pallas_call x1, Pallas kernels, on_device(): call(functools.partial(rotate_body, own * domains), 'rotated', [IN_SMEM,...  7.84 us
    unnamed x15, local copies, waits for them, and re-layouts  5.07 us
  transfers between devices with their start and end apart: 9, of which 1 were waited for; matrix products, arithmetic and copies ran while one was open for 1% of the time, Pallas kernels for 24%

profile of v1, /device:TPU:1, one launch (start us, length us, event | category | flops | bytes accessed | tf_op | source)
XLA Modules:
  0.0 234.1 jit_solution(9170413039761412123)
XLA Ops:
  6.5 0.0 all-gather.2.cloned.1.call-start
  6.5 1.1 broadcast_in_dim.30.mass_ref
  7.6 0.0 copy-start.2
  7.6 0.7 copy-done.2
  8.3 1.0 scaled_start.1
  9.4 1.3 collective-permute-start
  10.7 0.0 copy-start.4
  10.7 2.2 copy-done.4
  12.9 8.8 %local_products.3 = (f32[4096,128]{1,0:T(8,128)S(1)}, f32[256,128]{1,0:T(8,128)S(1)}) custom-call(s32[8,512]{1,0:T(8,128)S(1)} %copy-done.1, s32[8,4096]{1,0:T(8,128)S(1)} %broadcast_in_dim.29.links_ref, f32[2304,128]{1,0:T(8,128)S(1)} %get-tuple-element.21.scaled_ref, bf16[8,512,512]{2,1,0:T(8,128)(2,1)S(1)} %copy-done.4), custom_call_target="tpu_custom_call" | custom-call | flops 5000000000 | bytes 16777216 | tf_op jit(solution)/shard_map/local_products/pallas_call | solution.py:326
  21.7 10.3 %collective-permute-start.1 = (f32[256,128]{1,0:T(8,128)S(1)}, f32[256,128]{1,0:T(8,128)S(1)}, u32[]{:S(2)}, u32[]{:S(2)}) collective-permute-start(f32[256,128]{1,0:T(8,128)S(1)} %get-tuple-element.25), channel_id=1, source_target_pairs={{0,8},{8,16},{16,24},{24,32},{32,40},{40,48},{48,56},{56,64},{64,7... | collective-permute-start | bytes 393224 | tf_op jit(solution)/shard_map/ppermute | solution.py:263
  32.0 3.0 %face_matrix.1 = (bf16[4096,512]{1,0:T(8,128)(2,1)S(1)}, f32[256,256]{1,0:T(8,128)S(1)}) custom-call(s32[8,4096]{1,0:T(8,128)S(1)} %broadcast_in_dim.29.links_ref, bf16[8,512,512]{2,1,0:T(8,128)(2,1)S(1)} %copy-done.5), custom_call_target="tpu_custom_call" | custom-call | flops 3000000000 | bytes 8388608 | tf_op jit(solution)/shard_map/face_matrix/pallas_call | solution.py:321
  35.0 8.2 %collective-permute-start.2 = (f32[256,256]{1,0:T(8,128)S(1)}, f32[256,256]{1,0:T(8,128)S(1)}, u32[]{:S(2)}, u32[]{:S(2)}) collective-permute-start(f32[256,256]{1,0:T(8,128)S(1)} %get-tuple-element.26), channel_id=1, source_target_pairs={{0,8},{8,16},{16,24},{24,32},{32,40},{40,48},{48,56},{56,64},{64,7... | collective-permute-start | bytes 786440 | tf_op jit(solution)/shard_map/ppermute | solution.py:263
  43.2 0.0 collective-permute-done.rows_ref
  43.2 0.0 copy-start.3
  43.2 8.5 %assembled.3.summed_ref = f32[2048,128]{1,0:T(8,128)S(1)} custom-call(s32[8,512]{1,0:T(8,128)S(1)} %copy-done.1, f32[4096,128]{1,0:T(8,128)S(1)} %get-tuple-element.22.products_ref, bf16[4096,512]{1,0:T(8,128)(2,1)S(1)} %get-tuple-element.23.spread_ref, bf16[256,128]{1,0:T(8,128)(2,1)S(1)} %collective-permute-done.rows_ref), custom_call_target="tpu_custom_call" | custom-call | flops 5000000000 | bytes 16777216 | tf_op jit(solution)/shard_map/assembled/pallas_call | solution.py:328
  51.7 0.0 collective-permute-done.1.arrived_ref
  51.8 0.0 collective-permute-done.2.block_ref
  51.8 1.7 first_step.1
  53.5 1.3 collective-permute-start.3
  54.8 8.8 %local_products.4 = (f32[4096,128]{1,0:T(8,128)S(1)}, f32[256,128]{1,0:T(8,128)S(1)}) custom-call(s32[8,512]{1,0:T(8,128)S(1)} %copy-done.1, s32[8,4096]{1,0:T(8,128)S(1)} %broadcast_in_dim.29.links_ref, f32[2304,128]{1,0:T(8,128)S(1)} %get-tuple-element.27.scaled_ref, bf16[8,512,512]{2,1,0:T(8,128)(2,1)S(1)} %copy-done.5), custom_call_target="tpu_custom_call" | custom-call | flops 5000000000 | bytes 16777216 | tf_op jit(solution)/shard_map/local_products/pallas_call | solution.py:326
  63.6 7.9 %collective-permute-start.4 = (f32[256,128]{1,0:T(8,128)S(1)}, f32[256,128]{1,0:T(8,128)S(1)}, u32[]{:S(2)}, u32[]{:S(2)}) collective-permute-start(f32[256,128]{1,0:T(8,128)S(1)} %get-tuple-element.30), channel_id=1, source_target_pairs={{0,8},{8,16},{16,24},{24,32},{32,40},{40,48},{48,56},{56,64},{64,7... | collective-permute-start | bytes 393224 | tf_op jit(solution)/shard_map/ppermute | solution.py:263
  71.5 0.0 collective-permute-done.3.rows_ref
  71.5 8.5 %assembled.4.summed_ref = f32[2048,128]{1,0:T(8,128)S(1)} custom-call(s32[8,512]{1,0:T(8,128)S(1)} %copy-done.1, f32[4096,128]{1,0:T(8,128)S(1)} %get-tuple-element.28.products_ref, bf16[4096,512]{1,0:T(8,128)(2,1)S(1)} %get-tuple-element.23.spread_ref, bf16[256,128]{1,0:T(8,128)(2,1)S(1)} %collective-permute-done.3.rows_ref), custom_call_target="tpu_custom_call" | custom-call | flops 5000000000 | bytes 16777216 | tf_op jit(solution)/shard_map/assembled/pallas_call | solution.py:328
  80.0 0.0 collective-permute-done.4.arrived_ref
  80.1 1.8 next_step.1
  81.9 1.5 collective-permute-start.5
  83.3 8.8 %local_products.5 = (f32[4096,128]{1,0:T(8,128)S(1)}, f32[256,128]{1,0:T(8,128)S(1)}) custom-call(s32[8,512]{1,0:T(8,128)S(1)} %copy-done.1, s32[8,4096]{1,0:T(8,128)S(1)} %broadcast_in_dim.29.links_ref, f32[2304,128]{1,0:T(8,128)S(1)} %get-tuple-element.32.scaled_ref, bf16[8,512,512]{2,1,0:T(8,128)(2,1)S(1)} %copy-done.5), custom_call_target="tpu_custom_call" | custom-call | flops 5000000000 | bytes 16777216 | tf_op jit(solution)/shard_map/local_products/pallas_call | solution.py:326
  92.2 7.9 %collective-permute-start.6 = (f32[256,128]{1,0:T(8,128)S(1)}, f32[256,128]{1,0:T(8,128)S(1)}, u32[]{:S(2)}, u32[]{:S(2)}) collective-permute-start(f32[256,128]{1,0:T(8,128)S(1)} %get-tuple-element.35), channel_id=1, source_target_pairs={{0,8},{8,16},{16,24},{24,32},{32,40},{40,48},{48,56},{56,64},{64,7... | collective-permute-start | bytes 393224 | tf_op jit(solution)/shard_map/ppermute | solution.py:263
  100.1 0.0 collective-permute-done.5.rows_ref
  100.1 8.5 %assembled.5.summed_ref = f32[2048,128]{1,0:T(8,128)S(1)} custom-call(s32[8,512]{1,0:T(8,128)S(1)} %copy-done.1, f32[4096,128]{1,0:T(8,128)S(1)} %get-tuple-element.33.products_ref, bf16[4096,512]{1,0:T(8,128)(2,1)S(1)} %get-tuple-element.23.spread_ref, bf16[256,128]{1,0:T(8,128)(2,1)S(1)} %collective-permute-done.5.rows_ref), custom_call_target="tpu_custom_call" | custom-call | flops 5000000000 | bytes 16777216 | tf_op jit(solution)/shard_map/assembled/pallas_call | solution.py:328
  108.6 0.0 collective-permute-done.6.arrived_ref
  108.6 1.5 filtered.1
  110.2 0.0 all-gather.2.cloned.1.call-update
  110.2 23.8 %all_to_all.35.rows_ref = bf16[8,256,128]{2,1,0:T(8,128)(2,1)S(1)} all-to-all(bf16[8,256,128]{2,1,0:T(8,128)(2,1)} %bitcast.2), channel_id=1, replica_groups=mesh['dom_0'=4,'dom_1'=4,'dom_2'=2,'band_0'=4,'band_1'=2] {'band_0','ban..., dimensions={0} | all-to-all | bytes 1048576 | tf_op jit(solution)/shard_map/all_to_all | solution.py:267
  134.0 0.5 gram.1
  134.5 5.4 %all_to_all.36 = bf16[2,2304,128]{2,1,0:T(8,128)(2,1)S(1)} all-to-all(bf16[2,2304,128]{2,1,0:T(8,128)(2,1)S(1)} %bitcast.10), channel_id=1, replica_groups=mesh['dom_0'=4,'dom_1'=4,'dom_2'=2,'band_0'=4,'band_1'=2] {'band_1'}, dimensions={0} | all-to-all | bytes 2359296 | tf_op jit(solution)/shard_map/all_to_all | solution.py:267
  140.0 0.6 reduce_sum.36
  140.5 31.1 %all_to_all.37 = bf16[16,144,128]{2,1,0:T(8,128)(2,1)S(1)} all-to-all(bf16[16,144,128]{2,1,0:T(8,128)(2,1)S(1)} %bitcast.16), channel_id=1, replica_groups=mesh['dom_0'=4,'dom_1'=4,'dom_2'=2,'band_0'=4,'band_1'=2] {'dom_0','dom_1'}, dimensions={0} | all-to-all | bytes 1179648 | tf_op jit(solution)/shard_map/all_to_all | solution.py:267
  171.7 0.1 reduce_sum.37
  171.8 12.2 %all_to_all.38 = bf16[8,18,128]{2,1,0:T(8,128)(2,1)S(1)} all-to-all(bf16[8,18,128]{2,1,0:T(8,128)(2,1)S(1)} %reshape.30), channel_id=1, replica_groups=mesh['dom_0'=4,'dom_1'=4,'dom_2'=2,'band_0'=4,'band_1'=2] {'dom_2','band..., dimensions={0} | all-to-all | bytes 73728 | tf_op jit(solution)/shard_map/all_to_all | solution.py:267
  184.0 9.4 %all_to_all.39 = bf16[8,18,128]{2,1,0:T(8,128)(2,1)S(1)} all-to-all(bf16[8,18,128]{2,1,0:T(8,128)(2,1)S(1)} %broadcast_in_dim.31), channel_id=1, replica_groups=mesh['dom_0'=4,'dom_1'=4,'dom_2'=2,'band_0'=4,'band_1'=2] {'dom_2','band..., dimensions={0} | all-to-all | bytes 73728 | tf_op jit(solution)/shard_map/all_to_all | solution.py:267
  193.4 0.9 broadcast_in_dim.32
  194.3 3.8 %all-to-all-start.5 = ((bf16[16,144,128]{2,1,0:T(8,128)(2,1)}), bf16[16,144,128]{2,1,0:T(8,128)(2,1)S(1)}, u32[]{:S(2)}, u32[]{:S(2)}) async-start(bf16[16,144,128]{2,1,0:T(8,128)(2,1)} %broadcast_in_dim.32), calls=%async_computation.5 | async-start | bytes 1179648 | tf_op jit(solution)/shard_map/all_to_all | solution.py:267
  198.1 9.6 %all-to-all-done.5 = bf16[16,144,128]{2,1,0:T(8,128)(2,1)S(1)} async-done(((bf16[16,144,128]{2,1,0:T(8,128)(2,1)}), bf16[16,144,128]{2,1,0:T(8,128)(2,1)S(1)}, u32[]{:S(2)}, u32[]{:S(2)}) %all-to-all-start.5) | async-done | bytes 589856 | tf_op jit(solution)/shard_map/all_to_all | solution.py:267
  207.7 0.1 broadcast_in_dim.33
  207.8 9.5 %all_to_all.40 = bf16[2,2304,128]{2,1,0:T(8,128)(2,1)S(1)} all-to-all(bf16[2,2304,128]{2,1,0:T(8,128)(2,1)S(1)} %broadcast_in_dim.33), channel_id=1, replica_groups=mesh['dom_0'=4,'dom_1'=4,'dom_2'=2,'band_0'=4,'band_1'=2] {'band_1'}, dimensions={0} | all-to-all | bytes 2359296 | tf_op jit(solution)/shard_map/all_to_all | solution.py:267
  217.2 2.2 copy-done.6
  219.4 7.8 %rotated.1 = f32[2048,128]{1,0:T(8,128)} custom-call(s32[1]{0:T(128)} %bitcast.band_ref, bf16[36,128,128]{2,1,0:T(8,128)(2,1)S(1)} %bitcast.9, bf16[16384,128]{1,0:T(8,128)(2,1)S(1)} %copy-done.6), custom_call_target="tpu_custom_call" | custom-call | flops 3000000000 | bytes 8388608 | tf_op jit(solution)/shard_map/rotated/pallas_call | solution.py:360
  (16 shorter events, 0.1 us)
Async XLA Ops:
  6.5 1.1 copy-start
  6.5 4.1 %copy-start.1 = (s32[8,512]{1,0:T(8,128)S(1)}, s32[8,512]{1,0:T(8,128)}, u32[]{:S(2)}) copy-start(s32[8,512]{1,0:T(8,128)} %index_ref.11) | copy-start | bytes 49156
  6.5 210.7 %all-gather.2.cloned.1.call-start = ((), (), s32[]{:S(2)}) async-start(), calls=%async_computation.7 | async-start | bytes 4718592 | tf_op jit(solution)/shard_map/all_gather | solution.py:348
  7.6 0.7 copy-start.2
  9.4 33.8 %collective-permute-start = (bf16[256,128]{1,0:T(8,128)(2,1)S(1)}, bf16[256,128]{1,0:T(8,128)(2,1)S(1)}, u32[]{:S(2)}, u32[]{:S(2)}) collective-permute-start(bf16[256,128]{1,0:T(8,128)(2,1)S(1)} %get-tuple-element.24.rows_ref), channel_id=1, source_target_pairs={{8,0},{16,8},{24,16},{32,24},{40,32},{48,40},{56,48},{64,56},{72,6... | collective-permute-start | bytes 196616 | tf_op jit(solution)/shard_map/ppermute | solution.py:263
  10.7 2.2 copy-start.4
  12.9 19.1 %copy-start.5 = (bf16[8,512,512]{2,1,0:T(8,128)(2,1)S(1)}, bf16[8,512,512]{2,1,0:T(8,128)(2,1)}, u32[]{:S(2)}) copy-start(bf16[8,512,512]{2,1,0:T(8,128)(2,1)} %cells_ref.7) | copy-start | bytes 12582916
  21.7 30.0 %collective-permute-start.1 = (f32[256,128]{1,0:T(8,128)S(1)}, f32[256,128]{1,0:T(8,128)S(1)}, u32[]{:S(2)}, u32[]{:S(2)}) collective-permute-start(f32[256,128]{1,0:T(8,128)S(1)} %get-tuple-element.25), channel_id=1, source_target_pairs={{0,8},{8,16},{16,24},{24,32},{32,40},{40,48},{48,56},{56,64},{64,7... | collective-permute-start | bytes 393224 | tf_op jit(solution)/shard_map/ppermute | solution.py:263
  35.0 16.7 %collective-permute-start.2 = (f32[256,256]{1,0:T(8,128)S(1)}, f32[256,256]{1,0:T(8,128)S(1)}, u32[]{:S(2)}, u32[]{:S(2)}) collective-permute-start(f32[256,256]{1,0:T(8,128)S(1)} %get-tuple-element.26), channel_id=1, source_target_pairs={{0,8},{8,16},{16,24},{24,32},{32,40},{40,48},{48,56},{56,64},{64,7... | collective-permute-start | bytes 786440 | tf_op jit(solution)/shard_map/ppermute | solution.py:263
  43.2 8.6 %copy-start.3 = (s32[256]{0:T(256)S(1)}, s32[256]{0:T(256)}, u32[]{:S(2)}) copy-start(s32[256]{0:T(256)} %param.9) | copy-start | bytes 3076
  53.5 18.1 %collective-permute-start.3 = (bf16[256,128]{1,0:T(8,128)(2,1)S(1)}, bf16[256,128]{1,0:T(8,128)(2,1)S(1)}, u32[]{:S(2)}, u32[]{:S(2)}) collective-permute-start(bf16[256,128]{1,0:T(8,128)(2,1)S(1)} %get-tuple-element.29.rows_ref), channel_id=1, source_target_pairs={{8,0},{16,8},{24,16},{32,24},{40,32},{48,40},{56,48},{64,56},{72,6... | collective-permute-start | bytes 196616 | tf_op jit(solution)/shard_map/ppermute | solution.py:263
  63.6 16.4 %collective-permute-start.4 = (f32[256,128]{1,0:T(8,128)S(1)}, f32[256,128]{1,0:T(8,128)S(1)}, u32[]{:S(2)}, u32[]{:S(2)}) collective-permute-start(f32[256,128]{1,0:T(8,128)S(1)} %get-tuple-element.30), channel_id=1, source_target_pairs={{0,8},{8,16},{16,24},{24,32},{32,40},{40,48},{48,56},{56,64},{64,7... | collective-permute-start | bytes 393224 | tf_op jit(solution)/shard_map/ppermute | solution.py:263
  81.9 18.2 %collective-permute-start.5 = (bf16[256,128]{1,0:T(8,128)(2,1)S(1)}, bf16[256,128]{1,0:T(8,128)(2,1)S(1)}, u32[]{:S(2)}, u32[]{:S(2)}) collective-permute-start(bf16[256,128]{1,0:T(8,128)(2,1)S(1)} %get-tuple-element.34.rows_ref), channel_id=1, source_target_pairs={{8,0},{16,8},{24,16},{32,24},{40,32},{48,40},{56,48},{64,56},{72,6... | collective-permute-start | bytes 196616 | tf_op jit(solution)/shard_map/ppermute | solution.py:263
  92.2 16.4 %collective-permute-start.6 = (f32[256,128]{1,0:T(8,128)S(1)}, f32[256,128]{1,0:T(8,128)S(1)}, u32[]{:S(2)}, u32[]{:S(2)}) collective-permute-start(f32[256,128]{1,0:T(8,128)S(1)} %get-tuple-element.35), channel_id=1, source_target_pairs={{0,8},{8,16},{16,24},{24,32},{32,40},{40,48},{48,56},{56,64},{64,7... | collective-permute-start | bytes 393224 | tf_op jit(solution)/shard_map/ppermute | solution.py:263
  194.3 13.4 %all-to-all-start.5 = ((bf16[16,144,128]{2,1,0:T(8,128)(2,1)}), bf16[16,144,128]{2,1,0:T(8,128)(2,1)S(1)}, u32[]{:S(2)}, u32[]{:S(2)}) async-start(bf16[16,144,128]{2,1,0:T(8,128)(2,1)} %broadcast_in_dim.32), calls=%async_computation.5 | async-start | bytes 1179648 | tf_op jit(solution)/shard_map/all_to_all | solution.py:267
  217.2 2.2 copy-start.6
Sparse Core Ops, SparseCore 0:
  110.3 66.1 all-gather.1

commit v2 on v1

--- a/solution.py
+++ b/solution.py
@@ -16,12 +16,13 @@
 BAND = ("band_0", "band_1")
 PLANE = ("dom_0", "dom_1")
 COLUMN = ("dom_2", "band_0")
+CHIP = ("band_0",)
 CORE = ("band_1",)
 F32 = jnp.float32
 BF16 = jnp.bfloat16
 IN_VMEM = pl.BlockSpec(memory_space=pltpu.VMEM)
 IN_SMEM = pl.BlockSpec(memory_space=pltpu.SMEM)
-IN_ANY = pl.BlockSpec(memory_space=pl.ANY)
+IN_HBM = pl.BlockSpec(memory_space=pltpu.HBM)
 
 
 def shape(dims, dtype):
@@ -93,7 +94,12 @@
     block_ref[...] = total[:, :face] + total[:, face:]
 
 
-def local_body(own, face, index_ref, links_ref, scaled_ref, cells_ref, products_ref, sent_ref, held):
+def local_body(
+    own, face, index_ref, links_ref, scaled_ref, matrices_ref, products_ref, sent_ref, held,
+    cells_ref, sem,
+):
+    copy = pltpu.make_async_copy(matrices_ref, cells_ref, sem)
+    copy.start()
     cells, nodes, _ = cells_ref.shape
     width = scaled_ref.shape[1]
 
@@ -104,6 +110,7 @@
         return carry
 
     lax.fori_loop(0, nodes // 8, take, 0)
+    copy.wait()
     total = jnp.zeros((face, 2 * width), F32)
     for cell in range(cells):
         part = slice(cell * nodes, (cell + 1) * nodes)
@@ -191,19 +198,30 @@
     ).astype(BF16)
 
 
-def gram_body(rows_ref, blocks_ref):
-    groups = rows_ref.shape[0]
-    width = rows_ref.shape[2]
-    every = jnp.concatenate([rows_ref[g] for g in range(groups)], 1)
-    at = 0
-    for g in range(groups):
-        panel = lax.dot_general(
-            rows_ref[g], every[:, g * width :], (((0,), (0,)), ((), ())),
-            preferred_element_type=F32,
-        )
-        for h in range(groups - g):
-            blocks_ref[at] = panel[:, h * width : (h + 1) * width].astype(BF16)
-            at += 1
+def gram_body(core_ref, rows_ref, blocks_ref):
+    cores, chips = rows_ref.shape[:2]
+    width = rows_ref.shape[3]
+    groups = chips * cores
+    group = [rows_ref[g % cores, g // cores] for g in range(groups)]
+    half = blocks_ref.shape[0]
+
+    def blocks(first):
+        at = 0
+        for g in range(groups):
+            wanted = [h for h in range(g, groups) if first <= at + h - g < first + half]
+            if wanted:
+                panel = lax.dot_general(
+                    group[g], jnp.concatenate([group[h] for h in wanted], 1),
+                    (((0,), (0,)), ((), ())), preferred_element_type=F32,
+                )
+                for i, h in enumerate(wanted):
+                    blocks_ref[at + h - g - first] = panel[
+                        :, i * width : (i + 1) * width
+                    ].astype(BF16)
+            at += groups - g
+
+    for core in range(cores):
+        pl.when(core_ref[0] == core)(functools.partial(blocks, core * half))
 
 
 def rotate_body(nodes, band_ref, blocks_ref, every_ref, rotated_ref, gram, rows, sem):
@@ -219,15 +237,13 @@
     at = 0
     for g in range(groups):
         for h in range(g, groups):
-            block = blocks_ref[at].astype(F32)
+            block = blocks_ref[at]
             at += 1
-            gram[g * width : (g + 1) * width, h * width : (h + 1) * width] = block.astype(BF16)
+            gram[g * width : (g + 1) * width, h * width : (h + 1) * width] = block
             if h == g:
-                diagonal = diagonal + jnp.where(same, block, 0.0)
+                diagonal = diagonal + jnp.where(same, block.astype(F32), 0.0)
             else:
-                gram[h * width : (h + 1) * width, g * width : (g + 1) * width] = block.T.astype(
-                    BF16
-                )
+                gram[h * width : (h + 1) * width, g * width : (g + 1) * width] = block.T
     trace = jnp.sum(jnp.sum(diagonal, axis=0, keepdims=True), axis=1, keepdims=True)
     unit = states / trace
     first = pl.multiple_of(band_ref[0] * width, width)
@@ -307,9 +323,14 @@
         [], 3 * 10**9, 8 * 2**20,
     )
     local = call(
-        functools.partial(local_body, own, face), "local_products", [IN_SMEM] + [IN_VMEM] * 3,
+        functools.partial(local_body, own, face), "local_products", [IN_SMEM] + [IN_VMEM] * 2 + [IN_HBM],
         [shape((entries, width), F32), shape((face, width), F32)],
-        [pltpu.VMEM((entries, width), F32)], 5 * 10**9, 16 * 2**20,
+        [
+            pltpu.VMEM((entries, width), F32),
+            pltpu.VMEM(cell_matrices.shape, BF16),
+            pltpu.SemaphoreType.DMA,
+        ],
+        5 * 10**9, 16 * 2**20,
     )
     assemble = call(
         assemble_body, "assembled", [IN_SMEM] + [IN_VMEM] * 3, wide,
@@ -345,20 +366,27 @@
             )(face_list, faces, *parts, previous, current)
             previous, current = current, following
 
+    chips, cores = lax.axis_size(CHIP), lax.axis_size(CORE)
+    mine = exchanged(rounded.reshape(chips, own // chips, width), CHIP)
+    rounded, mine = lax.optimization_barrier((rounded, mine))
     every = lax.all_gather(rounded, BAND, axis=0, tiled=True)
-    nodes_rows = exchanged(rounded.reshape(bands, own // bands, width), BAND)
+    both = exchanged(jnp.broadcast_to(mine, (cores, *mine.shape)), CORE)
     pairs = bands * (bands + 1) // 2
+    half = pairs // cores
+    core = lax.axis_index(CORE).astype(jnp.int32).reshape(1)
     gram = call(
-        gram_body, "gram", [IN_VMEM], shape((pairs, width, width), BF16), [], 10**9, 2 * 2**20,
-    )(nodes_rows)
-    gram = gram.reshape(pairs * width, width)
-    for axes in (CORE, PLANE, COLUMN):
-        gram = sum_of_share(gram, axes)
-    for axes in (COLUMN, PLANE, CORE):
+        gram_body, "gram", [IN_SMEM, IN_VMEM], shape((half, width, width), BF16), [],
+        10**9, 3 * 2**20,
+    )(core, both)
+    gram = sum_of_share(gram.reshape(half * width, width), PLANE)
+    columns = lax.axis_size(COLUMN)
+    gram = exchanged(jnp.broadcast_to(gram, (columns, *gram.shape)), COLUMN)
+    gram = gram.astype(F32).sum(axis=0).astype(BF16)
+    for axes in (PLANE, CORE):
         gram = shares_of_all(gram, axes)
     band = lax.axis_index(BAND).astype(jnp.int32).reshape(1)
     return call(
-        functools.partial(rotate_body, own * domains), "rotated", [IN_SMEM, IN_VMEM, IN_ANY], wide,
+        functools.partial(rotate_body, own * domains), "rotated", [IN_SMEM, IN_VMEM, IN_HBM], wide,
         [
             pltpu.VMEM((bands * width, bands * width), BF16),
             pltpu.VMEM((bands * own, width), BF16),

time: 235 us -> 225 us (0.957)
  blocking collectives: 91.4 us -> 79.5 us
    all_to_all x6 -> x5, blocking collectives: 91.4 us -> 79.5 us  [exchanged(): return lax.all_to_all(pieces, axes, split_axis=0, concat_axis=0, tiled=True)]
    unnamed x15 -> x17, local copies, waits for them, and re-layouts: 5.07 us -> 6.11 us
  transfers between devices with their start and end apart: 9 -> 9, of which waited for: 1 -> 1; matrix products, arithmetic and copies ran while one was open for 1% -> 1% of each run, Pallas kernels for 24% -> 25%
where the time goes in v2:
time: 225 us
  blocking collectives  79.5 us (35%)
  Pallas kernels  70.5 us (31%)
  starting transfers between devices  41.9 us (19%)
  between operations  13.7 us (6%)
  waiting for transfers between devices  10.5 us (5%)
  local copies, waits for them, and re-layouts  8.3 us (4%)
    all_to_all x5, blocking collectives, exchanged(): return lax.all_to_all(pieces, axes, split_axis=0, concat_axis=0, tiled=True)  79.5 us
    ppermute x7, starting transfers between devices, passed_along(): lax.ppermute(value, DOM, [(source, source + steps) for source in range(in...  38.3 us
    pallas_call x3, Pallas kernels, on_device(): products, sent = local(connectivity, links, scaled, cell_matrices)  27.3 us
    pallas_call x3, Pallas kernels, on_device(): summed = assemble(connectivity, products, spread, received)  25.5 us
    all_to_all x1, waiting for transfers between devices, exchanged(): return lax.all_to_all(pieces, axes, split_axis=0, concat_axis=0, tiled=True)  10.4 us
    pallas_call x1, Pallas kernels, on_device(): call(functools.partial(rotate_body, own * domains), 'rotated', [IN_SMEM,...  7.89 us
    unnamed x17, local copies, waits for them, and re-layouts  6.11 us
  transfers between devices with their start and end apart: 9, of which 1 were waited for; matrix products, arithmetic and copies ran while one was open for 1% of the time, Pallas kernels for 25%

profile of v2, /device:TPU:1, one launch (start us, length us, event | category | flops | bytes accessed | tf_op | source)
XLA Modules:
  0.0 224.5 jit_solution(5382765949581399480)
XLA Ops:
  6.5 1.0 broadcast_in_dim.33.mass_ref
  7.6 0.0 copy-start
  7.6 1.0 copy-done
  8.6 0.7 copy-done.3
  9.3 1.1 scaled_start.1
  10.4 1.3 collective-permute-start
  11.7 0.0 copy-start.5
  11.7 2.2 copy-done.5
  13.9 9.1 %local_products.3 = (f32[4096,128]{1,0:T(8,128)S(1)}, f32[256,128]{1,0:T(8,128)S(1)}) custom-call(s32[8,512]{1,0:T(8,128)S(1)} %copy-done.2, s32[8,4096]{1,0:T(8,128)S(1)} %broadcast_in_dim.32.links_ref, f32[2304,128]{1,0:T(8,128)S(1)} %get-tuple-element.23.scaled_ref, bf16[8,512,512]{2,1,0:T(8,128)(2,1)S(1)} %copy-done.5), custom_call_target="tpu_custom_call" | custom-call | flops 5000000000 | bytes 16777216 | tf_op jit(solution)/shard_map/local_products/pallas_call | solution.py:347
  23.0 10.3 %collective-permute-start.1 = (f32[256,128]{1,0:T(8,128)S(1)}, f32[256,128]{1,0:T(8,128)S(1)}, u32[]{:S(2)}, u32[]{:S(2)}) collective-permute-start(f32[256,128]{1,0:T(8,128)S(1)} %get-tuple-element.27), channel_id=1, source_target_pairs={{0,8},{8,16},{16,24},{24,32},{32,40},{40,48},{48,56},{56,64},{64,7... | collective-permute-start | bytes 393224 | tf_op jit(solution)/shard_map/ppermute | solution.py:279
  33.3 3.0 %face_matrix.1 = (bf16[4096,512]{1,0:T(8,128)(2,1)S(1)}, f32[256,256]{1,0:T(8,128)S(1)}) custom-call(s32[8,4096]{1,0:T(8,128)S(1)} %broadcast_in_dim.32.links_ref, bf16[8,512,512]{2,1,0:T(8,128)(2,1)S(1)} %copy-done.6), custom_call_target="tpu_custom_call" | custom-call | flops 3000000000 | bytes 8388608 | tf_op jit(solution)/shard_map/face_matrix/pallas_call | solution.py:342
  36.3 8.2 %collective-permute-start.2 = (f32[256,256]{1,0:T(8,128)S(1)}, f32[256,256]{1,0:T(8,128)S(1)}, u32[]{:S(2)}, u32[]{:S(2)}) collective-permute-start(f32[256,256]{1,0:T(8,128)S(1)} %get-tuple-element.28), channel_id=1, source_target_pairs={{0,8},{8,16},{16,24},{24,32},{32,40},{40,48},{48,56},{56,64},{64,7... | collective-permute-start | bytes 786440 | tf_op jit(solution)/shard_map/ppermute | solution.py:279
  44.5 0.0 collective-permute-done.rows_ref
  44.5 0.0 copy-start.4
  44.5 0.0 copy-start.1
  44.5 8.5 %assembled.3.summed_ref = f32[2048,128]{1,0:T(8,128)S(1)} custom-call(s32[8,512]{1,0:T(8,128)S(1)} %copy-done.2, f32[4096,128]{1,0:T(8,128)S(1)} %get-tuple-element.24.products_ref, bf16[4096,512]{1,0:T(8,128)(2,1)S(1)} %get-tuple-element.25.spread_ref, bf16[256,128]{1,0:T(8,128)(2,1)S(1)} %collective-permute-done.rows_ref), custom_call_target="tpu_custom_call" | custom-call | flops 5000000000 | bytes 16777216 | tf_op jit(solution)/shard_map/assembled/pallas_call | solution.py:349
  53.0 0.0 collective-permute-done.1.arrived_ref
  53.0 0.0 collective-permute-done.2.block_ref
  53.1 1.7 first_step.1
  54.7 1.3 collective-permute-start.3
  56.0 9.1 %local_products.4 = (f32[4096,128]{1,0:T(8,128)S(1)}, f32[256,128]{1,0:T(8,128)S(1)}) custom-call(s32[8,512]{1,0:T(8,128)S(1)} %copy-done.2, s32[8,4096]{1,0:T(8,128)S(1)} %broadcast_in_dim.32.links_ref, f32[2304,128]{1,0:T(8,128)S(1)} %get-tuple-element.29.scaled_ref, bf16[8,512,512]{2,1,0:T(8,128)(2,1)S(1)} %copy-done.6), custom_call_target="tpu_custom_call" | custom-call | flops 5000000000 | bytes 16777216 | tf_op jit(solution)/shard_map/local_products/pallas_call | solution.py:347
  65.2 7.9 %collective-permute-start.4 = (f32[256,128]{1,0:T(8,128)S(1)}, f32[256,128]{1,0:T(8,128)S(1)}, u32[]{:S(2)}, u32[]{:S(2)}) collective-permute-start(f32[256,128]{1,0:T(8,128)S(1)} %get-tuple-element.32), channel_id=1, source_target_pairs={{0,8},{8,16},{16,24},{24,32},{32,40},{40,48},{48,56},{56,64},{64,7... | collective-permute-start | bytes 393224 | tf_op jit(solution)/shard_map/ppermute | solution.py:279
  73.1 0.0 collective-permute-done.3.rows_ref
  73.1 8.5 %assembled.4.summed_ref = f32[2048,128]{1,0:T(8,128)S(1)} custom-call(s32[8,512]{1,0:T(8,128)S(1)} %copy-done.2, f32[4096,128]{1,0:T(8,128)S(1)} %get-tuple-element.30.products_ref, bf16[4096,512]{1,0:T(8,128)(2,1)S(1)} %get-tuple-element.25.spread_ref, bf16[256,128]{1,0:T(8,128)(2,1)S(1)} %collective-permute-done.3.rows_ref), custom_call_target="tpu_custom_call" | custom-call | flops 5000000000 | bytes 16777216 | tf_op jit(solution)/shard_map/assembled/pallas_call | solution.py:349
  81.6 0.0 collective-permute-done.4.arrived_ref
  81.6 1.8 next_step.1
  83.4 1.5 collective-permute-start.5
  84.9 9.1 %local_products.5 = (f32[4096,128]{1,0:T(8,128)S(1)}, f32[256,128]{1,0:T(8,128)S(1)}) custom-call(s32[8,512]{1,0:T(8,128)S(1)} %copy-done.2, s32[8,4096]{1,0:T(8,128)S(1)} %broadcast_in_dim.32.links_ref, f32[2304,128]{1,0:T(8,128)S(1)} %get-tuple-element.34.scaled_ref, bf16[8,512,512]{2,1,0:T(8,128)(2,1)S(1)} %copy-done.6), custom_call_target="tpu_custom_call" | custom-call | flops 5000000000 | bytes 16777216 | tf_op jit(solution)/shard_map/local_products/pallas_call | solution.py:347
  94.0 7.9 %collective-permute-start.6 = (f32[256,128]{1,0:T(8,128)S(1)}, f32[256,128]{1,0:T(8,128)S(1)}, u32[]{:S(2)}, u32[]{:S(2)}) collective-permute-start(f32[256,128]{1,0:T(8,128)S(1)} %get-tuple-element.37), channel_id=1, source_target_pairs={{0,8},{8,16},{16,24},{24,32},{32,40},{40,48},{48,56},{56,64},{64,7... | collective-permute-start | bytes 393224 | tf_op jit(solution)/shard_map/ppermute | solution.py:279
  101.9 0.0 collective-permute-done.5.rows_ref
  101.9 8.5 %assembled.5.summed_ref = f32[2048,128]{1,0:T(8,128)S(1)} custom-call(s32[8,512]{1,0:T(8,128)S(1)} %copy-done.2, f32[4096,128]{1,0:T(8,128)S(1)} %get-tuple-element.35.products_ref, bf16[4096,512]{1,0:T(8,128)(2,1)S(1)} %get-tuple-element.25.spread_ref, bf16[256,128]{1,0:T(8,128)(2,1)S(1)} %collective-permute-done.5.rows_ref), custom_call_target="tpu_custom_call" | custom-call | flops 5000000000 | bytes 16777216 | tf_op jit(solution)/shard_map/assembled/pallas_call | solution.py:349
  110.5 0.0 collective-permute-done.6.arrived_ref
  110.5 1.5 filtered.1
  112.0 18.5 %all_to_all.30 = bf16[4,512,128]{2,1,0:T(8,128)(2,1)S(1)} all-to-all(bf16[4,512,128]{2,1,0:T(8,128)(2,1)} %bitcast.3), channel_id=1, replica_groups=mesh['dom_0'=4,'dom_1'=4,'dom_2'=2,'band_0'=4,'band_1'=2] {'band_0'}, dimensions={0} | all-to-all | bytes 1048576 | tf_op jit(solution)/shard_map/all_to_all | solution.py:283
  130.5 0.0 all-gather.2.cloned.1.call-update
  130.6 0.1 broadcast_in_dim.34
  130.7 7.1 %all_to_all.31.rows_ref = bf16[2,4,512,128]{3,2,1,0:T(8,128)(2,1)S(1)} all-to-all(bf16[2,4,512,128]{3,2,1,0:T(8,128)(2,1)S(1)} %broadcast_in_dim.34), channel_id=1, replica_groups=mesh['dom_0'=4,'dom_1'=4,'dom_2'=2,'band_0'=4,'band_1'=2] {'band_1'}, dimensions={0} | all-to-all | bytes 2097152 | tf_op jit(solution)/shard_map/all_to_all | solution.py:283
  137.9 0.7 gram.1
  138.6 24.1 %all_to_all.32 = bf16[16,144,128]{2,1,0:T(8,128)(2,1)S(1)} all-to-all(bf16[16,144,128]{2,1,0:T(8,128)(2,1)S(1)} %bitcast.10), channel_id=1, replica_groups=mesh['dom_0'=4,'dom_1'=4,'dom_2'=2,'band_0'=4,'band_1'=2] {'dom_0','dom_1'}, dimensions={0} | all-to-all | bytes 1179648 | tf_op jit(solution)/shard_map/all_to_all | solution.py:283
  162.7 0.1 reduce_sum.24
  162.8 22.6 %all_to_all.33 = bf16[8,144,128]{2,1,0:T(8,128)(2,1)S(1)} all-to-all(bf16[8,144,128]{2,1,0:T(8,128)(2,1)S(1)} %broadcast_in_dim.35), channel_id=1, replica_groups=mesh['dom_0'=4,'dom_1'=4,'dom_2'=2,'band_0'=4,'band_1'=2] {'dom_2','band..., dimensions={0} | all-to-all | bytes 589824 | tf_op jit(solution)/shard_map/all_to_all | solution.py:283
  185.5 0.9 broadcast_in_dim.36
  186.4 3.6 %all-to-all-start.4 = ((bf16[16,144,128]{2,1,0:T(8,128)(2,1)}), bf16[16,144,128]{2,1,0:T(8,128)(2,1)S(1)}, u32[]{:S(2)}, u32[]{:S(2)}) async-start(bf16[16,144,128]{2,1,0:T(8,128)(2,1)} %broadcast_in_dim.36), calls=%async_computation.4 | async-start | bytes 1179648 | tf_op jit(solution)/shard_map/all_to_all | solution.py:283
  190.0 10.4 %all-to-all-done.4 = bf16[16,144,128]{2,1,0:T(8,128)(2,1)S(1)} async-done(((bf16[16,144,128]{2,1,0:T(8,128)(2,1)}), bf16[16,144,128]{2,1,0:T(8,128)(2,1)S(1)}, u32[]{:S(2)}, u32[]{:S(2)}) %all-to-all-start.4) | async-done | bytes 589856 | tf_op jit(solution)/shard_map/all_to_all | solution.py:283
  200.4 0.1 broadcast_in_dim.37
  200.5 7.1 %all_to_all.34 = bf16[2,2304,128]{2,1,0:T(8,128)(2,1)S(1)} all-to-all(bf16[2,2304,128]{2,1,0:T(8,128)(2,1)S(1)} %broadcast_in_dim.37), channel_id=1, replica_groups=mesh['dom_0'=4,'dom_1'=4,'dom_2'=2,'band_0'=4,'band_1'=2] {'band_1'}, dimensions={0} | all-to-all | bytes 2359296 | tf_op jit(solution)/shard_map/all_to_all | solution.py:283
  207.6 2.2 copy-done.7
  209.7 7.9 %rotated.1 = f32[2048,128]{1,0:T(8,128)} custom-call(s32[1]{0:T(128)} %bitcast.band_ref, bf16[36,128,128]{2,1,0:T(8,128)(2,1)S(1)} %bitcast.9, bf16[16384,128]{1,0:T(8,128)(2,1)S(1)} %copy-done.7), custom_call_target="tpu_custom_call" | custom-call | flops 3000000000 | bytes 8388608 | tf_op jit(solution)/shard_map/rotated/pallas_call | solution.py:388
  (15 shorter events, 0.1 us)
Async XLA Ops:
  6.5 5.1 %copy-start.2 = (s32[8,512]{1,0:T(8,128)S(1)}, s32[8,512]{1,0:T(8,128)}, u32[]{:S(2)}) copy-start(s32[8,512]{1,0:T(8,128)} %index_ref.11) | copy-start | bytes 49156
  6.5 201.0 %all-gather.2.cloned.1.call-start = ((), (), s32[]{:S(2)}) async-start(), calls=%async_computation.6 | async-start | bytes 4718592 | tf_op jit(solution)/shard_map/all_gather | solution.py:372
  7.6 1.0 copy-start
  8.6 0.7 copy-start.3
  10.4 34.1 %collective-permute-start = (bf16[256,128]{1,0:T(8,128)(2,1)S(1)}, bf16[256,128]{1,0:T(8,128)(2,1)S(1)}, u32[]{:S(2)}, u32[]{:S(2)}) collective-permute-start(bf16[256,128]{1,0:T(8,128)(2,1)S(1)} %get-tuple-element.26.rows_ref), channel_id=1, source_target_pairs={{8,0},{16,8},{24,16},{32,24},{40,32},{48,40},{56,48},{64,56},{72,6... | collective-permute-start | bytes 196616 | tf_op jit(solution)/shard_map/ppermute | solution.py:279
  11.7 2.2 copy-start.5
  13.9 19.4 %copy-start.6 = (bf16[8,512,512]{2,1,0:T(8,128)(2,1)S(1)}, bf16[8,512,512]{2,1,0:T(8,128)(2,1)}, u32[]{:S(2)}) copy-start(bf16[8,512,512]{2,1,0:T(8,128)(2,1)} %matrices_ref.5) | copy-start | bytes 12582916
  23.0 30.0 %collective-permute-start.1 = (f32[256,128]{1,0:T(8,128)S(1)}, f32[256,128]{1,0:T(8,128)S(1)}, u32[]{:S(2)}, u32[]{:S(2)}) collective-permute-start(f32[256,128]{1,0:T(8,128)S(1)} %get-tuple-element.27), channel_id=1, source_target_pairs={{0,8},{8,16},{16,24},{24,32},{32,40},{40,48},{48,56},{56,64},{64,7... | collective-permute-start | bytes 393224 | tf_op jit(solution)/shard_map/ppermute | solution.py:279
  36.3 16.7 %collective-permute-start.2 = (f32[256,256]{1,0:T(8,128)S(1)}, f32[256,256]{1,0:T(8,128)S(1)}, u32[]{:S(2)}, u32[]{:S(2)}) collective-permute-start(f32[256,256]{1,0:T(8,128)S(1)} %get-tuple-element.28), channel_id=1, source_target_pairs={{0,8},{8,16},{16,24},{24,32},{32,40},{40,48},{48,56},{56,64},{64,7... | collective-permute-start | bytes 786440 | tf_op jit(solution)/shard_map/ppermute | solution.py:279
  44.5 8.6 %copy-start.4 = (s32[256]{0:T(256)S(1)}, s32[256]{0:T(256)}, u32[]{:S(2)}) copy-start(s32[256]{0:T(256)} %param.9) | copy-start | bytes 3076
  44.5 8.6 %copy-start.1 = (bf16[2048,128]{1,0:T(8,128)(2,1)S(1)}, bf16[2048,128]{1,0:T(8,128)(2,1)}, u32[]{:S(2)}) copy-start(bf16[2048,128]{1,0:T(8,128)(2,1)} %previous_ref.1) | copy-start | bytes 1572868
  54.7 18.3 %collective-permute-start.3 = (bf16[256,128]{1,0:T(8,128)(2,1)S(1)}, bf16[256,128]{1,0:T(8,128)(2,1)S(1)}, u32[]{:S(2)}, u32[]{:S(2)}) collective-permute-start(bf16[256,128]{1,0:T(8,128)(2,1)S(1)} %get-tuple-element.31.rows_ref), channel_id=1, source_target_pairs={{8,0},{16,8},{24,16},{32,24},{40,32},{48,40},{56,48},{64,56},{72,6... | collective-permute-start | bytes 196616 | tf_op jit(solution)/shard_map/ppermute | solution.py:279
  65.2 16.4 %collective-permute-start.4 = (f32[256,128]{1,0:T(8,128)S(1)}, f32[256,128]{1,0:T(8,128)S(1)}, u32[]{:S(2)}, u32[]{:S(2)}) collective-permute-start(f32[256,128]{1,0:T(8,128)S(1)} %get-tuple-element.32), channel_id=1, source_target_pairs={{0,8},{8,16},{16,24},{24,32},{32,40},{40,48},{48,56},{56,64},{64,7... | collective-permute-start | bytes 393224 | tf_op jit(solution)/shard_map/ppermute | solution.py:279
  83.4 18.5 %collective-permute-start.5 = (bf16[256,128]{1,0:T(8,128)(2,1)S(1)}, bf16[256,128]{1,0:T(8,128)(2,1)S(1)}, u32[]{:S(2)}, u32[]{:S(2)}) collective-permute-start(bf16[256,128]{1,0:T(8,128)(2,1)S(1)} %get-tuple-element.36.rows_ref), channel_id=1, source_target_pairs={{8,0},{16,8},{24,16},{32,24},{40,32},{48,40},{56,48},{64,56},{72,6... | collective-permute-start | bytes 196616 | tf_op jit(solution)/shard_map/ppermute | solution.py:279
  94.0 16.4 %collective-permute-start.6 = (f32[256,128]{1,0:T(8,128)S(1)}, f32[256,128]{1,0:T(8,128)S(1)}, u32[]{:S(2)}, u32[]{:S(2)}) collective-permute-start(f32[256,128]{1,0:T(8,128)S(1)} %get-tuple-element.37), channel_id=1, source_target_pairs={{0,8},{8,16},{16,24},{24,32},{32,40},{40,48},{48,56},{56,64},{64,7... | collective-permute-start | bytes 393224 | tf_op jit(solution)/shard_map/ppermute | solution.py:279
  186.4 14.0 %all-to-all-start.4 = ((bf16[16,144,128]{2,1,0:T(8,128)(2,1)}), bf16[16,144,128]{2,1,0:T(8,128)(2,1)S(1)}, u32[]{:S(2)}, u32[]{:S(2)}) async-start(bf16[16,144,128]{2,1,0:T(8,128)(2,1)} %broadcast_in_dim.36), calls=%async_computation.4 | async-start | bytes 1179648 | tf_op jit(solution)/shard_map/all_to_all | solution.py:283
  207.6 2.2 copy-start.7
Sparse Core Ops, SparseCore 0:
  130.7 69.2 all-gather.1

commit v3 on v2

--- a/solution.py
+++ b/solution.py
@@ -22,7 +22,7 @@
 BF16 = jnp.bfloat16
 IN_VMEM = pl.BlockSpec(memory_space=pltpu.VMEM)
 IN_SMEM = pl.BlockSpec(memory_space=pltpu.SMEM)
-IN_HBM = pl.BlockSpec(memory_space=pltpu.HBM)
+IN_ANY = pl.BlockSpec(memory_space=pl.ANY)
 
 
 def shape(dims, dtype):
@@ -80,37 +80,50 @@
     return one_hot(links == lax.broadcasted_iota(jnp.int32, (face, nodes), 0) + own)
 
 
-def face_matrix_body(own, face, links_ref, cells_ref, spread_ref, block_ref):
-    cells, nodes, _ = cells_ref.shape
-    total = jnp.zeros((face, 2 * face), F32)
+def take_entries(index_ref, scaled_ref, held):
+    cells, nodes = index_ref.shape
+
+    def take(i, carry):
+        for cell in range(cells):
+            rows = [scaled_ref[pl.ds(index_ref[cell, i * 8 + u], 1), :] for u in range(8)]
+            held[pl.ds(pl.multiple_of(cell * nodes + i * 8, 8), 8), :] = jnp.concatenate(rows, 0)
+        return carry
+
+    lax.fori_loop(0, nodes // 8, take, 0)
+
+
+def opening_body(
+    own, face, index_ref, links_ref, scaled_ref, matrices_ref, products_ref, spread_ref, sent_ref,
+    held, cells_ref, sem,
+):
+    copy = pltpu.make_async_copy(matrices_ref, cells_ref, sem)
+    copy.start()
+    take_entries(index_ref, scaled_ref, held)
+    copy.wait()
+    cells, nodes = index_ref.shape
+    width = scaled_ref.shape[1]
+    total = jnp.zeros((face, 2 * width), F32)
+    block = jnp.zeros((face, 2 * face), F32)
     for cell in range(cells):
+        part = slice(cell * nodes, (cell + 1) * nodes)
         hits = face_hits(links_ref, own, face, cell, nodes)
         columns = lax.dot_general(
             cells_ref[cell], hits, (((1,), (1,)), ((), ())), preferred_element_type=F32
         )
         both = halves(columns)
-        spread_ref[cell * nodes : (cell + 1) * nodes, :] = both
-        total = total + dot(hits, both)
-    block_ref[...] = total[:, :face] + total[:, face:]
-
-
-def local_body(
-    own, face, index_ref, links_ref, scaled_ref, matrices_ref, products_ref, sent_ref, held,
-    cells_ref, sem,
-):
-    copy = pltpu.make_async_copy(matrices_ref, cells_ref, sem)
-    copy.start()
-    cells, nodes, _ = cells_ref.shape
+        spread_ref[part, :] = both
+        block = block + dot(hits, both)
+        product = dot(cells_ref[cell], held[part, :].astype(BF16))
+        products_ref[part, :] = product
+        total = total + dot(hits, halves(product))
+    sent_ref[:, :width] = total[:, :width] + total[:, width:]
+    sent_ref[:, width:] = block[:, :face] + block[:, face:]
+
+
+def local_body(own, face, index_ref, links_ref, scaled_ref, cells_ref, products_ref, sent_ref, held):
+    take_entries(index_ref, scaled_ref, held)
+    cells, nodes = index_ref.shape
     width = scaled_ref.shape[1]
-
-    def take(i, carry):
-        for cell in range(cells):
-            rows = [scaled_ref[pl.ds(index_ref[cell, i * 8 + u], 1), :] for u in range(8)]
-            held[pl.ds(pl.multiple_of(cell * nodes + i * 8, 8), 8), :] = jnp.concatenate(rows, 0)
-        return carry
-
-    lax.fori_loop(0, nodes // 8, take, 0)
-    copy.wait()
     total = jnp.zeros((face, 2 * width), F32)
     for cell in range(cells):
         part = slice(cell * nodes, (cell + 1) * nodes)
@@ -160,7 +173,8 @@
     own, width = summed_ref.shape
     face = rows_ref.shape[0]
     rows = rows_ref[...]
-    contribution = arrived_ref[...] + dot(halves(block_ref[...]), jnp.concatenate([rows, rows], 0))
+    block = block_ref[:, width:]
+    contribution = arrived_ref[:, :width] + dot(halves(block), jnp.concatenate([rows, rows], 0))
     hits = one_hot(lax.broadcasted_iota(jnp.int32, (own, face), 0) == faces_ref[:1, :])
     added = dot(hits, halves(contribution))
     return mass_ref[...] * (summed_ref[...] + (added[:, :width] + added[:, width:]))
@@ -190,12 +204,12 @@
 
 def last_body(
     faces_ref, summed_ref, arrived_ref, block_ref, rows_ref, mass_ref, previous_ref, current_ref,
-    rounded_ref,
+    filtered_ref, rounded_ref,
 ):
     image = applied(faces_ref, summed_ref, arrived_ref, block_ref, rows_ref, mass_ref)
-    rounded_ref[...] = (
-        2.0 * (image - CENTER * current_ref[...]) / HALF - previous_ref[...].astype(F32)
-    ).astype(BF16)
+    filtered = 2.0 * (image - CENTER * current_ref[...]) / HALF - previous_ref[...].astype(F32)
+    filtered_ref[...] = filtered
+    rounded_ref[...] = filtered.astype(BF16)
 
 
 def gram_body(core_ref, rows_ref, blocks_ref):
@@ -224,53 +238,58 @@
         pl.when(core_ref[0] == core)(functools.partial(blocks, core * half))
 
 
-def rotate_body(nodes, band_ref, blocks_ref, every_ref, rotated_ref, gram, rows, sem):
-    copy = pltpu.make_async_copy(every_ref, rows, sem)
-    copy.start()
-    states = gram.shape[0]
-    width = rotated_ref.shape[1]
-    groups = states // width
+def correct_body(nodes, core_ref, blocks_ref, rows_ref, change_ref, scale_ref, excess, first, second):
+    cores, chips, own, width = rows_ref.shape
+    groups = chips * cores
+    states = groups * width
     same = lax.broadcasted_iota(jnp.int32, (width, width), 0) == lax.broadcasted_iota(
         jnp.int32, (width, width), 1
     )
+    places = [(g, h) for g in range(groups) for h in range(g, groups)]
     diagonal = jnp.zeros((width, width), F32)
-    at = 0
-    for g in range(groups):
-        for h in range(g, groups):
-            block = blocks_ref[at]
-            at += 1
-            gram[g * width : (g + 1) * width, h * width : (h + 1) * width] = block
-            if h == g:
-                diagonal = diagonal + jnp.where(same, block.astype(F32), 0.0)
-            else:
-                gram[h * width : (h + 1) * width, g * width : (g + 1) * width] = block.T
+    for at, (g, h) in enumerate(places):
+        if g == h:
+            diagonal = diagonal + jnp.where(same, blocks_ref[at].astype(F32), 0.0)
     trace = jnp.sum(jnp.sum(diagonal, axis=0, keepdims=True), axis=1, keepdims=True)
     unit = states / trace
-    first = pl.multiple_of(band_ref[0] * width, width)
-    unity = (
-        lax.broadcasted_iota(jnp.int32, (states, width), 0)
-        == lax.broadcasted_iota(jnp.int32, (states, width), 1) + first
-    ).astype(F32)
-
-    def times_y(v):
-        both = dot(gram[...], halves(v))
-        return (both[:, :width] + both[:, width:]) * unit
-
-    once = 1.5 * unity - 0.5 * (gram[:, pl.ds(first, width)].astype(F32) * unit)
-    right = 1.5 * once - 0.5 * times_y(once)
-    middle = times_y(right)
-    product = 1.5 * middle - 0.5 * times_y(middle)
-    root = 1.5 * once - 0.5 * product
-    mean_eigen = trace / (states * nodes)
-    both = halves(root / jnp.sqrt(mean_eigen))
-    copy.wait()
-    own = rotated_ref.shape[0]
-    total = jnp.zeros((own, 2 * width), F32)
-    for g in range(groups):
-        total = total + dot(
-            rows[g * own : (g + 1) * own, :], both[g * width : (g + 1) * width, :]
-        )
-    rotated_ref[...] = total[:, :width] + total[:, width:]
+    for at, (g, h) in enumerate(places):
+        block = blocks_ref[at].astype(F32) * unit
+        if g == h:
+            block = block - same.astype(F32)
+        block = block.astype(BF16)
+        excess[g * width : (g + 1) * width, h * width : (h + 1) * width] = block
+        if g != h:
+            excess[h * width : (h + 1) * width, g * width : (g + 1) * width] = block.T
+    scale = 1.0 / jnp.sqrt(trace / (states * nodes))
+    scale_ref[...] = jnp.broadcast_to(scale, scale_ref.shape)
+
+    def at_core(rows):
+        starts = [pl.multiple_of((cores * p + core_ref[0]) * width, width) for p in range(chips)]
+        return jnp.concatenate([excess[rows, pl.ds(s, width)] for s in starts], 1)
+
+    tall = states // 4
+    parts = [slice(i * tall, (i + 1) * tall) for i in range(4)]
+    for rows in parts:
+        second[rows, :] = at_core(rows)
+    for rows in parts:
+        square = dot(excess[rows, :], second[...])
+        first[rows, :] = (0.0625 * square - 0.3125 * second[rows, :].astype(F32)).astype(BF16)
+    for rows in parts:
+        cube = dot(excess[rows, :], first[...]) + 0.375 * at_core(rows).astype(F32)
+        second[rows, :] = cube.astype(BF16)
+    for rows in parts:
+        added = dot(excess[rows, :], second[...]) - 0.5 * at_core(rows).astype(F32)
+        first[rows, :] = (added * scale).astype(BF16)
+    for p in range(own // width):
+        some = slice(p * width, (p + 1) * width)
+        every = jnp.concatenate([rows_ref[g % cores, g // cores, some, :] for g in range(groups)], 1)
+        change = dot(every, first[...]).astype(BF16)
+        for q in range(chips):
+            change_ref[q, some, :] = change[:, q * width : (q + 1) * width]
+
+
+def finish_body(filtered_ref, change_ref, scale_ref, rotated_ref):
+    rotated_ref[...] = filtered_ref[...] * scale_ref[:1, :] + change_ref[...].astype(F32)
 
 
 def passed_along(value, steps):
@@ -317,20 +336,24 @@
         start_body, "scaled_start", [IN_SMEM] + [IN_VMEM] * 2, [scaled_shape, rows_shape], [picked],
         10**6, 3 * 2**20,
     )
-    face_matrix = call(
-        functools.partial(face_matrix_body, own, face), "face_matrix", [IN_VMEM] * 2,
-        [shape((entries, 2 * face), BF16), shape((face, face), F32)],
-        [], 3 * 10**9, 8 * 2**20,
-    )
-    local = call(
-        functools.partial(local_body, own, face), "local_products", [IN_SMEM] + [IN_VMEM] * 2 + [IN_HBM],
-        [shape((entries, width), F32), shape((face, width), F32)],
+    opening = call(
+        functools.partial(opening_body, own, face), "opening_products",
+        [IN_SMEM] + [IN_VMEM] * 2 + [IN_ANY],
+        [
+            shape((entries, width), F32), shape((entries, 2 * face), BF16),
+            shape((face, width + face), F32),
+        ],
         [
             pltpu.VMEM((entries, width), F32),
             pltpu.VMEM(cell_matrices.shape, BF16),
             pltpu.SemaphoreType.DMA,
         ],
-        5 * 10**9, 16 * 2**20,
+        8 * 10**9, 16 * 2**20, 46,
+    )
+    local = call(
+        functools.partial(local_body, own, face), "local_products", [IN_SMEM] + [IN_VMEM] * 3,
+        [shape((entries, width), F32), shape((face, width), F32)],
+        [pltpu.VMEM((entries, width), F32)], 5 * 10**9, 16 * 2**20,
     )
     assemble = call(
         assemble_body, "assembled", [IN_SMEM] + [IN_VMEM] * 3, wide,
@@ -339,18 +362,20 @@
     )
 
     scaled, rows = start(face_list, wavefunctions, mass)
-    spread, block = face_matrix(links, cell_matrices)
-    block = passed_along(block, 1)
     previous, current = None, wavefunctions
     for sweep in range(DEGREE):
         received = passed_along(rows, -1)
-        products, sent = local(connectivity, links, scaled, cell_matrices)
-        arrived = passed_along(sent, 1)
+        if sweep == 0:
+            products, spread, sent = opening(connectivity, links, scaled, cell_matrices)
+            arrived = block = passed_along(sent, 1)
+        else:
+            products, sent = local(connectivity, links, scaled, cell_matrices)
+            arrived = passed_along(sent, 1)
         summed = assemble(connectivity, products, spread, received)
         parts = (summed, arrived, block, rows, mass)
         if sweep == DEGREE - 1:
-            rounded = call(
-                last_body, "filtered", [IN_VMEM] * 8, shape((own, width), BF16), [],
+            filtered, rounded = call(
+                last_body, "filtered", [IN_VMEM] * 8, [wide, shape((own, width), BF16)], [],
                 10**9, 6 * 2**20,
             )(faces, *parts, previous, current)
         elif sweep == 0:
@@ -368,8 +393,6 @@
 
     chips, cores = lax.axis_size(CHIP), lax.axis_size(CORE)
     mine = exchanged(rounded.reshape(chips, own // chips, width), CHIP)
-    rounded, mine = lax.optimization_barrier((rounded, mine))
-    every = lax.all_gather(rounded, BAND, axis=0, tiled=True)
     both = exchanged(jnp.broadcast_to(mine, (cores, *mine.shape)), CORE)
     pairs = bands * (bands + 1) // 2
     half = pairs // cores
@@ -384,16 +407,21 @@
     gram = gram.astype(F32).sum(axis=0).astype(BF16)
     for axes in (PLANE, CORE):
         gram = shares_of_all(gram, axes)
-    band = lax.axis_index(BAND).astype(jnp.int32).reshape(1)
-    return call(
-        functools.partial(rotate_body, own * domains), "rotated", [IN_SMEM, IN_VMEM, IN_HBM], wide,
+    states = bands * width
+    change, scale = call(
+        functools.partial(correct_body, own * domains), "correction", [IN_SMEM, IN_VMEM, IN_VMEM],
+        [shape(mine.shape, BF16), shape((8, width), F32)],
         [
-            pltpu.VMEM((bands * width, bands * width), BF16),
-            pltpu.VMEM((bands * own, width), BF16),
-            pltpu.SemaphoreType.DMA,
+            pltpu.VMEM((states, states), BF16),
+            pltpu.VMEM((states, chips * width), BF16),
+            pltpu.VMEM((states, chips * width), BF16),
         ],
-        3 * 10**9, 8 * 2**20,
-    )(band, gram.reshape(pairs, width, width), every)
+        4 * 10**9, 8 * 2**20,
+    )(core, gram.reshape(pairs, width, width), both)
+    change = exchanged(change, CHIP).reshape(own, width)
+    return call(finish_body, "rotated", [IN_VMEM] * 3, wide, [], 10**6, 3 * 2**20)(
+        filtered, change, scale
+    )
 
 
 def solution(mesh):

time: 225 us -> 214 us (0.951)
  between operations: 13.7 us -> 0.31 us
  blocking collectives: 79.5 us -> 88.7 us
  local copies, waits for them, and re-layouts: 8.3 us -> 3.12 us
  Pallas kernels: 70.5 us -> 67.9 us
    pallas_call x3 -> x2, Pallas kernels: 27.3 us -> 17.7 us  [on_device(): products, sent = local(connectivity, links, scaled, cell_matrices)]
    all_to_all x5 -> x6, blocking collectives: 79.5 us -> 88.7 us  [exchanged(): return lax.all_to_all(pieces, axes, split_axis=0, concat_axis=0, tiled=True)]
    pallas_call x3 -> x4, Pallas kernels: 12.4 us -> 19.4 us  [the longest x1 11.4 us: on_device(): products, spread, sent = opening(connectivity, links, scaled, cell_matrices)]
    all_to_all x1, starting transfers between devices: 3.59 us -> 9.87 us  [exchanged(): return lax.all_to_all(pieces, axes, split_axis=0, concat_axis=0, tiled=True)]
    ppermute x7 -> x6, starting transfers between devices: 38.3 us -> 32.6 us  [passed_along(): lax.ppermute(value, DOM, [(source, source + steps) for source in range(in...]
    unnamed x17 -> x13, local copies, waits for them, and re-layouts: 6.11 us -> 1.75 us
  transfers between devices with their start and end apart: 9 -> 7, of which waited for: 1 -> 1; matrix products, arithmetic and copies ran while one was open for 1% -> 0% of each run, Pallas kernels for 25% -> 26%
where the time goes in v3:
time: 214 us; the launch traced here: 213 us
  blocking collectives  88.7 us (41%)
  Pallas kernels  67.9 us (32%)
  starting transfers between devices  42.5 us (20%)
  waiting for transfers between devices  10.9 us (5%)
  local copies, waits for them, and re-layouts  3.12 us (1%)
    all_to_all x6, blocking collectives, exchanged(): return lax.all_to_all(pieces, axes, split_axis=0, concat_axis=0, tiled=True)  88.7 us
    ppermute x6, starting transfers between devices, passed_along(): lax.ppermute(value, DOM, [(source, source + steps) for source in range(in...  32.6 us
    pallas_call x3, Pallas kernels, on_device(): summed = assemble(connectivity, products, spread, received)  25.5 us
    pallas_call x2, Pallas kernels, on_device(): products, sent = local(connectivity, links, scaled, cell_matrices)  17.7 us
    pallas_call x1, Pallas kernels, on_device(): products, spread, sent = opening(connectivity, links, scaled, cell_matrices)  11.4 us
    all_to_all x1, waiting for transfers between devices, exchanged(): return lax.all_to_all(pieces, axes, split_axis=0, concat_axis=0, tiled=True)  10.8 us
    all_to_all x1, starting transfers between devices, exchanged(): return lax.all_to_all(pieces, axes, split_axis=0, concat_axis=0, tiled=True)  9.87 us
    pallas_call x1, Pallas kernels, on_device(): call(functools.partial(correct_body, own * domains), 'correction', [IN_SM...  5.36 us
  transfers between devices with their start and end apart: 7, of which 1 were waited for; matrix products, arithmetic and copies ran while one was open for 0% of the time, Pallas kernels for 26%

profile of v3, /device:TPU:1, one launch (start us, length us, event | category | flops | bytes accessed | tf_op | source)
XLA Modules:
  0.0 213.4 jit_solution(3811646999023242194)
XLA Ops:
  0.0 1.0 broadcast_in_dim.33.mass_ref
  1.0 0.0 copy-start
  1.1 1.0 copy-done
  2.1 0.7 copy-done.3
  2.8 1.1 scaled_start.1
  3.8 1.3 collective-permute-start
  5.1 0.0 copy-done.2
  5.2 11.4 %opening_products.1 = (f32[4096,128]{1,0:T(8,128)S(1)}, bf16[4096,512]{1,0:T(8,128)(2,1)S(1)}, f32[256,384]{1,0:T(8,128)S(1)}) custom-call(s32[8,512]{1,0:T(8,128)S(1)} %copy-done.2, s32[8,4096]{1,0:T(8,128)S(1)} %broadcast_in_dim.32.links_ref, f32[2304,128]{1,0:T(8,128)S(1)} %get-tuple-element.24.scaled_ref, bf16[8,512,512]{2,1,0:T(8,128)(2,1)} %cells_ref.3), custom_call_target="tpu_custom_call" | custom-call | flops 8000000000 | bytes 16777216 | tf_op jit(solution)/shard_map/opening_products/pallas_call | solution.py:369
  16.6 10.3 %collective-permute-start.1 = (f32[256,384]{1,0:T(8,128)S(1)}, f32[256,384]{1,0:T(8,128)S(1)}, u32[]{:S(2)}, u32[]{:S(2)}) collective-permute-start(f32[256,384]{1,0:T(8,128)S(1)} %get-tuple-element.28), channel_id=1, source_target_pairs={{0,8},{8,16},{16,24},{24,32},{32,40},{40,48},{48,56},{56,64},{64,7... | collective-permute-start | bytes 1179656 | tf_op jit(solution)/shard_map/ppermute | solution.py:298
  26.9 0.0 collective-permute-done.rows_ref
  26.9 0.0 copy-start.4
  26.9 0.0 copy-start.1
  26.9 0.0 copy-start.5
  27.0 8.5 %assembled.3.summed_ref = f32[2048,128]{1,0:T(8,128)S(1)} custom-call(s32[8,512]{1,0:T(8,128)S(1)} %copy-done.2, f32[4096,128]{1,0:T(8,128)S(1)} %get-tuple-element.25.products_ref, bf16[4096,512]{1,0:T(8,128)(2,1)S(1)} %get-tuple-element.26.spread_ref, bf16[256,128]{1,0:T(8,128)(2,1)S(1)} %collective-permute-done.rows_ref), custom_call_target="tpu_custom_call" | custom-call | flops 5000000000 | bytes 16777216 | tf_op jit(solution)/shard_map/assembled/pallas_call | solution.py:374
  35.5 0.0 collective-permute-done.1.arrived_ref.block_ref
  35.5 0.0 copy-done.4
  35.5 0.0 copy-done.1
  35.5 1.7 first_step.1
  37.2 1.3 collective-permute-start.2
  38.5 0.0 copy-done.5
  38.5 8.8 %local_products.2 = (f32[4096,128]{1,0:T(8,128)S(1)}, f32[256,128]{1,0:T(8,128)S(1)}) custom-call(s32[8,512]{1,0:T(8,128)S(1)} %copy-done.2, s32[8,4096]{1,0:T(8,128)S(1)} %broadcast_in_dim.32.links_ref, f32[2304,128]{1,0:T(8,128)S(1)} %get-tuple-element.29.scaled_ref, bf16[8,512,512]{2,1,0:T(8,128)(2,1)S(1)} %copy-done.5), custom_call_target="tpu_custom_call" | custom-call | flops 5000000000 | bytes 16777216 | tf_op jit(solution)/shard_map/local_products/pallas_call | solution.py:372
  47.4 8.8 %collective-permute-start.3 = (f32[256,128]{1,0:T(8,128)S(1)}, f32[256,128]{1,0:T(8,128)S(1)}, u32[]{:S(2)}, u32[]{:S(2)}) collective-permute-start(f32[256,128]{1,0:T(8,128)S(1)} %get-tuple-element.32), channel_id=1, source_target_pairs={{0,8},{8,16},{16,24},{24,32},{32,40},{40,48},{48,56},{56,64},{64,7... | collective-permute-start | bytes 393224 | tf_op jit(solution)/shard_map/ppermute | solution.py:298
  56.1 0.0 collective-permute-done.2.rows_ref
  56.1 8.5 %assembled.4.summed_ref = f32[2048,128]{1,0:T(8,128)S(1)} custom-call(s32[8,512]{1,0:T(8,128)S(1)} %copy-done.2, f32[4096,128]{1,0:T(8,128)S(1)} %get-tuple-element.30.products_ref, bf16[4096,512]{1,0:T(8,128)(2,1)S(1)} %get-tuple-element.26.spread_ref, bf16[256,128]{1,0:T(8,128)(2,1)S(1)} %collective-permute-done.2.rows_ref), custom_call_target="tpu_custom_call" | custom-call | flops 5000000000 | bytes 16777216 | tf_op jit(solution)/shard_map/assembled/pallas_call | solution.py:374
  64.7 0.0 collective-permute-done.3.arrived_ref
  64.7 1.8 next_step.1
  66.5 1.5 collective-permute-start.4
  68.0 8.8 %local_products.3 = (f32[4096,128]{1,0:T(8,128)S(1)}, f32[256,128]{1,0:T(8,128)S(1)}) custom-call(s32[8,512]{1,0:T(8,128)S(1)} %copy-done.2, s32[8,4096]{1,0:T(8,128)S(1)} %broadcast_in_dim.32.links_ref, f32[2304,128]{1,0:T(8,128)S(1)} %get-tuple-element.34.scaled_ref, bf16[8,512,512]{2,1,0:T(8,128)(2,1)S(1)} %copy-done.5), custom_call_target="tpu_custom_call" | custom-call | flops 5000000000 | bytes 16777216 | tf_op jit(solution)/shard_map/local_products/pallas_call | solution.py:372
  76.8 9.4 %collective-permute-start.5 = (f32[256,128]{1,0:T(8,128)S(1)}, f32[256,128]{1,0:T(8,128)S(1)}, u32[]{:S(2)}, u32[]{:S(2)}) collective-permute-start(f32[256,128]{1,0:T(8,128)S(1)} %get-tuple-element.37), channel_id=1, source_target_pairs={{0,8},{8,16},{16,24},{24,32},{32,40},{40,48},{48,56},{56,64},{64,7... | collective-permute-start | bytes 393224 | tf_op jit(solution)/shard_map/ppermute | solution.py:298
  86.3 0.0 collective-permute-done.4.rows_ref
  86.3 8.5 %assembled.5.summed_ref = f32[2048,128]{1,0:T(8,128)S(1)} custom-call(s32[8,512]{1,0:T(8,128)S(1)} %copy-done.2, f32[4096,128]{1,0:T(8,128)S(1)} %get-tuple-element.35.products_ref, bf16[4096,512]{1,0:T(8,128)(2,1)S(1)} %get-tuple-element.26.spread_ref, bf16[256,128]{1,0:T(8,128)(2,1)S(1)} %collective-permute-done.4.rows_ref), custom_call_target="tpu_custom_call" | custom-call | flops 5000000000 | bytes 16777216 | tf_op jit(solution)/shard_map/assembled/pallas_call | solution.py:374
  94.8 0.0 collective-permute-done.5.arrived_ref
  94.8 1.5 filtered.1
  96.3 9.9 %all-to-all-start = ((bf16[4,512,128]{2,1,0:T(8,128)(2,1)}), bf16[4,512,128]{2,1,0:T(8,128)(2,1)S(1)}, u32[]{:S(2)}, u32[]{:S(2)}) async-start(bf16[4,512,128]{2,1,0:T(8,128)(2,1)} %bitcast.2), calls=%async_computation | async-start | bytes 1048576 | tf_op jit(solution)/shard_map/all_to_all | solution.py:302
  106.2 10.8 %all-to-all-done = bf16[4,512,128]{2,1,0:T(8,128)(2,1)S(1)} async-done(((bf16[4,512,128]{2,1,0:T(8,128)(2,1)}), bf16[4,512,128]{2,1,0:T(8,128)(2,1)S(1)}, u32[]{:S(2)}, u32[]{:S(2)}) %all-to-all-start) | async-done | bytes 524320 | tf_op jit(solution)/shard_map/all_to_all | solution.py:302
  117.0 0.1 broadcast_in_dim.34
  117.2 8.8 %all_to_all.35.rows_ref = bf16[2,4,512,128]{3,2,1,0:T(8,128)(2,1)S(1)} all-to-all(bf16[2,4,512,128]{3,2,1,0:T(8,128)(2,1)S(1)} %broadcast_in_dim.34), channel_id=1, replica_groups=mesh['dom_0'=4,'dom_1'=4,'dom_2'=2,'band_0'=4,'band_1'=2] {'band_1'}, dimensions={0} | all-to-all | bytes 2097152 | tf_op jit(solution)/shard_map/all_to_all | solution.py:302
  126.0 0.7 gram.1
  126.7 25.0 %all_to_all.36 = bf16[16,144,128]{2,1,0:T(8,128)(2,1)S(1)} all-to-all(bf16[16,144,128]{2,1,0:T(8,128)(2,1)S(1)} %bitcast.11), channel_id=1, replica_groups=mesh['dom_0'=4,'dom_1'=4,'dom_2'=2,'band_0'=4,'band_1'=2] {'dom_0','dom_1'}, dimensions={0} | all-to-all | bytes 1179648 | tf_op jit(solution)/shard_map/all_to_all | solution.py:302
  151.7 0.1 reduce_sum.24
  151.8 15.8 %all_to_all.37 = bf16[8,144,128]{2,1,0:T(8,128)(2,1)S(1)} all-to-all(bf16[8,144,128]{2,1,0:T(8,128)(2,1)S(1)} %broadcast_in_dim.35), channel_id=1, replica_groups=mesh['dom_0'=4,'dom_1'=4,'dom_2'=2,'band_0'=4,'band_1'=2] {'dom_2','band..., dimensions={0} | all-to-all | bytes 589824 | tf_op jit(solution)/shard_map/all_to_all | solution.py:302
  167.7 0.1 broadcast_in_dim.36
  167.8 13.4 %all_to_all.38 = bf16[16,144,128]{2,1,0:T(8,128)(2,1)S(1)} all-to-all(bf16[16,144,128]{2,1,0:T(8,128)(2,1)S(1)} %broadcast_in_dim.36), channel_id=1, replica_groups=mesh['dom_0'=4,'dom_1'=4,'dom_2'=2,'band_0'=4,'band_1'=2] {'dom_0','dom_1'}, dimensions={0} | all-to-all | bytes 1179648 | tf_op jit(solution)/shard_map/all_to_all | solution.py:302
  181.2 0.1 broadcast_in_dim.37
  181.3 9.0 %all_to_all.39 = bf16[2,2304,128]{2,1,0:T(8,128)(2,1)S(1)} all-to-all(bf16[2,2304,128]{2,1,0:T(8,128)(2,1)S(1)} %broadcast_in_dim.37), channel_id=1, replica_groups=mesh['dom_0'=4,'dom_1'=4,'dom_2'=2,'band_0'=4,'band_1'=2] {'band_1'}, dimensions={0} | all-to-all | bytes 2359296 | tf_op jit(solution)/shard_map/all_to_all | solution.py:302
  190.3 5.4 %correction.1 = (bf16[4,512,128]{2,1,0:T(8,128)(2,1)S(1)}, f32[8,128]{1,0:T(8,128)S(1)}) custom-call(s32[1]{0:T(128)} %bitcast.1.core_ref, bf16[36,128,128]{2,1,0:T(8,128)(2,1)S(1)} %bitcast.10, bf16[2,4,512,128]{3,2,1,0:T(8,128)(2,1)S(1)} %all_to_all.35.rows_ref), custom_call_target="tpu_custom_call" | custom-call | flops 4000000000 | bytes 8388608 | tf_op jit(solution)/shard_map/correction/pallas_call | solution.py:411
  195.7 16.6 %all_to_all.40 = bf16[4,512,128]{2,1,0:T(8,128)(2,1)S(1)} all-to-all(bf16[4,512,128]{2,1,0:T(8,128)(2,1)S(1)} %get-tuple-element.41), channel_id=1, replica_groups=mesh['dom_0'=4,'dom_1'=4,'dom_2'=2,'band_0'=4,'band_1'=2] {'band_0'}, dimensions={0} | all-to-all | bytes 1048576 | tf_op jit(solution)/shard_map/all_to_all | solution.py:302
  212.3 1.1 rotated.1
  (7 shorter events, 0.1 us)
Async XLA Ops:
  0.0 5.1 %copy-start.2 = (s32[8,512]{1,0:T(8,128)S(1)}, s32[8,512]{1,0:T(8,128)}, u32[]{:S(2)}) copy-start(s32[8,512]{1,0:T(8,128)} %index_ref.11) | copy-start | bytes 49156
  1.0 1.0 copy-start
  2.1 0.7 copy-start.3
  3.8 23.1 %collective-permute-start = (bf16[256,128]{1,0:T(8,128)(2,1)S(1)}, bf16[256,128]{1,0:T(8,128)(2,1)S(1)}, u32[]{:S(2)}, u32[]{:S(2)}) collective-permute-start(bf16[256,128]{1,0:T(8,128)(2,1)S(1)} %get-tuple-element.27.rows_ref), channel_id=1, source_target_pairs={{8,0},{16,8},{24,16},{32,24},{40,32},{48,40},{56,48},{64,56},{72,6... | collective-permute-start | bytes 196616 | tf_op jit(solution)/shard_map/ppermute | solution.py:298
  16.6 18.9 %collective-permute-start.1 = (f32[256,384]{1,0:T(8,128)S(1)}, f32[256,384]{1,0:T(8,128)S(1)}, u32[]{:S(2)}, u32[]{:S(2)}) collective-permute-start(f32[256,384]{1,0:T(8,128)S(1)} %get-tuple-element.28), channel_id=1, source_target_pairs={{0,8},{8,16},{16,24},{24,32},{32,40},{40,48},{48,56},{56,64},{64,7... | collective-permute-start | bytes 1179656 | tf_op jit(solution)/shard_map/ppermute | solution.py:298
  26.9 8.6 %copy-start.4 = (s32[256]{0:T(256)S(1)}, s32[256]{0:T(256)}, u32[]{:S(2)}) copy-start(s32[256]{0:T(256)} %param.9) | copy-start | bytes 3076
  26.9 8.6 %copy-start.1 = (bf16[2048,128]{1,0:T(8,128)(2,1)S(1)}, bf16[2048,128]{1,0:T(8,128)(2,1)}, u32[]{:S(2)}) copy-start(bf16[2048,128]{1,0:T(8,128)(2,1)} %previous_ref.1) | copy-start | bytes 1572868
  26.9 11.5 %copy-start.5 = (bf16[8,512,512]{2,1,0:T(8,128)(2,1)S(1)}, bf16[8,512,512]{2,1,0:T(8,128)(2,1)}, u32[]{:S(2)}) copy-start(bf16[8,512,512]{2,1,0:T(8,128)(2,1)} %cells_ref.3) | copy-start | bytes 12582916
  37.2 18.9 %collective-permute-start.2 = (bf16[256,128]{1,0:T(8,128)(2,1)S(1)}, bf16[256,128]{1,0:T(8,128)(2,1)S(1)}, u32[]{:S(2)}, u32[]{:S(2)}) collective-permute-start(bf16[256,128]{1,0:T(8,128)(2,1)S(1)} %get-tuple-element.31.rows_ref), channel_id=1, source_target_pairs={{8,0},{16,8},{24,16},{32,24},{40,32},{48,40},{56,48},{64,56},{72,6... | collective-permute-start | bytes 196616 | tf_op jit(solution)/shard_map/ppermute | solution.py:298
  47.4 17.3 %collective-permute-start.3 = (f32[256,128]{1,0:T(8,128)S(1)}, f32[256,128]{1,0:T(8,128)S(1)}, u32[]{:S(2)}, u32[]{:S(2)}) collective-permute-start(f32[256,128]{1,0:T(8,128)S(1)} %get-tuple-element.32), channel_id=1, source_target_pairs={{0,8},{8,16},{16,24},{24,32},{32,40},{40,48},{48,56},{56,64},{64,7... | collective-permute-start | bytes 393224 | tf_op jit(solution)/shard_map/ppermute | solution.py:298
  66.5 19.8 %collective-permute-start.4 = (bf16[256,128]{1,0:T(8,128)(2,1)S(1)}, bf16[256,128]{1,0:T(8,128)(2,1)S(1)}, u32[]{:S(2)}, u32[]{:S(2)}) collective-permute-start(bf16[256,128]{1,0:T(8,128)(2,1)S(1)} %get-tuple-element.36.rows_ref), channel_id=1, source_target_pairs={{8,0},{16,8},{24,16},{32,24},{40,32},{48,40},{56,48},{64,56},{72,6... | collective-permute-start | bytes 196616 | tf_op jit(solution)/shard_map/ppermute | solution.py:298
  76.8 18.0 %collective-permute-start.5 = (f32[256,128]{1,0:T(8,128)S(1)}, f32[256,128]{1,0:T(8,128)S(1)}, u32[]{:S(2)}, u32[]{:S(2)}) collective-permute-start(f32[256,128]{1,0:T(8,128)S(1)} %get-tuple-element.37), channel_id=1, source_target_pairs={{0,8},{8,16},{16,24},{24,32},{32,40},{40,48},{48,56},{56,64},{64,7... | collective-permute-start | bytes 393224 | tf_op jit(solution)/shard_map/ppermute | solution.py:298
  96.3 20.7 %all-to-all-start = ((bf16[4,512,128]{2,1,0:T(8,128)(2,1)}), bf16[4,512,128]{2,1,0:T(8,128)(2,1)S(1)}, u32[]{:S(2)}, u32[]{:S(2)}) async-start(bf16[4,512,128]{2,1,0:T(8,128)(2,1)} %bitcast.2), calls=%async_computation | async-start | bytes 1048576 | tf_op jit(solution)/shard_map/all_to_all | solution.py:302

commit v4 on v3

--- a/solution.py
+++ b/solution.py
@@ -80,25 +80,39 @@
     return one_hot(links == lax.broadcasted_iota(jnp.int32, (face, nodes), 0) + own)
 
 
-def take_entries(index_ref, scaled_ref, held):
+def take_entries(index_ref, column_ref, scaled_ref, held, narrow):
     cells, nodes = index_ref.shape
+    extent, width = scaled_ref.shape
+    copied = cells - column_ref.shape[0] // nodes
+    narrow[...] = scaled_ref[...].astype(BF16)
+    steps = 4
+    some = nodes // steps
+    rest = column_ref.shape[0] // steps
 
     def take(i, carry):
-        for cell in range(cells):
-            rows = [scaled_ref[pl.ds(index_ref[cell, i * 8 + u], 1), :] for u in range(8)]
-            held[pl.ds(pl.multiple_of(cell * nodes + i * 8, 8), 8), :] = jnp.concatenate(rows, 0)
+        first = pl.multiple_of(i * rest, rest)
+        named = column_ref[pl.ds(first, rest), :]
+        lane = lax.broadcasted_iota(jnp.int32, (rest, 128), 1)
+        hits = jnp.concatenate([one_hot(named == lane + t) for t in range(0, extent, 128)], 1)
+        product = dot(hits, narrow[...])
+        for k in range(some // 8):
+            for cell in range(copied):
+                at = i * some + k * 8
+                rows = [scaled_ref[pl.ds(index_ref[cell, at + u], 1), :] for u in range(8)]
+                held[pl.ds(pl.multiple_of(cell * nodes + at, 8), 8), :] = jnp.concatenate(rows, 0)
+        held[pl.ds(copied * nodes + first, rest), :] = product
         return carry
 
-    lax.fori_loop(0, nodes // 8, take, 0)
+    lax.fori_loop(0, steps, take, 0)
 
 
 def opening_body(
-    own, face, index_ref, links_ref, scaled_ref, matrices_ref, products_ref, spread_ref, sent_ref,
-    held, cells_ref, sem,
+    own, face, index_ref, links_ref, column_ref, scaled_ref, matrices_ref, products_ref,
+    spread_ref, block_ref, sent_ref, held, narrow, cells_ref, sem,
 ):
     copy = pltpu.make_async_copy(matrices_ref, cells_ref, sem)
     copy.start()
-    take_entries(index_ref, scaled_ref, held)
+    take_entries(index_ref, column_ref, scaled_ref, held, narrow)
     copy.wait()
     cells, nodes = index_ref.shape
     width = scaled_ref.shape[1]
@@ -116,12 +130,15 @@
         product = dot(cells_ref[cell], held[part, :].astype(BF16))
         products_ref[part, :] = product
         total = total + dot(hits, halves(product))
-    sent_ref[:, :width] = total[:, :width] + total[:, width:]
-    sent_ref[:, width:] = block[:, :face] + block[:, face:]
-
-
-def local_body(own, face, index_ref, links_ref, scaled_ref, cells_ref, products_ref, sent_ref, held):
-    take_entries(index_ref, scaled_ref, held)
+    sent_ref[...] = total[:, :width] + total[:, width:]
+    block_ref[...] = halves(block[:, :face] + block[:, face:])
+
+
+def local_body(
+    own, face, index_ref, links_ref, column_ref, scaled_ref, cells_ref, products_ref, sent_ref,
+    held, narrow,
+):
+    take_entries(index_ref, column_ref, scaled_ref, held, narrow)
     cells, nodes = index_ref.shape
     width = scaled_ref.shape[1]
     total = jnp.zeros((face, 2 * width), F32)
@@ -133,35 +150,61 @@
     sent_ref[...] = total[:, :width] + total[:, width:]
 
 
-def assemble_body(index_ref, products_ref, spread_ref, rows_ref, summed_ref, whole, *totals):
+def returned_body(sent_ref, block_ref, rows_ref, total_ref):
+    rows = rows_ref[...]
+    total_ref[...] = sent_ref[...] + dot(block_ref[...], jnp.concatenate([rows, rows], 0))
+
+
+def assemble_body(
+    index_ref, links_ref, products_ref, spread_ref, rows_ref, summed_ref, whole, split, *totals
+):
     cells, nodes = index_ref.shape
-    own = summed_ref.shape[0]
+    own, width = summed_ref.shape
+    added = len(totals)
     rows = rows_ref[...]
     twice = jnp.concatenate([rows, rows], 0)
     for cell in range(cells):
         part = slice(cell * nodes, (cell + 1) * nodes)
-        whole[part, :] = products_ref[part, :] + dot(spread_ref[part, :], twice)
+        product = products_ref[part, :] + dot(spread_ref[part, :], twice)
+        if cell < added:
+            whole[part, :] = product
+        else:
+            split[(cell - added) * nodes : (cell - added + 1) * nodes, :] = halves(product)
     for total in totals:
         total[...] = jnp.zeros_like(total)
+    steps = 4
+    some = nodes // steps
+    tall = own // steps
 
     def add(i, carry):
-        for u in range(4):
-            j = i * 4 + u
-            at = [pl.ds(index_ref[cell, j], 1) for cell in range(cells)]
+        first = pl.multiple_of(i * tall, tall)
+        row = lax.broadcasted_iota(jnp.int32, (tall, 128), 0) + first
+        hits = jnp.concatenate(
+            [
+                one_hot(links_ref[:1, t : t + 128] == row)
+                for t in range(added * nodes, cells * nodes, 128)
+            ],
+            1,
+        )
+        both = dot(hits, split[...])
+        for u in range(some):
+            j = i * some + u
+            at = [pl.ds(index_ref[cell, j], 1) for cell in range(added)]
             sums = [
                 totals[cell][at[cell], :] + whole[pl.ds(cell * nodes + j, 1), :]
-                for cell in range(cells)
+                for cell in range(added)
             ]
-            for cell in range(cells):
+            for cell in range(added):
                 totals[cell][at[cell], :] = sums[cell]
+        summed_ref[pl.ds(first, tall), :] = both[:, :width] + both[:, width:]
         return carry
 
-    lax.fori_loop(0, nodes // 4, add, 0)
+    lax.fori_loop(0, steps, add, 0)
 
     def collect(i, carry):
         part = pl.ds(pl.multiple_of(i * 64, 64), 64)
-        summed = totals[0][part, :]
-        for total in totals[1:]:
+        summed = summed_ref[part, :]
+        for total in totals:
             summed = summed + total[part, :]
         summed_ref[part, :] = summed
         return carry
@@ -169,33 +212,30 @@
     lax.fori_loop(0, own // 64, collect, 0)
 
 
-def applied(faces_ref, summed_ref, arrived_ref, block_ref, rows_ref, mass_ref):
+def applied(faces_ref, summed_ref, arrived_ref, mass_ref):
     own, width = summed_ref.shape
-    face = rows_ref.shape[0]
-    rows = rows_ref[...]
-    block = block_ref[:, width:]
-    contribution = arrived_ref[:, :width] + dot(halves(block), jnp.concatenate([rows, rows], 0))
+    face = arrived_ref.shape[0]
     hits = one_hot(lax.broadcasted_iota(jnp.int32, (own, face), 0) == faces_ref[:1, :])
-    added = dot(hits, halves(contribution))
+    added = dot(hits, halves(arrived_ref[...]))
     return mass_ref[...] * (summed_ref[...] + (added[:, :width] + added[:, width:]))
 
 
 def first_body(
-    face_ref, faces_ref, summed_ref, arrived_ref, block_ref, rows_ref, mass_ref, wave_ref,
+    face_ref, faces_ref, summed_ref, arrived_ref, mass_ref, wave_ref,
     current_ref, scaled_ref, sent_ref, picked,
 ):
     own, width = summed_ref.shape
-    image = applied(faces_ref, summed_ref, arrived_ref, block_ref, rows_ref, mass_ref)
+    image = applied(faces_ref, summed_ref, arrived_ref, mass_ref)
     current_ref[...] = (image - CENTER * wave_ref[...].astype(F32)) / HALF
     scale_rows(own, width, current_ref[...], mass_ref, face_ref, scaled_ref, sent_ref, picked)
 
 
 def next_body(
-    face_ref, faces_ref, summed_ref, arrived_ref, block_ref, rows_ref, mass_ref, previous_ref,
+    face_ref, faces_ref, summed_ref, arrived_ref, mass_ref, previous_ref,
     current_ref, following_ref, scaled_ref, sent_ref, picked,
 ):
     own, width = summed_ref.shape
-    image = applied(faces_ref, summed_ref, arrived_ref, block_ref, rows_ref, mass_ref)
+    image = applied(faces_ref, summed_ref, arrived_ref, mass_ref)
     following_ref[...] = 2.0 * (image - CENTER * current_ref[...]) / HALF - previous_ref[
         ...
     ].astype(F32)
@@ -203,10 +243,10 @@
 
 
 def last_body(
-    faces_ref, summed_ref, arrived_ref, block_ref, rows_ref, mass_ref, previous_ref, current_ref,
+    faces_ref, summed_ref, arrived_ref, mass_ref, previous_ref, current_ref,
     filtered_ref, rounded_ref,
 ):
-    image = applied(faces_ref, summed_ref, arrived_ref, block_ref, rows_ref, mass_ref)
+    image = applied(faces_ref, summed_ref, arrived_ref, mass_ref)
     filtered = 2.0 * (image - CENTER * current_ref[...]) / HALF - previous_ref[...].astype(F32)
     filtered_ref[...] = filtered
     rounded_ref[...] = filtered.astype(BF16)
@@ -325,6 +365,10 @@
 
     mass = jnp.broadcast_to(mass_scale[:, None], (own, width))
     links = jnp.broadcast_to(connectivity.reshape(1, entries), (8, entries))
+    copied = cells // 2
+    column = jnp.broadcast_to(
+        connectivity[copied:].reshape(-1, 1), ((cells - copied) * cell_nodes, 128)
+    )
     faces = jnp.broadcast_to(face_index.reshape(1, face), (8, face))
     face_list = face_index.reshape(1, face)
 
@@ -336,28 +380,32 @@
         start_body, "scaled_start", [IN_SMEM] + [IN_VMEM] * 2, [scaled_shape, rows_shape], [picked],
         10**6, 3 * 2**20,
     )
+    gathering = [pltpu.VMEM((entries, width), F32), pltpu.VMEM((extent, width), BF16)]
     opening = call(
         functools.partial(opening_body, own, face), "opening_products",
-        [IN_SMEM] + [IN_VMEM] * 2 + [IN_ANY],
+        [IN_SMEM] + [IN_VMEM] * 3 + [IN_ANY],
         [
             shape((entries, width), F32), shape((entries, 2 * face), BF16),
-            shape((face, width + face), F32),
+            shape((face, 2 * face), BF16), shape((face, width), F32),
         ],
+        gathering + [pltpu.VMEM(cell_matrices.shape, BF16), pltpu.SemaphoreType.DMA],
+        8 * 10**9, 16 * 2**20, 45,
+    )
+    local = call(
+        functools.partial(local_body, own, face), "local_products", [IN_SMEM] + [IN_VMEM] * 4,
+        [shape((entries, width), F32), shape((face, width), F32)], gathering,
+        5 * 10**9, 16 * 2**20,
+    )
+    returned = call(
+        returned_body, "returned", [IN_VMEM] * 3, shape((face, width), F32), [], 10**8, 2**20,
+    )
+    assemble = call(
+        assemble_body, "assembled", [IN_SMEM] + [IN_VMEM] * 4, wide,
         [
-            pltpu.VMEM((entries, width), F32),
-            pltpu.VMEM(cell_matrices.shape, BF16),
-            pltpu.SemaphoreType.DMA,
-        ],
-        8 * 10**9, 16 * 2**20, 46,
-    )
-    local = call(
-        functools.partial(local_body, own, face), "local_products", [IN_SMEM] + [IN_VMEM] * 3,
-        [shape((entries, width), F32), shape((face, width), F32)],
-        [pltpu.VMEM((entries, width), F32)], 5 * 10**9, 16 * 2**20,
-    )
-    assemble = call(
-        assemble_body, "assembled", [IN_SMEM] + [IN_VMEM] * 3, wide,
-        [pltpu.VMEM((entries, width), F32)] + [pltpu.VMEM((extent, width), F32)] * cells,
+            pltpu.VMEM((copied * cell_nodes, width), F32),
+            pltpu.VMEM((entries - copied * cell_nodes, 2 * width), BF16),
+        ]
+        + [pltpu.VMEM((extent, width), F32)] * copied,
         5 * 10**9, 16 * 2**20,
     )
 
@@ -366,27 +414,28 @@
     for sweep in range(DEGREE):
         received = passed_along(rows, -1)
         if sweep == 0:
-            products, spread, sent = opening(connectivity, links, scaled, cell_matrices)
-            arrived = block = passed_along(sent, 1)
+            products, spread, block, sent = opening(
+                connectivity, links, column, scaled, cell_matrices
+            )
         else:
-            products, sent = local(connectivity, links, scaled, cell_matrices)
-            arrived = passed_along(sent, 1)
-        summed = assemble(connectivity, products, spread, received)
-        parts = (summed, arrived, block, rows, mass)
+            products, sent = local(connectivity, links, column, scaled, cell_matrices)
+        arrived = passed_along(returned(sent, block, received), 1)
+        summed = assemble(connectivity, links, products, spread, received)
+        parts = (summed, arrived, mass)
         if sweep == DEGREE - 1:
             filtered, rounded = call(
-                last_body, "filtered", [IN_VMEM] * 8, [wide, shape((own, width), BF16)], [],
+                last_body, "filtered", [IN_VMEM] * 6, [wide, shape((own, width), BF16)], [],
                 10**9, 6 * 2**20,
             )(faces, *parts, previous, current)
         elif sweep == 0:
             following, scaled, rows = call(
-                first_body, "first_step", [IN_SMEM] + [IN_VMEM] * 7,
+                first_body, "first_step", [IN_SMEM] + [IN_VMEM] * 5,
                 [wide, scaled_shape, rows_shape], [picked], 10**9, 6 * 2**20,
             )(face_list, faces, *parts, current)
             previous, current = current, following
         else:
             following, scaled, rows = call(
-                next_body, "next_step", [IN_SMEM] + [IN_VMEM] * 8,
+                next_body, "next_step", [IN_SMEM] + [IN_VMEM] * 6,
                 [wide, scaled_shape, rows_shape], [picked], 10**9, 6 * 2**20,
             )(face_list, faces, *parts, previous, current)
             previous, current = current, following

time: 214 us -> 191 us (0.89)
  Pallas kernels: 67.9 us -> 51.7 us
  starting transfers between devices: 42.5 us -> 32.9 us
  waiting for transfers between devices: 10.9 us -> 15.2 us
    pallas_call x9 -> x12, Pallas kernels: 59.6 us -> 43.5 us  [the longest x3 17 us: on_device(): summed = assemble(connectivity, links, products, spread, received)]
    all_to_all x1, starting transfers between devices: 9.87 us -> 3.62 us  [exchanged(): return lax.all_to_all(pieces, axes, split_axis=0, concat_axis=0, tiled=True)]
    ppermute x6, waiting for transfers between devices: 0.02 us -> 4.29 us  [passed_along(): lax.ppermute(value, DOM, [(source, source + steps) for source in range(in...]
    ppermute x6, starting transfers between devices: 32.6 us -> 29.2 us  [passed_along(): lax.ppermute(value, DOM, [(source, source + steps) for source in range(in...]
  transfers between devices with their start and end apart: 7 -> 7, of which waited for: 1 -> 4; matrix products, arithmetic and copies ran while one was open for 0% -> 0% of each run, Pallas kernels for 26% -> 20%
where the time goes in v4:
time: 191 us
  blocking collectives  87.1 us (46%)
  Pallas kernels  51.7 us (27%)
  starting transfers between devices  32.9 us (17%)
  waiting for transfers between devices  15.2 us (8%)
  local copies, waits for them, and re-layouts  3.45 us (2%)
    all_to_all x6, blocking collectives, exchanged(): return lax.all_to_all(pieces, axes, split_axis=0, concat_axis=0, tiled=True)  87.1 us
    ppermute x6, starting transfers between devices, passed_along(): lax.ppermute(value, DOM, [(source, source + steps) for source in range(in...  29.2 us
    pallas_call x3, Pallas kernels, on_device(): summed = assemble(connectivity, links, products, spread, received)  17 us
    pallas_call x2, Pallas kernels, on_device(): products, sent = local(connectivity, links, column, scaled, cell_matrices)  12.6 us
    all_to_all x1, waiting for transfers between devices, exchanged(): return lax.all_to_all(pieces, axes, split_axis=0, concat_axis=0, tiled=True)  10.9 us
    pallas_call x1, Pallas kernels, on_device(): opening(connectivity, links, column, scaled, cell_matrices)  8.91 us
    pallas_call x1, Pallas kernels, on_device(): call(functools.partial(correct_body, own * domains), 'correction', [IN_SM...  5.36 us
    ppermute x6, waiting for transfers between devices, passed_along(): lax.ppermute(value, DOM, [(source, source + steps) for source in range(in...  4.29 us
  transfers between devices with their start and end apart: 7, of which 4 were waited for; matrix products, arithmetic and copies ran while one was open for 0% of the time, Pallas kernels for 20%

profile of v4, /device:TPU:1, one launch (start us, length us, event | category | flops | bytes accessed | tf_op | source)
XLA Modules:
  0.0 190.8 jit_solution(7914395505635049468)
XLA Ops:
  0.0 1.0 broadcast_in_dim.42.mass_ref
  1.0 0.0 copy-start
  1.1 1.0 copy-done
  2.1 0.7 copy-done.3
  2.8 1.1 scaled_start.1
  3.8 1.3 collective-permute-start
  5.2 0.3 broadcast_in_dim.41.column_ref
  5.5 8.9 %opening_products.1 = (f32[4096,128]{1,0:T(8,128)S(1)}, bf16[4096,512]{1,0:T(8,128)(2,1)S(1)}, bf16[256,512]{1,0:T(8,128)(2,1)S(1)}, f32[256,128]{1,0:T(8,128)S(1)}) custom-call(s32[8,512]{1,0:T(8,128)S(1)} %copy-done.2, s32[8,4096]{1,0:T(8,128)S(1)} %broadcast_in_dim.39.links_ref, s32[2048,128]{1,0:T(8,128)S(1)} %broadcast_in_dim.41.column_ref, ...), custom_call_target="tpu_custom_call" | custom-call | flops 8000000000 | bytes 16777216 | tf_op jit(solution)/shard_map/opening_products/pallas_call | solution.py:417
  14.4 0.8 collective-permute-done.rows_ref
  15.2 0.2 returned.3
  15.4 9.5 %collective-permute-start.1 = (f32[256,128]{1,0:T(8,128)S(1)}, f32[256,128]{1,0:T(8,128)S(1)}, u32[]{:S(2)}, u32[]{:S(2)}) collective-permute-start(f32[256,128]{1,0:T(8,128)S(1)} %returned.3), channel_id=1, source_target_pairs={{0,8},{8,16},{16,24},{24,32},{32,40},{40,48},{48,56},{56,64},{64,7... | collective-permute-start | bytes 393224 | tf_op jit(solution)/shard_map/ppermute | solution.py:338
  25.0 0.0 copy-start.4
  25.0 0.0 copy-start.1
  25.0 0.0 copy-start.5
  25.0 5.7 %assembled.3.summed_ref = f32[2048,128]{1,0:T(8,128)S(1)} custom-call(s32[8,512]{1,0:T(8,128)S(1)} %copy-done.2, s32[8,4096]{1,0:T(8,128)S(1)} %broadcast_in_dim.39.links_ref, f32[4096,128]{1,0:T(8,128)S(1)} %get-tuple-element.26.products_ref, bf16[4096,512]{1,0:T(8,128)(2,1)S(1)} %get-tuple-element.27.spread_ref, ...), custom_call_target="tpu_custom_call" | custom-call | flops 5000000000 | bytes 16777216 | tf_op jit(solution)/shard_map/assembled/pallas_call | solution.py:423
  30.7 0.0 collective-permute-done.1.arrived_ref
  30.7 1.5 first_step.1
  32.2 1.3 collective-permute-start.2
  33.5 6.3 %local_products.2 = (f32[4096,128]{1,0:T(8,128)S(1)}, f32[256,128]{1,0:T(8,128)S(1)}) custom-call(s32[8,512]{1,0:T(8,128)S(1)} %copy-done.2, s32[8,4096]{1,0:T(8,128)S(1)} %broadcast_in_dim.39.links_ref, s32[2048,128]{1,0:T(8,128)S(1)} %broadcast_in_dim.41.column_ref, f32[2304,128]{1,0:T(8,128)S(1)} %get-tuple-element.31.scaled_ref, ...), custom_call_target="tpu_custom_call" | custom-call | flops 5000000000 | bytes 16777216 | tf_op jit(solution)/shard_map/local_products/pallas_call | solution.py:421
  39.8 2.2 %collective-permute-done.2.rows_ref = bf16[256,128]{1,0:T(8,128)(2,1)S(1)} collective-permute-done((bf16[256,128]{1,0:T(8,128)(2,1)S(1)}, bf16[256,128]{1,0:T(8,128)(2,1)S(1)}, u32[]{:S(2)}, u32[]{:S(2)}) %collective-permute-start.2) | collective-permute-done | bytes 65568 | tf_op jit(solution)/shard_map/ppermute | solution.py:338
  42.0 0.2 returned.4
  42.2 8.3 %collective-permute-start.3 = (f32[256,128]{1,0:T(8,128)S(1)}, f32[256,128]{1,0:T(8,128)S(1)}, u32[]{:S(2)}, u32[]{:S(2)}) collective-permute-start(f32[256,128]{1,0:T(8,128)S(1)} %returned.4), channel_id=1, source_target_pairs={{0,8},{8,16},{16,24},{24,32},{32,40},{40,48},{48,56},{56,64},{64,7... | collective-permute-start | bytes 393224 | tf_op jit(solution)/shard_map/ppermute | solution.py:338
  50.6 5.7 %assembled.4.summed_ref = f32[2048,128]{1,0:T(8,128)S(1)} custom-call(s32[8,512]{1,0:T(8,128)S(1)} %copy-done.2, s32[8,4096]{1,0:T(8,128)S(1)} %broadcast_in_dim.39.links_ref, f32[4096,128]{1,0:T(8,128)S(1)} %get-tuple-element.32.products_ref, bf16[4096,512]{1,0:T(8,128)(2,1)S(1)} %get-tuple-element.27.spread_ref, ...), custom_call_target="tpu_custom_call" | custom-call | flops 5000000000 | bytes 16777216 | tf_op jit(solution)/shard_map/assembled/pallas_call | solution.py:423
  56.2 0.0 collective-permute-done.3.arrived_ref
  56.2 1.6 next_step.1
  57.8 1.3 collective-permute-start.4
  59.1 6.3 %local_products.3 = (f32[4096,128]{1,0:T(8,128)S(1)}, f32[256,128]{1,0:T(8,128)S(1)}) custom-call(s32[8,512]{1,0:T(8,128)S(1)} %copy-done.2, s32[8,4096]{1,0:T(8,128)S(1)} %broadcast_in_dim.39.links_ref, s32[2048,128]{1,0:T(8,128)S(1)} %broadcast_in_dim.41.column_ref, f32[2304,128]{1,0:T(8,128)S(1)} %get-tuple-element.36.scaled_ref, ...), custom_call_target="tpu_custom_call" | custom-call | flops 5000000000 | bytes 16777216 | tf_op jit(solution)/shard_map/local_products/pallas_call | solution.py:421
  65.4 1.3 collective-permute-done.4.rows_ref
  66.7 0.2 returned.5
  67.0 7.5 %collective-permute-start.5 = (f32[256,128]{1,0:T(8,128)S(1)}, f32[256,128]{1,0:T(8,128)S(1)}, u32[]{:S(2)}, u32[]{:S(2)}) collective-permute-start(f32[256,128]{1,0:T(8,128)S(1)} %returned.5), channel_id=1, source_target_pairs={{0,8},{8,16},{16,24},{24,32},{32,40},{40,48},{48,56},{56,64},{64,7... | collective-permute-start | bytes 393224 | tf_op jit(solution)/shard_map/ppermute | solution.py:338
  74.5 5.7 %assembled.5.summed_ref = f32[2048,128]{1,0:T(8,128)S(1)} custom-call(s32[8,512]{1,0:T(8,128)S(1)} %copy-done.2, s32[8,4096]{1,0:T(8,128)S(1)} %broadcast_in_dim.39.links_ref, f32[4096,128]{1,0:T(8,128)S(1)} %get-tuple-element.37.products_ref, bf16[4096,512]{1,0:T(8,128)(2,1)S(1)} %get-tuple-element.27.spread_ref, ...), custom_call_target="tpu_custom_call" | custom-call | flops 5000000000 | bytes 16777216 | tf_op jit(solution)/shard_map/assembled/pallas_call | solution.py:423
  80.1 0.0 collective-permute-done.5.arrived_ref
  80.2 1.3 filtered.1
  81.5 3.6 %all-to-all-start = ((bf16[4,512,128]{2,1,0:T(8,128)(2,1)}), bf16[4,512,128]{2,1,0:T(8,128)(2,1)S(1)}, u32[]{:S(2)}, u32[]{:S(2)}) async-start(bf16[4,512,128]{2,1,0:T(8,128)(2,1)} %bitcast.2), calls=%async_computation | async-start | bytes 1048576 | tf_op jit(solution)/shard_map/all_to_all | solution.py:342
  85.1 10.9 %all-to-all-done = bf16[4,512,128]{2,1,0:T(8,128)(2,1)S(1)} async-done(((bf16[4,512,128]{2,1,0:T(8,128)(2,1)}), bf16[4,512,128]{2,1,0:T(8,128)(2,1)S(1)}, u32[]{:S(2)}, u32[]{:S(2)}) %all-to-all-start) | async-done | bytes 524320 | tf_op jit(solution)/shard_map/all_to_all | solution.py:342
  96.0 0.1 broadcast_in_dim.43
  96.1 8.8 %all_to_all.35.rows_ref = bf16[2,4,512,128]{3,2,1,0:T(8,128)(2,1)S(1)} all-to-all(bf16[2,4,512,128]{3,2,1,0:T(8,128)(2,1)S(1)} %broadcast_in_dim.43), channel_id=1, replica_groups=mesh['dom_0'=4,'dom_1'=4,'dom_2'=2,'band_0'=4,'band_1'=2] {'band_1'}, dimensions={0} | all-to-all | bytes 2097152 | tf_op jit(solution)/shard_map/all_to_all | solution.py:342
  104.9 0.7 gram.1
  105.6 26.1 %all_to_all.36 = bf16[16,144,128]{2,1,0:T(8,128)(2,1)S(1)} all-to-all(bf16[16,144,128]{2,1,0:T(8,128)(2,1)S(1)} %bitcast.14), channel_id=1, replica_groups=mesh['dom_0'=4,'dom_1'=4,'dom_2'=2,'band_0'=4,'band_1'=2] {'dom_0','dom_1'}, dimensions={0} | all-to-all | bytes 1179648 | tf_op jit(solution)/shard_map/all_to_all | solution.py:342
  131.7 0.1 reduce_sum.24
  131.9 13.0 %all_to_all.37 = bf16[8,144,128]{2,1,0:T(8,128)(2,1)S(1)} all-to-all(bf16[8,144,128]{2,1,0:T(8,128)(2,1)S(1)} %broadcast_in_dim.44), channel_id=1, replica_groups=mesh['dom_0'=4,'dom_1'=4,'dom_2'=2,'band_0'=4,'band_1'=2] {'dom_2','band..., dimensions={0} | all-to-all | bytes 589824 | tf_op jit(solution)/shard_map/all_to_all | solution.py:342
  144.9 0.1 broadcast_in_dim.45
  145.0 13.4 %all_to_all.38 = bf16[16,144,128]{2,1,0:T(8,128)(2,1)S(1)} all-to-all(bf16[16,144,128]{2,1,0:T(8,128)(2,1)S(1)} %broadcast_in_dim.45), channel_id=1, replica_groups=mesh['dom_0'=4,'dom_1'=4,'dom_2'=2,'band_0'=4,'band_1'=2] {'dom_0','dom_1'}, dimensions={0} | all-to-all | bytes 1179648 | tf_op jit(solution)/shard_map/all_to_all | solution.py:342
  158.4 0.1 broadcast_in_dim.46
  158.5 9.1 %all_to_all.39 = bf16[2,2304,128]{2,1,0:T(8,128)(2,1)S(1)} all-to-all(bf16[2,2304,128]{2,1,0:T(8,128)(2,1)S(1)} %broadcast_in_dim.46), channel_id=1, replica_groups=mesh['dom_0'=4,'dom_1'=4,'dom_2'=2,'band_0'=4,'band_1'=2] {'band_1'}, dimensions={0} | all-to-all | bytes 2359296 | tf_op jit(solution)/shard_map/all_to_all | solution.py:342
  167.6 5.4 %correction.1 = (bf16[4,512,128]{2,1,0:T(8,128)(2,1)S(1)}, f32[8,128]{1,0:T(8,128)S(1)}) custom-call(s32[1]{0:T(128)} %bitcast.1.core_ref, bf16[36,128,128]{2,1,0:T(8,128)(2,1)S(1)} %bitcast.13, bf16[2,4,512,128]{3,2,1,0:T(8,128)(2,1)S(1)} %all_to_all.35.rows_ref), custom_call_target="tpu_custom_call" | custom-call | flops 4000000000 | bytes 8388608 | tf_op jit(solution)/shard_map/correction/pallas_call | solution.py:460
  172.9 16.7 %all_to_all.40 = bf16[4,512,128]{2,1,0:T(8,128)(2,1)S(1)} all-to-all(bf16[4,512,128]{2,1,0:T(8,128)(2,1)S(1)} %get-tuple-element.43), channel_id=1, replica_groups=mesh['dom_0'=4,'dom_1'=4,'dom_2'=2,'band_0'=4,'band_1'=2] {'band_0'}, dimensions={0} | all-to-all | bytes 1048576 | tf_op jit(solution)/shard_map/all_to_all | solution.py:342
  189.7 1.1 rotated.1
  (13 shorter events, 0.1 us)
Async XLA Ops:
  0.0 5.1 %copy-start.2 = (s32[8,512]{1,0:T(8,128)S(1)}, s32[8,512]{1,0:T(8,128)}, u32[]{:S(2)}) copy-start(s32[8,512]{1,0:T(8,128)} %index_ref.11) | copy-start | bytes 49156
  1.0 1.0 copy-start
  2.1 0.7 copy-start.3
  3.8 11.4 %collective-permute-start = (bf16[256,128]{1,0:T(8,128)(2,1)S(1)}, bf16[256,128]{1,0:T(8,128)(2,1)S(1)}, u32[]{:S(2)}, u32[]{:S(2)}) collective-permute-start(bf16[256,128]{1,0:T(8,128)(2,1)S(1)} %get-tuple-element.28), channel_id=1, source_target_pairs={{8,0},{16,8},{24,16},{32,24},{40,32},{48,40},{56,48},{64,56},{72,6... | collective-permute-start | bytes 196616 | tf_op jit(solution)/shard_map/ppermute | solution.py:338
  15.4 15.2 %collective-permute-start.1 = (f32[256,128]{1,0:T(8,128)S(1)}, f32[256,128]{1,0:T(8,128)S(1)}, u32[]{:S(2)}, u32[]{:S(2)}) collective-permute-start(f32[256,128]{1,0:T(8,128)S(1)} %returned.3), channel_id=1, source_target_pairs={{0,8},{8,16},{16,24},{24,32},{32,40},{40,48},{48,56},{56,64},{64,7... | collective-permute-start | bytes 393224 | tf_op jit(solution)/shard_map/ppermute | solution.py:338
  25.0 5.7 %copy-start.4 = (s32[256]{0:T(256)S(1)}, s32[256]{0:T(256)}, u32[]{:S(2)}) copy-start(s32[256]{0:T(256)} %param.9) | copy-start | bytes 3076
  25.0 5.7 %copy-start.1 = (bf16[2048,128]{1,0:T(8,128)(2,1)S(1)}, bf16[2048,128]{1,0:T(8,128)(2,1)}, u32[]{:S(2)}) copy-start(bf16[2048,128]{1,0:T(8,128)(2,1)} %previous_ref.1) | copy-start | bytes 1572868
  25.0 8.5 %copy-start.5 = (bf16[8,512,512]{2,1,0:T(8,128)(2,1)S(1)}, bf16[8,512,512]{2,1,0:T(8,128)(2,1)}, u32[]{:S(2)}) copy-start(bf16[8,512,512]{2,1,0:T(8,128)(2,1)} %cells_ref.3) | copy-start | bytes 12582916
  32.2 9.8 %collective-permute-start.2 = (bf16[256,128]{1,0:T(8,128)(2,1)S(1)}, bf16[256,128]{1,0:T(8,128)(2,1)S(1)}, u32[]{:S(2)}, u32[]{:S(2)}) collective-permute-start(bf16[256,128]{1,0:T(8,128)(2,1)S(1)} %get-tuple-element.33), channel_id=1, source_target_pairs={{8,0},{16,8},{24,16},{32,24},{40,32},{48,40},{56,48},{64,56},{72,6... | collective-permute-start | bytes 196616 | tf_op jit(solution)/shard_map/ppermute | solution.py:338
  42.2 14.0 %collective-permute-start.3 = (f32[256,128]{1,0:T(8,128)S(1)}, f32[256,128]{1,0:T(8,128)S(1)}, u32[]{:S(2)}, u32[]{:S(2)}) collective-permute-start(f32[256,128]{1,0:T(8,128)S(1)} %returned.4), channel_id=1, source_target_pairs={{0,8},{8,16},{16,24},{24,32},{32,40},{40,48},{48,56},{56,64},{64,7... | collective-permute-start | bytes 393224 | tf_op jit(solution)/shard_map/ppermute | solution.py:338
  57.8 8.9 %collective-permute-start.4 = (bf16[256,128]{1,0:T(8,128)(2,1)S(1)}, bf16[256,128]{1,0:T(8,128)(2,1)S(1)}, u32[]{:S(2)}, u32[]{:S(2)}) collective-permute-start(bf16[256,128]{1,0:T(8,128)(2,1)S(1)} %get-tuple-element.38), channel_id=1, source_target_pairs={{8,0},{16,8},{24,16},{32,24},{40,32},{48,40},{56,48},{64,56},{72,6... | collective-permute-start | bytes 196616 | tf_op jit(solution)/shard_map/ppermute | solution.py:338
  67.0 13.2 %collective-permute-start.5 = (f32[256,128]{1,0:T(8,128)S(1)}, f32[256,128]{1,0:T(8,128)S(1)}, u32[]{:S(2)}, u32[]{:S(2)}) collective-permute-start(f32[256,128]{1,0:T(8,128)S(1)} %returned.5), channel_id=1, source_target_pairs={{0,8},{8,16},{16,24},{24,32},{32,40},{40,48},{48,56},{56,64},{64,7... | collective-permute-start | bytes 393224 | tf_op jit(solution)/shard_map/ppermute | solution.py:338
  81.5 14.5 %all-to-all-start = ((bf16[4,512,128]{2,1,0:T(8,128)(2,1)}), bf16[4,512,128]{2,1,0:T(8,128)(2,1)S(1)}, u32[]{:S(2)}, u32[]{:S(2)}) async-start(bf16[4,512,128]{2,1,0:T(8,128)(2,1)} %bitcast.2), calls=%async_computation | async-start | bytes 1048576 | tf_op jit(solution)/shard_map/all_to_all | solution.py:342

commit v5 on v4

--- a/solution.py
+++ b/solution.py
@@ -152,7 +152,8 @@
 
 def returned_body(sent_ref, block_ref, rows_ref, total_ref):
     rows = rows_ref[...]
-    total_ref[...] = sent_ref[...] + dot(block_ref[...], jnp.concatenate([rows, rows], 0))
+    total = sent_ref[...] + dot(block_ref[...], jnp.concatenate([rows, rows], 0))
+    total_ref[...] = total.astype(BF16)
 
 
 def assemble_body(
@@ -213,11 +214,9 @@
 
 
 def applied(faces_ref, summed_ref, arrived_ref, mass_ref):
-    own, width = summed_ref.shape
-    face = arrived_ref.shape[0]
+    own, face = summed_ref.shape[0], arrived_ref.shape[0]
     hits = one_hot(lax.broadcasted_iota(jnp.int32, (own, face), 0) == faces_ref[:1, :])
-    added = dot(hits, halves(arrived_ref[...]))
-    return mass_ref[...] * (summed_ref[...] + (added[:, :width] + added[:, width:]))
+    return mass_ref[...] * (summed_ref[...] + dot(hits, arrived_ref[...]))
 
 
 def first_body(
@@ -397,7 +396,7 @@
         5 * 10**9, 16 * 2**20,
     )
     returned = call(
-        returned_body, "returned", [IN_VMEM] * 3, shape((face, width), F32), [], 10**8, 2**20,
+        returned_body, "returned", [IN_VMEM] * 3, rows_shape, [], 10**8, 2**20,
     )
     assemble = call(
         assemble_body, "assembled", [IN_SMEM] + [IN_VMEM] * 4, wide,

time: 191 us -> 191 us (level)
  blocking collectives: 87.1 us -> 84.3 us
  waiting for transfers between devices: 15.2 us -> 17.5 us
    all_to_all x6, blocking collectives: 87.1 us -> 84.3 us  [exchanged(): return lax.all_to_all(pieces, axes, split_axis=0, concat_axis=0, tiled=True)]
    all_to_all x1, waiting for transfers between devices: 10.9 us -> 13.1 us  [exchanged(): return lax.all_to_all(pieces, axes, split_axis=0, concat_axis=0, tiled=True)]
where the time goes in v5:
time: 191 us
  blocking collectives  84.3 us (44%)
  Pallas kernels  51.5 us (27%)
  starting transfers between devices  33.4 us (17%)
  waiting for transfers between devices  17.5 us (9%)
  local copies, waits for them, and re-layouts  3.45 us (2%)
    all_to_all x6, blocking collectives, exchanged(): return lax.all_to_all(pieces, axes, split_axis=0, concat_axis=0, tiled=True)  84.3 us
    ppermute x6, starting transfers between devices, passed_along(): lax.ppermute(value, DOM, [(source, source + steps) for source in range(in...  29.9 us
    pallas_call x3, Pallas kernels, on_device(): summed = assemble(connectivity, links, products, spread, received)  17 us
    all_to_all x1, waiting for transfers between devices, exchanged(): return lax.all_to_all(pieces, axes, split_axis=0, concat_axis=0, tiled=True)  13.1 us
    pallas_call x2, Pallas kernels, on_device(): products, sent = local(connectivity, links, column, scaled, cell_matrices)  12.5 us
    pallas_call x1, Pallas kernels, on_device(): opening(connectivity, links, column, scaled, cell_matrices)  8.87 us
    pallas_call x1, Pallas kernels, on_device(): call(functools.partial(correct_body, own * domains), 'correction', [IN_SM...  5.36 us
    ppermute x6, waiting for transfers between devices, passed_along(): lax.ppermute(value, DOM, [(source, source + steps) for source in range(in...  4.4 us
  transfers between devices with their start and end apart: 7, of which 4 were waited for; matrix products, arithmetic and copies ran while one was open for 0% of the time, Pallas kernels for 20%

profile of v5, /device:TPU:1, one launch (start us, length us, event | category | flops | bytes accessed | tf_op | source)
XLA Modules:
  0.0 190.6 jit_solution(3507622606995950054)
XLA Ops:
  0.0 1.0 broadcast_in_dim.42.mass_ref
  1.0 0.0 copy-start
  1.1 1.0 copy-done
  2.1 0.7 copy-done.3
  2.8 1.1 scaled_start.1
  3.8 1.3 collective-permute-start
  5.2 0.3 broadcast_in_dim.41.column_ref
  5.5 8.9 %opening_products.1 = (f32[4096,128]{1,0:T(8,128)S(1)}, bf16[4096,512]{1,0:T(8,128)(2,1)S(1)}, bf16[256,512]{1,0:T(8,128)(2,1)S(1)}, f32[256,128]{1,0:T(8,128)S(1)}) custom-call(s32[8,512]{1,0:T(8,128)S(1)} %copy-done.2, s32[8,4096]{1,0:T(8,128)S(1)} %broadcast_in_dim.39.links_ref, s32[2048,128]{1,0:T(8,128)S(1)} %broadcast_in_dim.41.column_ref, ...), custom_call_target="tpu_custom_call" | custom-call | flops 8000000000 | bytes 16777216 | tf_op jit(solution)/shard_map/opening_products/pallas_call | solution.py:416
  14.4 0.8 collective-permute-done.rows_ref
  15.2 0.2 returned.3
  15.4 9.5 %collective-permute-start.1 = (bf16[256,128]{1,0:T(8,128)(2,1)S(1)}, bf16[256,128]{1,0:T(8,128)(2,1)S(1)}, u32[]{:S(2)}, u32[]{:S(2)}) collective-permute-start(bf16[256,128]{1,0:T(8,128)(2,1)S(1)} %returned.3), channel_id=1, source_target_pairs={{0,8},{8,16},{16,24},{24,32},{32,40},{40,48},{48,56},{56,64},{64,7... | collective-permute-start | bytes 196616 | tf_op jit(solution)/shard_map/ppermute | solution.py:337
  24.9 0.0 copy-start.4
  24.9 0.0 copy-start.1
  25.0 0.0 copy-start.5
  25.0 5.7 %assembled.3.summed_ref = f32[2048,128]{1,0:T(8,128)S(1)} custom-call(s32[8,512]{1,0:T(8,128)S(1)} %copy-done.2, s32[8,4096]{1,0:T(8,128)S(1)} %broadcast_in_dim.39.links_ref, f32[4096,128]{1,0:T(8,128)S(1)} %get-tuple-element.26.products_ref, bf16[4096,512]{1,0:T(8,128)(2,1)S(1)} %get-tuple-element.27.spread_ref, ...), custom_call_target="tpu_custom_call" | custom-call | flops 5000000000 | bytes 16777216 | tf_op jit(solution)/shard_map/assembled/pallas_call | solution.py:422
  30.6 0.0 collective-permute-done.1.arrived_ref
  30.7 1.4 first_step.1
  32.1 1.3 collective-permute-start.2
  33.4 6.3 %local_products.2 = (f32[4096,128]{1,0:T(8,128)S(1)}, f32[256,128]{1,0:T(8,128)S(1)}) custom-call(s32[8,512]{1,0:T(8,128)S(1)} %copy-done.2, s32[8,4096]{1,0:T(8,128)S(1)} %broadcast_in_dim.39.links_ref, s32[2048,128]{1,0:T(8,128)S(1)} %broadcast_in_dim.41.column_ref, f32[2304,128]{1,0:T(8,128)S(1)} %get-tuple-element.31.scaled_ref, ...), custom_call_target="tpu_custom_call" | custom-call | flops 5000000000 | bytes 16777216 | tf_op jit(solution)/shard_map/local_products/pallas_call | solution.py:420
  39.7 2.2 %collective-permute-done.2.rows_ref = bf16[256,128]{1,0:T(8,128)(2,1)S(1)} collective-permute-done((bf16[256,128]{1,0:T(8,128)(2,1)S(1)}, bf16[256,128]{1,0:T(8,128)(2,1)S(1)}, u32[]{:S(2)}, u32[]{:S(2)}) %collective-permute-start.2) | collective-permute-done | bytes 65568 | tf_op jit(solution)/shard_map/ppermute | solution.py:337
  42.0 0.2 returned.4
  42.2 9.1 %collective-permute-start.3 = (bf16[256,128]{1,0:T(8,128)(2,1)S(1)}, bf16[256,128]{1,0:T(8,128)(2,1)S(1)}, u32[]{:S(2)}, u32[]{:S(2)}) collective-permute-start(bf16[256,128]{1,0:T(8,128)(2,1)S(1)} %returned.4), channel_id=1, source_target_pairs={{0,8},{8,16},{16,24},{24,32},{32,40},{40,48},{48,56},{56,64},{64,7... | collective-permute-start | bytes 196616 | tf_op jit(solution)/shard_map/ppermute | solution.py:337
  51.3 5.7 %assembled.4.summed_ref = f32[2048,128]{1,0:T(8,128)S(1)} custom-call(s32[8,512]{1,0:T(8,128)S(1)} %copy-done.2, s32[8,4096]{1,0:T(8,128)S(1)} %broadcast_in_dim.39.links_ref, f32[4096,128]{1,0:T(8,128)S(1)} %get-tuple-element.32.products_ref, bf16[4096,512]{1,0:T(8,128)(2,1)S(1)} %get-tuple-element.27.spread_ref, ...), custom_call_target="tpu_custom_call" | custom-call | flops 5000000000 | bytes 16777216 | tf_op jit(solution)/shard_map/assembled/pallas_call | solution.py:422
  57.0 0.0 collective-permute-done.3.arrived_ref
  57.0 1.5 next_step.1
  58.5 1.3 collective-permute-start.4
  59.8 6.3 %local_products.3 = (f32[4096,128]{1,0:T(8,128)S(1)}, f32[256,128]{1,0:T(8,128)S(1)}) custom-call(s32[8,512]{1,0:T(8,128)S(1)} %copy-done.2, s32[8,4096]{1,0:T(8,128)S(1)} %broadcast_in_dim.39.links_ref, s32[2048,128]{1,0:T(8,128)S(1)} %broadcast_in_dim.41.column_ref, f32[2304,128]{1,0:T(8,128)S(1)} %get-tuple-element.36.scaled_ref, ...), custom_call_target="tpu_custom_call" | custom-call | flops 5000000000 | bytes 16777216 | tf_op jit(solution)/shard_map/local_products/pallas_call | solution.py:420
  66.1 1.3 collective-permute-done.4.rows_ref
  67.5 0.2 returned.5
  67.7 7.4 %collective-permute-start.5 = (bf16[256,128]{1,0:T(8,128)(2,1)S(1)}, bf16[256,128]{1,0:T(8,128)(2,1)S(1)}, u32[]{:S(2)}, u32[]{:S(2)}) collective-permute-start(bf16[256,128]{1,0:T(8,128)(2,1)S(1)} %returned.5), channel_id=1, source_target_pairs={{0,8},{8,16},{16,24},{24,32},{32,40},{40,48},{48,56},{56,64},{64,7... | collective-permute-start | bytes 196616 | tf_op jit(solution)/shard_map/ppermute | solution.py:337
  75.1 5.7 %assembled.5.summed_ref = f32[2048,128]{1,0:T(8,128)S(1)} custom-call(s32[8,512]{1,0:T(8,128)S(1)} %copy-done.2, s32[8,4096]{1,0:T(8,128)S(1)} %broadcast_in_dim.39.links_ref, f32[4096,128]{1,0:T(8,128)S(1)} %get-tuple-element.37.products_ref, bf16[4096,512]{1,0:T(8,128)(2,1)S(1)} %get-tuple-element.27.spread_ref, ...), custom_call_target="tpu_custom_call" | custom-call | flops 5000000000 | bytes 16777216 | tf_op jit(solution)/shard_map/assembled/pallas_call | solution.py:422
  80.7 0.0 collective-permute-done.5.arrived_ref
  80.7 1.3 filtered.1
  82.1 3.5 %all-to-all-start = ((bf16[4,512,128]{2,1,0:T(8,128)(2,1)}), bf16[4,512,128]{2,1,0:T(8,128)(2,1)S(1)}, u32[]{:S(2)}, u32[]{:S(2)}) async-start(bf16[4,512,128]{2,1,0:T(8,128)(2,1)} %bitcast.2), calls=%async_computation | async-start | bytes 1048576 | tf_op jit(solution)/shard_map/all_to_all | solution.py:341
  85.5 13.1 %all-to-all-done = bf16[4,512,128]{2,1,0:T(8,128)(2,1)S(1)} async-done(((bf16[4,512,128]{2,1,0:T(8,128)(2,1)}), bf16[4,512,128]{2,1,0:T(8,128)(2,1)S(1)}, u32[]{:S(2)}, u32[]{:S(2)}) %all-to-all-start) | async-done | bytes 524320 | tf_op jit(solution)/shard_map/all_to_all | solution.py:341
  98.6 0.1 broadcast_in_dim.43
  98.7 6.5 %all_to_all.35.rows_ref = bf16[2,4,512,128]{3,2,1,0:T(8,128)(2,1)S(1)} all-to-all(bf16[2,4,512,128]{3,2,1,0:T(8,128)(2,1)S(1)} %broadcast_in_dim.43), channel_id=1, replica_groups=mesh['dom_0'=4,'dom_1'=4,'dom_2'=2,'band_0'=4,'band_1'=2] {'band_1'}, dimensions={0} | all-to-all | bytes 2097152 | tf_op jit(solution)/shard_map/all_to_all | solution.py:341
  105.3 0.7 gram.1
  106.0 24.3 %all_to_all.36 = bf16[16,144,128]{2,1,0:T(8,128)(2,1)S(1)} all-to-all(bf16[16,144,128]{2,1,0:T(8,128)(2,1)S(1)} %bitcast.14), channel_id=1, replica_groups=mesh['dom_0'=4,'dom_1'=4,'dom_2'=2,'band_0'=4,'band_1'=2] {'dom_0','dom_1'}, dimensions={0} | all-to-all | bytes 1179648 | tf_op jit(solution)/shard_map/all_to_all | solution.py:341
  130.3 0.1 reduce_sum.24
  130.4 14.2 %all_to_all.37 = bf16[8,144,128]{2,1,0:T(8,128)(2,1)S(1)} all-to-all(bf16[8,144,128]{2,1,0:T(8,128)(2,1)S(1)} %broadcast_in_dim.44), channel_id=1, replica_groups=mesh['dom_0'=4,'dom_1'=4,'dom_2'=2,'band_0'=4,'band_1'=2] {'dom_2','band..., dimensions={0} | all-to-all | bytes 589824 | tf_op jit(solution)/shard_map/all_to_all | solution.py:341
  144.7 0.1 broadcast_in_dim.45
  144.8 13.4 %all_to_all.38 = bf16[16,144,128]{2,1,0:T(8,128)(2,1)S(1)} all-to-all(bf16[16,144,128]{2,1,0:T(8,128)(2,1)S(1)} %broadcast_in_dim.45), channel_id=1, replica_groups=mesh['dom_0'=4,'dom_1'=4,'dom_2'=2,'band_0'=4,'band_1'=2] {'dom_0','dom_1'}, dimensions={0} | all-to-all | bytes 1179648 | tf_op jit(solution)/shard_map/all_to_all | solution.py:341
  158.2 0.1 broadcast_in_dim.46
  158.3 9.1 %all_to_all.39 = bf16[2,2304,128]{2,1,0:T(8,128)(2,1)S(1)} all-to-all(bf16[2,2304,128]{2,1,0:T(8,128)(2,1)S(1)} %broadcast_in_dim.46), channel_id=1, replica_groups=mesh['dom_0'=4,'dom_1'=4,'dom_2'=2,'band_0'=4,'band_1'=2] {'band_1'}, dimensions={0} | all-to-all | bytes 2359296 | tf_op jit(solution)/shard_map/all_to_all | solution.py:341
  167.4 5.4 %correction.1 = (bf16[4,512,128]{2,1,0:T(8,128)(2,1)S(1)}, f32[8,128]{1,0:T(8,128)S(1)}) custom-call(s32[1]{0:T(128)} %bitcast.1.core_ref, bf16[36,128,128]{2,1,0:T(8,128)(2,1)S(1)} %bitcast.13, bf16[2,4,512,128]{3,2,1,0:T(8,128)(2,1)S(1)} %all_to_all.35.rows_ref), custom_call_target="tpu_custom_call" | custom-call | flops 4000000000 | bytes 8388608 | tf_op jit(solution)/shard_map/correction/pallas_call | solution.py:459
  172.8 16.7 %all_to_all.40 = bf16[4,512,128]{2,1,0:T(8,128)(2,1)S(1)} all-to-all(bf16[4,512,128]{2,1,0:T(8,128)(2,1)S(1)} %get-tuple-element.43), channel_id=1, replica_groups=mesh['dom_0'=4,'dom_1'=4,'dom_2'=2,'band_0'=4,'band_1'=2] {'band_0'}, dimensions={0} | all-to-all | bytes 1048576 | tf_op jit(solution)/shard_map/all_to_all | solution.py:341
  189.5 1.1 rotated.1
  (13 shorter events, 0.1 us)
Async XLA Ops:
  0.0 5.1 %copy-start.2 = (s32[8,512]{1,0:T(8,128)S(1)}, s32[8,512]{1,0:T(8,128)}, u32[]{:S(2)}) copy-start(s32[8,512]{1,0:T(8,128)} %index_ref.11) | copy-start | bytes 49156
  1.0 1.0 copy-start
  2.1 0.7 copy-start.3
  3.8 11.4 %collective-permute-start = (bf16[256,128]{1,0:T(8,128)(2,1)S(1)}, bf16[256,128]{1,0:T(8,128)(2,1)S(1)}, u32[]{:S(2)}, u32[]{:S(2)}) collective-permute-start(bf16[256,128]{1,0:T(8,128)(2,1)S(1)} %get-tuple-element.28), channel_id=1, source_target_pairs={{8,0},{16,8},{24,16},{32,24},{40,32},{48,40},{56,48},{64,56},{72,6... | collective-permute-start | bytes 196616 | tf_op jit(solution)/shard_map/ppermute | solution.py:337
  15.4 15.2 %collective-permute-start.1 = (bf16[256,128]{1,0:T(8,128)(2,1)S(1)}, bf16[256,128]{1,0:T(8,128)(2,1)S(1)}, u32[]{:S(2)}, u32[]{:S(2)}) collective-permute-start(bf16[256,128]{1,0:T(8,128)(2,1)S(1)} %returned.3), channel_id=1, source_target_pairs={{0,8},{8,16},{16,24},{24,32},{32,40},{40,48},{48,56},{56,64},{64,7... | collective-permute-start | bytes 196616 | tf_op jit(solution)/shard_map/ppermute | solution.py:337
  24.9 5.7 %copy-start.4 = (s32[256]{0:T(256)S(1)}, s32[256]{0:T(256)}, u32[]{:S(2)}) copy-start(s32[256]{0:T(256)} %param.9) | copy-start | bytes 3076
  24.9 5.7 %copy-start.1 = (bf16[2048,128]{1,0:T(8,128)(2,1)S(1)}, bf16[2048,128]{1,0:T(8,128)(2,1)}, u32[]{:S(2)}) copy-start(bf16[2048,128]{1,0:T(8,128)(2,1)} %previous_ref.1) | copy-start | bytes 1572868
  25.0 8.5 %copy-start.5 = (bf16[8,512,512]{2,1,0:T(8,128)(2,1)S(1)}, bf16[8,512,512]{2,1,0:T(8,128)(2,1)}, u32[]{:S(2)}) copy-start(bf16[8,512,512]{2,1,0:T(8,128)(2,1)} %cells_ref.3) | copy-start | bytes 12582916
  32.1 9.8 %collective-permute-start.2 = (bf16[256,128]{1,0:T(8,128)(2,1)S(1)}, bf16[256,128]{1,0:T(8,128)(2,1)S(1)}, u32[]{:S(2)}, u32[]{:S(2)}) collective-permute-start(bf16[256,128]{1,0:T(8,128)(2,1)S(1)} %get-tuple-element.33), channel_id=1, source_target_pairs={{8,0},{16,8},{24,16},{32,24},{40,32},{48,40},{56,48},{64,56},{72,6... | collective-permute-start | bytes 196616 | tf_op jit(solution)/shard_map/ppermute | solution.py:337
  42.2 14.8 %collective-permute-start.3 = (bf16[256,128]{1,0:T(8,128)(2,1)S(1)}, bf16[256,128]{1,0:T(8,128)(2,1)S(1)}, u32[]{:S(2)}, u32[]{:S(2)}) collective-permute-start(bf16[256,128]{1,0:T(8,128)(2,1)S(1)} %returned.4), channel_id=1, source_target_pairs={{0,8},{8,16},{16,24},{24,32},{32,40},{40,48},{48,56},{56,64},{64,7... | collective-permute-start | bytes 196616 | tf_op jit(solution)/shard_map/ppermute | solution.py:337
  58.5 8.9 %collective-permute-start.4 = (bf16[256,128]{1,0:T(8,128)(2,1)S(1)}, bf16[256,128]{1,0:T(8,128)(2,1)S(1)}, u32[]{:S(2)}, u32[]{:S(2)}) collective-permute-start(bf16[256,128]{1,0:T(8,128)(2,1)S(1)} %get-tuple-element.38), channel_id=1, source_target_pairs={{8,0},{16,8},{24,16},{32,24},{40,32},{48,40},{56,48},{64,56},{72,6... | collective-permute-start | bytes 196616 | tf_op jit(solution)/shard_map/ppermute | solution.py:337
  67.7 13.1 %collective-permute-start.5 = (bf16[256,128]{1,0:T(8,128)(2,1)S(1)}, bf16[256,128]{1,0:T(8,128)(2,1)S(1)}, u32[]{:S(2)}, u32[]{:S(2)}) collective-permute-start(bf16[256,128]{1,0:T(8,128)(2,1)S(1)} %returned.5), channel_id=1, source_target_pairs={{0,8},{8,16},{16,24},{24,32},{32,40},{40,48},{48,56},{56,64},{64,7... | collective-permute-start | bytes 196616 | tf_op jit(solution)/shard_map/ppermute | solution.py:337
  82.1 16.5 %all-to-all-start = ((bf16[4,512,128]{2,1,0:T(8,128)(2,1)}), bf16[4,512,128]{2,1,0:T(8,128)(2,1)S(1)}, u32[]{:S(2)}, u32[]{:S(2)}) async-start(bf16[4,512,128]{2,1,0:T(8,128)(2,1)} %bitcast.2), calls=%async_computation | async-start | bytes 1048576 | tf_op jit(solution)/shard_map/all_to_all | solution.py:341

commit v6 on v4

--- a/solution.py
+++ b/solution.py
@@ -80,74 +80,110 @@
     return one_hot(links == lax.broadcasted_iota(jnp.int32, (face, nodes), 0) + own)
 
 
-def take_entries(index_ref, column_ref, scaled_ref, held, narrow):
+def local_products(
+    own, face, index_ref, links_ref, column_ref, scaled_ref, cells_ref, products_ref, sent_ref,
+    held, narrow, received=None,
+):
     cells, nodes = index_ref.shape
     extent, width = scaled_ref.shape
-    copied = cells - column_ref.shape[0] // nodes
+    named_from = cells - column_ref.shape[0] // nodes
+    copied = named_from if received is None else cells - 1
     narrow[...] = scaled_ref[...].astype(BF16)
-    steps = 4
-    some = nodes // steps
-    rest = column_ref.shape[0] // steps
-
-    def take(i, carry):
-        first = pl.multiple_of(i * rest, rest)
-        named = column_ref[pl.ds(first, rest), :]
-        lane = lax.broadcasted_iota(jnp.int32, (rest, 128), 1)
+    sent_ref[...] = jnp.zeros_like(sent_ref)
+
+    def part(cell):
+        return slice(cell * nodes, (cell + 1) * nodes)
+
+    def by_one_hot(cell):
+        named = column_ref[part(cell - named_from), :]
+        lane = lax.broadcasted_iota(jnp.int32, (nodes, 128), 1)
         hits = jnp.concatenate([one_hot(named == lane + t) for t in range(0, extent, 128)], 1)
-        product = dot(hits, narrow[...])
-        for k in range(some // 8):
-            for cell in range(copied):
-                at = i * some + k * 8
-                rows = [scaled_ref[pl.ds(index_ref[cell, at + u], 1), :] for u in range(8)]
-                held[pl.ds(pl.multiple_of(cell * nodes + at, 8), 8), :] = jnp.concatenate(rows, 0)
-        held[pl.ds(copied * nodes + first, rest), :] = product
-        return carry
-
-    lax.fori_loop(0, steps, take, 0)
+        held[part(cell), :] = dot(hits, narrow[...])
+
+    def multiply(cell):
+        product = dot(cells_ref[cell], held[part(cell), :].astype(BF16))
+        products_ref[part(cell), :] = product
+        both = dot(face_hits(links_ref, own, face, cell, nodes), halves(product))
+        sent_ref[...] += both[:, :width] + both[:, width:]
+
+    def copy_rows(cell):
+        for at in range(0, nodes, 8):
+            rows = [scaled_ref[pl.ds(index_ref[cell, at + u], 1), :] for u in range(8)]
+            held[cell * nodes + at : cell * nodes + at + 8, :] = jnp.concatenate(rows, 0)
+
+    beside = [[] for _ in range(copied)]
+    for i, cell in enumerate(range(copied, cells)):
+        beside[i].append(functools.partial(by_one_hot, cell))
+    after = []
+    if received is None:
+        waiting = list(range(copied, cells)) + list(range(copied))
+        done = 0
+        for stage in range(cells - copied, copied):
+            for cell in waiting[done : done + 3]:
+                if cell >= copied or cell < stage:
+                    beside[stage].append(functools.partial(multiply, cell))
+                    done += 1
+    else:
+        for cell in range(cells):
+            stage = min(1 + cell // 2 if cell < 4 else cell - 1, copied - 1)
+            beside[stage].append(functools.partial(received, cell))
+        waiting = list(range(cells))
+        done = 0
+        for stage in range(3, copied):
+            beside[stage].append(functools.partial(multiply, waiting[done]))
+            done += 1
+    after = [functools.partial(multiply, cell) for cell in waiting[done:]]
+    for cell in range(copied):
+        for task in beside[cell]:
+            task()
+        copy_rows(cell)
+    for task in after:
+        task()
 
 
 def opening_body(
     own, face, index_ref, links_ref, column_ref, scaled_ref, matrices_ref, products_ref,
-    spread_ref, block_ref, sent_ref, held, narrow, cells_ref, sem,
-):
-    copy = pltpu.make_async_copy(matrices_ref, cells_ref, sem)
-    copy.start()
-    take_entries(index_ref, column_ref, scaled_ref, held, narrow)
-    copy.wait()
+    spread_ref, block_ref, sent_ref, low_ref, held, narrow, cells_ref, block, sems,
+):
     cells, nodes = index_ref.shape
-    width = scaled_ref.shape[1]
-    total = jnp.zeros((face, 2 * width), F32)
-    block = jnp.zeros((face, 2 * face), F32)
-    for cell in range(cells):
-        part = slice(cell * nodes, (cell + 1) * nodes)
+    copies = [
+        pltpu.make_async_copy(matrices_ref.at[c], cells_ref.at[c], sems.at[c])
+        for c in range(cells)
+    ]
+    for copy in copies:
+        copy.start()
+    block[...] = jnp.zeros_like(block)
+
+    def received(cell):
+        copies[cell].wait()
         hits = face_hits(links_ref, own, face, cell, nodes)
         columns = lax.dot_general(
             cells_ref[cell], hits, (((1,), (1,)), ((), ())), preferred_element_type=F32
         )
         both = halves(columns)
-        spread_ref[part, :] = both
-        block = block + dot(hits, both)
-        product = dot(cells_ref[cell], held[part, :].astype(BF16))
-        products_ref[part, :] = product
-        total = total + dot(hits, halves(product))
-    sent_ref[...] = total[:, :width] + total[:, width:]
-    block_ref[...] = halves(block[:, :face] + block[:, face:])
+        spread_ref[cell * nodes : (cell + 1) * nodes, :] = both
+        block[...] += dot(hits, both)
+        low = jnp.max(jnp.abs(both[:, face:].astype(F32)), axis=0, keepdims=True)
+        low_ref[cell : cell + 1, :] = jnp.max(low, axis=1, keepdims=True) + jnp.zeros(
+            (1, low_ref.shape[1]), F32
+        )
+
+    local_products(
+        own, face, index_ref, links_ref, column_ref, scaled_ref, cells_ref, products_ref, sent_ref,
+        held, narrow, received,
+    )
+    total = block[...]
+    block_ref[...] = halves(total[:, :face] + total[:, face:])
 
 
 def local_body(
     own, face, index_ref, links_ref, column_ref, scaled_ref, cells_ref, products_ref, sent_ref,
     held, narrow,
 ):
-    take_entries(index_ref, column_ref, scaled_ref, held, narrow)
-    cells, nodes = index_ref.shape
-    width = scaled_ref.shape[1]
-    total = jnp.zeros((face, 2 * width), F32)
-    for cell in range(cells):
-        part = slice(cell * nodes, (cell + 1) * nodes)
-        product = dot(cells_ref[cell], held[part, :].astype(BF16))
-        products_ref[part, :] = product
-        total = total + dot(face_hits(links_ref, own, face, cell, nodes), halves(product))
-    sent_ref[...] = total[:, :width] + total[:, width:]
+    local_products(
+        own, face, index_ref, links_ref, column_ref, scaled_ref, cells_ref, products_ref, sent_ref,
+        held, narrow,
+    )
 
 
 def returned_body(sent_ref, block_ref, rows_ref, total_ref):
@@ -156,20 +192,23 @@
 
 
 def assemble_body(
-    index_ref, links_ref, products_ref, spread_ref, rows_ref, summed_ref, whole, split, *totals
+    index_ref, low_ref, links_ref, products_ref, spread_ref, rows_ref, summed_ref, whole, split,
+    *totals
 ):
     cells, nodes = index_ref.shape
     own, width = summed_ref.shape
     added = len(totals)
     rows = rows_ref[...]
-    twice = jnp.concatenate([rows, rows], 0)
+    face = rows.shape[0]
     for cell in range(cells):
         part = slice(cell * nodes, (cell + 1) * nodes)
-        product = products_ref[part, :] + dot(spread_ref[part, :], twice)
-        if cell < added:
-            whole[part, :] = product
-        else:
-            split[(cell - added) * nodes : (cell - added + 1) * nodes, :] = halves(product)
+        whole[part, :] = products_ref[part, :] + dot(spread_ref[part, :face], rows)
+
+        def add_low(part=part):
+            whole[part, :] += dot(spread_ref[part, face:], rows_ref[...])
+
+        pl.when(low_ref[cell, 0] != 0.0)(add_low)
+    split[...] = halves(whole[added * nodes :, :])
     for total in totals:
         total[...] = jnp.zeros_like(total)
     steps = 4
@@ -367,7 +406,7 @@
     links = jnp.broadcast_to(connectivity.reshape(1, entries), (8, entries))
     copied = cells // 2
     column = jnp.broadcast_to(
-        connectivity[copied:].reshape(-1, 1), ((cells - copied) * cell_nodes, 128)
+        connectivity[copied + 1 :].reshape(-1, 1), ((cells - copied - 1) * cell_nodes, 128)
     )
     faces = jnp.broadcast_to(face_index.reshape(1, face), (8, face))
     face_list = face_index.reshape(1, face)
@@ -386,9 +425,13 @@
         [IN_SMEM] + [IN_VMEM] * 3 + [IN_ANY],
         [
             shape((entries, width), F32), shape((entries, 2 * face), BF16),
-            shape((face, 2 * face), BF16), shape((face, width), F32),
+            shape((face, 2 * face), BF16), shape((face, width), F32), shape((cells, 128), F32),
         ],
-        gathering + [pltpu.VMEM(cell_matrices.shape, BF16), pltpu.SemaphoreType.DMA],
+        gathering
+        + [
+            pltpu.VMEM(cell_matrices.shape, BF16), pltpu.VMEM((face, 2 * face), F32),
+            pltpu.SemaphoreType.DMA((cells,)),
+        ],
         8 * 10**9, 16 * 2**20, 45,
     )
     local = call(
@@ -400,9 +443,9 @@
         returned_body, "returned", [IN_VMEM] * 3, shape((face, width), F32), [], 10**8, 2**20,
     )
     assemble = call(
-        assemble_body, "assembled", [IN_SMEM] + [IN_VMEM] * 4, wide,
+        assemble_body, "assembled", [IN_SMEM] * 2 + [IN_VMEM] * 4, wide,
         [
-            pltpu.VMEM((copied * cell_nodes, width), F32),
+            pltpu.VMEM((entries, width), F32),
             pltpu.VMEM((entries - copied * cell_nodes, 2 * width), BF16),
         ]
         + [pltpu.VMEM((extent, width), F32)] * copied,
@@ -414,13 +457,13 @@
     for sweep in range(DEGREE):
         received = passed_along(rows, -1)
         if sweep == 0:
-            products, spread, block, sent = opening(
+            products, spread, block, sent, low = opening(
                 connectivity, links, column, scaled, cell_matrices
             )
         else:
             products, sent = local(connectivity, links, column, scaled, cell_matrices)
         arrived = passed_along(returned(sent, block, received), 1)
-        summed = assemble(connectivity, links, products, spread, received)
+        summed = assemble(connectivity, low, links, products, spread, received)
         parts = (summed, arrived, mass)
         if sweep == DEGREE - 1:
             filtered, rounded = call(

time: 191 us -> 197 us (1.031)
  Pallas kernels: 51.7 us -> 56.5 us
    pallas_call x3, Pallas kernels: 17 us -> 20.1 us  [on_device(): summed = assemble(connectivity, low, links, products, spread, received)]
  transfers between devices with their start and end apart: 7 -> 7, of which waited for: 4 -> 3; matrix products, arithmetic and copies ran while one was open for 0% -> 0% of each run, Pallas kernels for 20% -> 22%
where the time goes in v6:
time: 197 us; the launch traced here: 196 us
  blocking collectives  88.3 us (45%)
  Pallas kernels  56.5 us (29%)
  starting transfers between devices  33.9 us (17%)
  waiting for transfers between devices  13.9 us (7%)
  local copies, waits for them, and re-layouts  3.39 us (2%)
    all_to_all x6, blocking collectives, exchanged(): return lax.all_to_all(pieces, axes, split_axis=0, concat_axis=0, tiled=True)  88.3 us
    ppermute x6, starting transfers between devices, passed_along(): lax.ppermute(value, DOM, [(source, source + steps) for source in range(in...  30.4 us
    pallas_call x3, Pallas kernels, on_device(): summed = assemble(connectivity, low, links, products, spread, received)  20.1 us
    pallas_call x2, Pallas kernels, on_device(): products, sent = local(connectivity, links, column, scaled, cell_matrices)  12.6 us
    all_to_all x1, waiting for transfers between devices, exchanged(): return lax.all_to_all(pieces, axes, split_axis=0, concat_axis=0, tiled=True)  10.8 us
    pallas_call x1, Pallas kernels, on_device(): opening(connectivity, links, column, scaled, cell_matrices)  10.6 us
    pallas_call x1, Pallas kernels, on_device(): call(functools.partial(correct_body, own * domains), 'correction', [IN_SM...  5.36 us
  transfers between devices with their start and end apart: 7, of which 3 were waited for; matrix products, arithmetic and copies ran while one was open for 0% of the time, Pallas kernels for 22%

profile of v6, /device:TPU:1, one launch (start us, length us, event | category | flops | bytes accessed | tf_op | source)
XLA Modules:
  0.0 196.4 jit_solution(4145144637296403041)
XLA Ops:
  0.0 1.0 broadcast_in_dim.42.mass_ref
  1.0 0.0 copy-start
  1.1 1.0 copy-done
  2.1 0.7 copy-done.3
  2.8 1.1 scaled_start.1
  3.8 1.3 collective-permute-start
  5.2 0.3 broadcast_in_dim.41.column_ref
  5.5 10.6 %opening_products.1 = (f32[4096,128]{1,0:T(8,128)S(1)}, bf16[4096,512]{1,0:T(8,128)(2,1)S(1)}, bf16[256,512]{1,0:T(8,128)(2,1)S(1)}, f32[256,128]{1,0:T(8,128)S(1)}, f32[8,128]{1,0:T(8,128)S(1)}) custom-call(s32[8,512]{1,0:T(8,128)S(1)} %copy-done.2, s32[8,4096]{1,0:T(8,128)S(1)} %broadcast_in_dim.39.links_ref, s32[1536,128]{1,0:T(8,128)S(1)} %broadcast_in_dim.41.column_ref, ...), custom_call_target="tpu_custom_call" | custom-call | flops 8000000000 | bytes 16777216 | tf_op jit(solution)/shard_map/opening_products/pallas_call | solution.py:460
  16.0 0.0 collective-permute-done.rows_ref
  16.1 0.2 returned.3
  16.3 10.3 %collective-permute-start.1 = (f32[256,128]{1,0:T(8,128)S(1)}, f32[256,128]{1,0:T(8,128)S(1)}, u32[]{:S(2)}, u32[]{:S(2)}) collective-permute-start(f32[256,128]{1,0:T(8,128)S(1)} %returned.3), channel_id=1, source_target_pairs={{0,8},{8,16},{16,24},{24,32},{32,40},{40,48},{48,56},{56,64},{64,7... | collective-permute-start | bytes 393224 | tf_op jit(solution)/shard_map/ppermute | solution.py:377
  26.6 0.0 copy-start.4
  26.6 0.0 copy-start.1
  26.6 0.0 copy-start.5
  26.6 6.7 %assembled.3.summed_ref = f32[2048,128]{1,0:T(8,128)S(1)} custom-call(s32[8,512]{1,0:T(8,128)S(1)} %copy-done.2, f32[8,128]{1,0:T(8,128)S(1)} %get-tuple-element.27.low_ref, s32[8,4096]{1,0:T(8,128)S(1)} %broadcast_in_dim.39.links_ref, f32[4096,128]{1,0:T(8,128)S(1)} %get-tuple-element.28.products_ref, bf16[4096,512]{1,0:T(8,128)(2,1)S(1)} %get-tuple-element.29.spread_ref, ...), custom_call_target="tpu_custom_call" | custom-call | flops 5000000000 | bytes 16777216 | tf_op jit(solution)/shard_map/assembled/pallas_call | solution.py:466
  33.3 0.0 collective-permute-done.1.arrived_ref
  33.3 1.5 first_step.1
  34.8 1.5 collective-permute-start.2
  36.3 6.3 %local_products.2 = (f32[4096,128]{1,0:T(8,128)S(1)}, f32[256,128]{1,0:T(8,128)S(1)}) custom-call(s32[8,512]{1,0:T(8,128)S(1)} %copy-done.2, s32[8,4096]{1,0:T(8,128)S(1)} %broadcast_in_dim.39.links_ref, s32[1536,128]{1,0:T(8,128)S(1)} %broadcast_in_dim.41.column_ref, f32[2304,128]{1,0:T(8,128)S(1)} %get-tuple-element.33.scaled_ref, ...), custom_call_target="tpu_custom_call" | custom-call | flops 5000000000 | bytes 16777216 | tf_op jit(solution)/shard_map/local_products/pallas_call | solution.py:464
  42.6 2.0 %collective-permute-done.2.rows_ref = bf16[256,128]{1,0:T(8,128)(2,1)S(1)} collective-permute-done((bf16[256,128]{1,0:T(8,128)(2,1)S(1)}, bf16[256,128]{1,0:T(8,128)(2,1)S(1)}, u32[]{:S(2)}, u32[]{:S(2)}) %collective-permute-start.2) | collective-permute-done | bytes 65568 | tf_op jit(solution)/shard_map/ppermute | solution.py:377
  44.6 0.2 returned.4
  44.9 8.2 %collective-permute-start.3 = (f32[256,128]{1,0:T(8,128)S(1)}, f32[256,128]{1,0:T(8,128)S(1)}, u32[]{:S(2)}, u32[]{:S(2)}) collective-permute-start(f32[256,128]{1,0:T(8,128)S(1)} %returned.4), channel_id=1, source_target_pairs={{0,8},{8,16},{16,24},{24,32},{32,40},{40,48},{48,56},{56,64},{64,7... | collective-permute-start | bytes 393224 | tf_op jit(solution)/shard_map/ppermute | solution.py:377
  53.0 6.7 %assembled.4.summed_ref = f32[2048,128]{1,0:T(8,128)S(1)} custom-call(s32[8,512]{1,0:T(8,128)S(1)} %copy-done.2, f32[8,128]{1,0:T(8,128)S(1)} %get-tuple-element.27.low_ref, s32[8,4096]{1,0:T(8,128)S(1)} %broadcast_in_dim.39.links_ref, f32[4096,128]{1,0:T(8,128)S(1)} %get-tuple-element.34.products_ref, bf16[4096,512]{1,0:T(8,128)(2,1)S(1)} %get-tuple-element.29.spread_ref, ...), custom_call_target="tpu_custom_call" | custom-call | flops 5000000000 | bytes 16777216 | tf_op jit(solution)/shard_map/assembled/pallas_call | solution.py:466
  59.7 0.0 collective-permute-done.3.arrived_ref
  59.7 1.6 next_step.1
  61.3 1.5 collective-permute-start.4
  62.8 6.3 %local_products.3 = (f32[4096,128]{1,0:T(8,128)S(1)}, f32[256,128]{1,0:T(8,128)S(1)}) custom-call(s32[8,512]{1,0:T(8,128)S(1)} %copy-done.2, s32[8,4096]{1,0:T(8,128)S(1)} %broadcast_in_dim.39.links_ref, s32[1536,128]{1,0:T(8,128)S(1)} %broadcast_in_dim.41.column_ref, f32[2304,128]{1,0:T(8,128)S(1)} %get-tuple-element.38.scaled_ref, ...), custom_call_target="tpu_custom_call" | custom-call | flops 5000000000 | bytes 16777216 | tf_op jit(solution)/shard_map/local_products/pallas_call | solution.py:464
  69.2 1.1 collective-permute-done.4.rows_ref
  70.2 0.2 returned.5
  70.5 7.7 %collective-permute-start.5 = (f32[256,128]{1,0:T(8,128)S(1)}, f32[256,128]{1,0:T(8,128)S(1)}, u32[]{:S(2)}, u32[]{:S(2)}) collective-permute-start(f32[256,128]{1,0:T(8,128)S(1)} %returned.5), channel_id=1, source_target_pairs={{0,8},{8,16},{16,24},{24,32},{32,40},{40,48},{48,56},{56,64},{64,7... | collective-permute-start | bytes 393224 | tf_op jit(solution)/shard_map/ppermute | solution.py:377
  78.1 6.7 %assembled.5.summed_ref = f32[2048,128]{1,0:T(8,128)S(1)} custom-call(s32[8,512]{1,0:T(8,128)S(1)} %copy-done.2, f32[8,128]{1,0:T(8,128)S(1)} %get-tuple-element.27.low_ref, s32[8,4096]{1,0:T(8,128)S(1)} %broadcast_in_dim.39.links_ref, f32[4096,128]{1,0:T(8,128)S(1)} %get-tuple-element.39.products_ref, bf16[4096,512]{1,0:T(8,128)(2,1)S(1)} %get-tuple-element.29.spread_ref, ...), custom_call_target="tpu_custom_call" | custom-call | flops 5000000000 | bytes 16777216 | tf_op jit(solution)/shard_map/assembled/pallas_call | solution.py:466
  84.8 0.0 collective-permute-done.5.arrived_ref
  84.8 1.4 filtered.1
  86.2 3.5 %all-to-all-start = ((bf16[4,512,128]{2,1,0:T(8,128)(2,1)}), bf16[4,512,128]{2,1,0:T(8,128)(2,1)S(1)}, u32[]{:S(2)}, u32[]{:S(2)}) async-start(bf16[4,512,128]{2,1,0:T(8,128)(2,1)} %bitcast.2), calls=%async_computation | async-start | bytes 1048576 | tf_op jit(solution)/shard_map/all_to_all | solution.py:381
  89.7 10.8 %all-to-all-done = bf16[4,512,128]{2,1,0:T(8,128)(2,1)S(1)} async-done(((bf16[4,512,128]{2,1,0:T(8,128)(2,1)}), bf16[4,512,128]{2,1,0:T(8,128)(2,1)S(1)}, u32[]{:S(2)}, u32[]{:S(2)}) %all-to-all-start) | async-done | bytes 524320 | tf_op jit(solution)/shard_map/all_to_all | solution.py:381
  100.5 0.1 broadcast_in_dim.43
  100.6 8.8 %all_to_all.35.rows_ref = bf16[2,4,512,128]{3,2,1,0:T(8,128)(2,1)S(1)} all-to-all(bf16[2,4,512,128]{3,2,1,0:T(8,128)(2,1)S(1)} %broadcast_in_dim.43), channel_id=1, replica_groups=mesh['dom_0'=4,'dom_1'=4,'dom_2'=2,'band_0'=4,'band_1'=2] {'band_1'}, dimensions={0} | all-to-all | bytes 2097152 | tf_op jit(solution)/shard_map/all_to_all | solution.py:381
  109.4 0.7 gram.1
  110.2 25.4 %all_to_all.36 = bf16[16,144,128]{2,1,0:T(8,128)(2,1)S(1)} all-to-all(bf16[16,144,128]{2,1,0:T(8,128)(2,1)S(1)} %bitcast.11), channel_id=1, replica_groups=mesh['dom_0'=4,'dom_1'=4,'dom_2'=2,'band_0'=4,'band_1'=2] {'dom_0','dom_1'}, dimensions={0} | all-to-all | bytes 1179648 | tf_op jit(solution)/shard_map/all_to_all | solution.py:381
  135.6 0.1 reduce_sum.24
  135.7 14.7 %all_to_all.37 = bf16[8,144,128]{2,1,0:T(8,128)(2,1)S(1)} all-to-all(bf16[8,144,128]{2,1,0:T(8,128)(2,1)S(1)} %broadcast_in_dim.44), channel_id=1, replica_groups=mesh['dom_0'=4,'dom_1'=4,'dom_2'=2,'band_0'=4,'band_1'=2] {'dom_2','band..., dimensions={0} | all-to-all | bytes 589824 | tf_op jit(solution)/shard_map/all_to_all | solution.py:381
  150.5 0.1 broadcast_in_dim.45
  150.6 13.4 %all_to_all.38 = bf16[16,144,128]{2,1,0:T(8,128)(2,1)S(1)} all-to-all(bf16[16,144,128]{2,1,0:T(8,128)(2,1)S(1)} %broadcast_in_dim.45), channel_id=1, replica_groups=mesh['dom_0'=4,'dom_1'=4,'dom_2'=2,'band_0'=4,'band_1'=2] {'dom_0','dom_1'}, dimensions={0} | all-to-all | bytes 1179648 | tf_op jit(solution)/shard_map/all_to_all | solution.py:381
  164.0 0.1 broadcast_in_dim.46
  164.1 9.1 %all_to_all.39 = bf16[2,2304,128]{2,1,0:T(8,128)(2,1)S(1)} all-to-all(bf16[2,2304,128]{2,1,0:T(8,128)(2,1)S(1)} %broadcast_in_dim.46), channel_id=1, replica_groups=mesh['dom_0'=4,'dom_1'=4,'dom_2'=2,'band_0'=4,'band_1'=2] {'band_1'}, dimensions={0} | all-to-all | bytes 2359296 | tf_op jit(solution)/shard_map/all_to_all | solution.py:381
  173.2 5.4 %correction.1 = (bf16[4,512,128]{2,1,0:T(8,128)(2,1)S(1)}, f32[8,128]{1,0:T(8,128)S(1)}) custom-call(s32[1]{0:T(128)} %bitcast.1.core_ref, bf16[36,128,128]{2,1,0:T(8,128)(2,1)S(1)} %bitcast.10, bf16[2,4,512,128]{3,2,1,0:T(8,128)(2,1)S(1)} %all_to_all.35.rows_ref), custom_call_target="tpu_custom_call" | custom-call | flops 4000000000 | bytes 8388608 | tf_op jit(solution)/shard_map/correction/pallas_call | solution.py:503
  178.6 16.7 %all_to_all.40 = bf16[4,512,128]{2,1,0:T(8,128)(2,1)S(1)} all-to-all(bf16[4,512,128]{2,1,0:T(8,128)(2,1)S(1)} %get-tuple-element.45), channel_id=1, replica_groups=mesh['dom_0'=4,'dom_1'=4,'dom_2'=2,'band_0'=4,'band_1'=2] {'band_0'}, dimensions={0} | all-to-all | bytes 1048576 | tf_op jit(solution)/shard_map/all_to_all | solution.py:381
  195.3 1.1 rotated.1
  (13 shorter events, 0.1 us)
Async XLA Ops:
  0.0 5.1 %copy-start.2 = (s32[8,512]{1,0:T(8,128)S(1)}, s32[8,512]{1,0:T(8,128)}, u32[]{:S(2)}) copy-start(s32[8,512]{1,0:T(8,128)} %index_ref.11) | copy-start | bytes 49156
  1.0 1.0 copy-start
  2.1 0.7 copy-start.3
  3.8 12.2 %collective-permute-start = (bf16[256,128]{1,0:T(8,128)(2,1)S(1)}, bf16[256,128]{1,0:T(8,128)(2,1)S(1)}, u32[]{:S(2)}, u32[]{:S(2)}) collective-permute-start(bf16[256,128]{1,0:T(8,128)(2,1)S(1)} %get-tuple-element.30), channel_id=1, source_target_pairs={{8,0},{16,8},{24,16},{32,24},{40,32},{48,40},{56,48},{64,56},{72,6... | collective-permute-start | bytes 196616 | tf_op jit(solution)/shard_map/ppermute | solution.py:377
  16.3 17.0 %collective-permute-start.1 = (f32[256,128]{1,0:T(8,128)S(1)}, f32[256,128]{1,0:T(8,128)S(1)}, u32[]{:S(2)}, u32[]{:S(2)}) collective-permute-start(f32[256,128]{1,0:T(8,128)S(1)} %returned.3), channel_id=1, source_target_pairs={{0,8},{8,16},{16,24},{24,32},{32,40},{40,48},{48,56},{56,64},{64,7... | collective-permute-start | bytes 393224 | tf_op jit(solution)/shard_map/ppermute | solution.py:377
  26.6 6.7 %copy-start.4 = (s32[256]{0:T(256)S(1)}, s32[256]{0:T(256)}, u32[]{:S(2)}) copy-start(s32[256]{0:T(256)} %param.9) | copy-start | bytes 3076
  26.6 6.7 %copy-start.1 = (bf16[2048,128]{1,0:T(8,128)(2,1)S(1)}, bf16[2048,128]{1,0:T(8,128)(2,1)}, u32[]{:S(2)}) copy-start(bf16[2048,128]{1,0:T(8,128)(2,1)} %previous_ref.1) | copy-start | bytes 1572868
  26.6 9.7 %copy-start.5 = (bf16[8,512,512]{2,1,0:T(8,128)(2,1)S(1)}, bf16[8,512,512]{2,1,0:T(8,128)(2,1)}, u32[]{:S(2)}) copy-start(bf16[8,512,512]{2,1,0:T(8,128)(2,1)} %cells_ref.3) | copy-start | bytes 12582916
  34.8 9.8 %collective-permute-start.2 = (bf16[256,128]{1,0:T(8,128)(2,1)S(1)}, bf16[256,128]{1,0:T(8,128)(2,1)S(1)}, u32[]{:S(2)}, u32[]{:S(2)}) collective-permute-start(bf16[256,128]{1,0:T(8,128)(2,1)S(1)} %get-tuple-element.35), channel_id=1, source_target_pairs={{8,0},{16,8},{24,16},{32,24},{40,32},{48,40},{56,48},{64,56},{72,6... | collective-permute-start | bytes 196616 | tf_op jit(solution)/shard_map/ppermute | solution.py:377
  44.9 14.9 %collective-permute-start.3 = (f32[256,128]{1,0:T(8,128)S(1)}, f32[256,128]{1,0:T(8,128)S(1)}, u32[]{:S(2)}, u32[]{:S(2)}) collective-permute-start(f32[256,128]{1,0:T(8,128)S(1)} %returned.4), channel_id=1, source_target_pairs={{0,8},{8,16},{16,24},{24,32},{32,40},{40,48},{48,56},{56,64},{64,7... | collective-permute-start | bytes 393224 | tf_op jit(solution)/shard_map/ppermute | solution.py:377
  61.3 8.9 %collective-permute-start.4 = (bf16[256,128]{1,0:T(8,128)(2,1)S(1)}, bf16[256,128]{1,0:T(8,128)(2,1)S(1)}, u32[]{:S(2)}, u32[]{:S(2)}) collective-permute-start(bf16[256,128]{1,0:T(8,128)(2,1)S(1)} %get-tuple-element.40), channel_id=1, source_target_pairs={{8,0},{16,8},{24,16},{32,24},{40,32},{48,40},{56,48},{64,56},{72,6... | collective-permute-start | bytes 196616 | tf_op jit(solution)/shard_map/ppermute | solution.py:377
  70.5 14.4 %collective-permute-start.5 = (f32[256,128]{1,0:T(8,128)S(1)}, f32[256,128]{1,0:T(8,128)S(1)}, u32[]{:S(2)}, u32[]{:S(2)}) collective-permute-start(f32[256,128]{1,0:T(8,128)S(1)} %returned.5), channel_id=1, source_target_pairs={{0,8},{8,16},{16,24},{24,32},{32,40},{40,48},{48,56},{56,64},{64,7... | collective-permute-start | bytes 393224 | tf_op jit(solution)/shard_map/ppermute | solution.py:377
  86.2 14.3 %all-to-all-start = ((bf16[4,512,128]{2,1,0:T(8,128)(2,1)}), bf16[4,512,128]{2,1,0:T(8,128)(2,1)S(1)}, u32[]{:S(2)}, u32[]{:S(2)}) async-start(bf16[4,512,128]{2,1,0:T(8,128)(2,1)} %bitcast.2), calls=%async_computation | async-start | bytes 1048576 | tf_op jit(solution)/shard_map/all_to_all | solution.py:381

commit v7 on v4

--- a/solution.py
+++ b/solution.py
@@ -55,10 +55,7 @@
     return jnp.where(hit, 1.0, 0.0).astype(BF16)
 
 
-def scale_rows(own, width, values, mass_ref, face_ref, scaled_ref, rows_ref, picked):
-    scaled_ref[:own, :] = (mass_ref[...] * values).astype(BF16).astype(F32)
-    scaled_ref[own:, :] = jnp.zeros((scaled_ref.shape[0] - own, width), F32)
-
+def pick_rows(face_ref, scaled_ref, rows_ref, picked):
     def take(i, carry):
         rows = [scaled_ref[pl.ds(face_ref[0, i * 8 + u], 1), :] for u in range(8)]
         picked[pl.ds(pl.multiple_of(i * 8, 8), 8), :] = jnp.concatenate(rows, 0)
@@ -68,11 +65,10 @@
     rows_ref[...] = picked[...].astype(BF16)
 
 
-def start_body(face_ref, wave_ref, mass_ref, scaled_ref, rows_ref, picked):
-    own, width = wave_ref.shape
-    scale_rows(
-        own, width, wave_ref[...].astype(F32), mass_ref, face_ref, scaled_ref, rows_ref, picked
-    )
+def scale_rows(own, width, values, mass_ref, face_ref, scaled_ref, rows_ref, picked):
+    scaled_ref[:own, :] = (mass_ref[...] * values).astype(BF16).astype(F32)
+    scaled_ref[own:, :] = jnp.zeros((scaled_ref.shape[0] - own, width), F32)
+    pick_rows(face_ref, scaled_ref, rows_ref, picked)
 
 
 def face_hits(links_ref, own, face, cell, nodes):
@@ -377,8 +373,7 @@
     rows_shape = shape((face, width), BF16)
     wide = shape((own, width), F32)
     start = call(
-        start_body, "scaled_start", [IN_SMEM] + [IN_VMEM] * 2, [scaled_shape, rows_shape], [picked],
-        10**6, 3 * 2**20,
+        pick_rows, "face_rows", [IN_SMEM, IN_VMEM], rows_shape, [picked], 10**6, 2**20,
     )
     gathering = [pltpu.VMEM((entries, width), F32), pltpu.VMEM((extent, width), BF16)]
     opening = call(
@@ -409,7 +404,9 @@
         5 * 10**9, 16 * 2**20,
     )
 
-    scaled, rows = start(face_list, wavefunctions, mass)
+    scaled = (mass_scale[:, None] * wavefunctions.astype(F32)).astype(BF16).astype(F32)
+    scaled = jnp.pad(scaled, ((0, face), (0, 0)))
+    rows = start(face_list, scaled)
     previous, current = None, wavefunctions
     for sweep in range(DEGREE):
         received = passed_along(rows, -1)

time: 191 us -> 190 us (level)
  local copies, waits for them, and re-layouts: 3.45 us -> 1.03 us
where the time goes in v7:
time: 190 us
  blocking collectives  87.1 us (46%)
  Pallas kernels  51.7 us (27%)
  starting transfers between devices  32.8 us (17%)
  waiting for transfers between devices  15.1 us (8%)
    all_to_all x6, blocking collectives, exchanged(): return lax.all_to_all(pieces, axes, split_axis=0, concat_axis=0, tiled=True)  87.1 us
    ppermute x6, starting transfers between devices, passed_along(): lax.ppermute(value, DOM, [(source, source + steps) for source in range(in...  29.2 us
    pallas_call x3, Pallas kernels, on_device(): summed = assemble(connectivity, links, products, spread, received)  17.1 us
    pallas_call x2, Pallas kernels, on_device(): products, sent = local(connectivity, links, column, scaled, cell_matrices)  12.6 us
    all_to_all x1, waiting for transfers between devices, exchanged(): return lax.all_to_all(pieces, axes, split_axis=0, concat_axis=0, tiled=True)  10.8 us
    pallas_call x1, Pallas kernels, on_device(): opening(connectivity, links, column, scaled, cell_matrices)  8.91 us
    pallas_call x1, Pallas kernels, on_device(): call(functools.partial(correct_body, own * domains), 'correction', [IN_SM...  5.35 us
    ppermute x6, waiting for transfers between devices, passed_along(): lax.ppermute(value, DOM, [(source, source + steps) for source in range(in...  4.29 us
  transfers between devices with their start and end apart: 7, of which 4 were waited for; matrix products, arithmetic and copies ran while one was open for 0% of the time, Pallas kernels for 20%

profile of v7, /device:TPU:1, one launch (start us, length us, event | category | flops | bytes accessed | tf_op | source)
XLA Modules:
  0.0 189.8 jit_solution(8704669049962792060)
XLA Ops:
  0.0 1.4 multiply_convert_fusion
  1.4 0.0 copy-start.1
  1.4 0.1 pad_convert_fusion.scaled_ref
  1.5 0.9 face_rows.1
  2.4 1.3 collective-permute-start
  3.8 0.3 broadcast_in_dim.40.column_ref
  4.1 8.9 %opening_products.1 = (f32[4096,128]{1,0:T(8,128)S(1)}, bf16[4096,512]{1,0:T(8,128)(2,1)S(1)}, bf16[256,512]{1,0:T(8,128)(2,1)S(1)}, f32[256,128]{1,0:T(8,128)S(1)}) custom-call(s32[8,512]{1,0:T(8,128)S(1)} %copy-done.1, s32[8,4096]{1,0:T(8,128)S(1)} %broadcast_in_dim.38.links_ref, s32[2048,128]{1,0:T(8,128)S(1)} %broadcast_in_dim.40.column_ref, ...), custom_call_target="tpu_custom_call" | custom-call | flops 8000000000 | bytes 16777216 | tf_op jit(solution)/shard_map/opening_products/pallas_call | solution.py:414
  13.0 0.8 collective-permute-done.rows_ref
  13.8 0.2 returned.3
  14.0 9.5 %collective-permute-start.1 = (f32[256,128]{1,0:T(8,128)S(1)}, f32[256,128]{1,0:T(8,128)S(1)}, u32[]{:S(2)}, u32[]{:S(2)}) collective-permute-start(f32[256,128]{1,0:T(8,128)S(1)} %returned.3), channel_id=1, source_target_pairs={{0,8},{8,16},{16,24},{24,32},{32,40},{40,48},{48,56},{56,64},{64,7... | collective-permute-start | bytes 393224 | tf_op jit(solution)/shard_map/ppermute | solution.py:334
  23.5 0.0 copy-start.4
  23.5 0.0 copy-start
  23.5 5.7 %assembled.3.summed_ref = f32[2048,128]{1,0:T(8,128)S(1)} custom-call(s32[8,512]{1,0:T(8,128)S(1)} %copy-done.1, s32[8,4096]{1,0:T(8,128)S(1)} %broadcast_in_dim.38.links_ref, f32[4096,128]{1,0:T(8,128)S(1)} %get-tuple-element.23.products_ref, bf16[4096,512]{1,0:T(8,128)(2,1)S(1)} %get-tuple-element.24.spread_ref, ...), custom_call_target="tpu_custom_call" | custom-call | flops 5000000000 | bytes 16777216 | tf_op jit(solution)/shard_map/assembled/pallas_call | solution.py:420
  29.2 0.0 collective-permute-done.1.arrived_ref
  29.3 0.0 copy-start.3
  29.3 0.3 mul.8.mass_ref
  29.6 1.5 first_step.1
  31.1 1.3 collective-permute-start.2
  32.4 6.3 %local_products.2 = (f32[4096,128]{1,0:T(8,128)S(1)}, f32[256,128]{1,0:T(8,128)S(1)}) custom-call(s32[8,512]{1,0:T(8,128)S(1)} %copy-done.1, s32[8,4096]{1,0:T(8,128)S(1)} %broadcast_in_dim.38.links_ref, s32[2048,128]{1,0:T(8,128)S(1)} %broadcast_in_dim.40.column_ref, f32[2304,128]{1,0:T(8,128)S(1)} %get-tuple-element.27.scaled_ref, ...), custom_call_target="tpu_custom_call" | custom-call | flops 5000000000 | bytes 16777216 | tf_op jit(solution)/shard_map/local_products/pallas_call | solution.py:418
  38.7 2.2 %collective-permute-done.2.rows_ref = bf16[256,128]{1,0:T(8,128)(2,1)S(1)} collective-permute-done((bf16[256,128]{1,0:T(8,128)(2,1)S(1)}, bf16[256,128]{1,0:T(8,128)(2,1)S(1)}, u32[]{:S(2)}, u32[]{:S(2)}) %collective-permute-start.2) | collective-permute-done | bytes 65568 | tf_op jit(solution)/shard_map/ppermute | solution.py:334
  41.0 0.2 returned.4
  41.2 8.3 %collective-permute-start.3 = (f32[256,128]{1,0:T(8,128)S(1)}, f32[256,128]{1,0:T(8,128)S(1)}, u32[]{:S(2)}, u32[]{:S(2)}) collective-permute-start(f32[256,128]{1,0:T(8,128)S(1)} %returned.4), channel_id=1, source_target_pairs={{0,8},{8,16},{16,24},{24,32},{32,40},{40,48},{48,56},{56,64},{64,7... | collective-permute-start | bytes 393224 | tf_op jit(solution)/shard_map/ppermute | solution.py:334
  49.5 5.7 %assembled.4.summed_ref = f32[2048,128]{1,0:T(8,128)S(1)} custom-call(s32[8,512]{1,0:T(8,128)S(1)} %copy-done.1, s32[8,4096]{1,0:T(8,128)S(1)} %broadcast_in_dim.38.links_ref, f32[4096,128]{1,0:T(8,128)S(1)} %get-tuple-element.28.products_ref, bf16[4096,512]{1,0:T(8,128)(2,1)S(1)} %get-tuple-element.24.spread_ref, ...), custom_call_target="tpu_custom_call" | custom-call | flops 5000000000 | bytes 16777216 | tf_op jit(solution)/shard_map/assembled/pallas_call | solution.py:420
  55.2 0.0 collective-permute-done.3.arrived_ref
  55.2 1.6 next_step.1
  56.8 1.3 collective-permute-start.4
  58.1 6.3 %local_products.3 = (f32[4096,128]{1,0:T(8,128)S(1)}, f32[256,128]{1,0:T(8,128)S(1)}) custom-call(s32[8,512]{1,0:T(8,128)S(1)} %copy-done.1, s32[8,4096]{1,0:T(8,128)S(1)} %broadcast_in_dim.38.links_ref, s32[2048,128]{1,0:T(8,128)S(1)} %broadcast_in_dim.40.column_ref, f32[2304,128]{1,0:T(8,128)S(1)} %get-tuple-element.32.scaled_ref, ...), custom_call_target="tpu_custom_call" | custom-call | flops 5000000000 | bytes 16777216 | tf_op jit(solution)/shard_map/local_products/pallas_call | solution.py:418
  64.5 1.3 collective-permute-done.4.rows_ref
  65.8 0.2 returned.5
  66.0 7.5 %collective-permute-start.5 = (f32[256,128]{1,0:T(8,128)S(1)}, f32[256,128]{1,0:T(8,128)S(1)}, u32[]{:S(2)}, u32[]{:S(2)}) collective-permute-start(f32[256,128]{1,0:T(8,128)S(1)} %returned.5), channel_id=1, source_target_pairs={{0,8},{8,16},{16,24},{24,32},{32,40},{40,48},{48,56},{56,64},{64,7... | collective-permute-start | bytes 393224 | tf_op jit(solution)/shard_map/ppermute | solution.py:334
  73.5 5.7 %assembled.5.summed_ref = f32[2048,128]{1,0:T(8,128)S(1)} custom-call(s32[8,512]{1,0:T(8,128)S(1)} %copy-done.1, s32[8,4096]{1,0:T(8,128)S(1)} %broadcast_in_dim.38.links_ref, f32[4096,128]{1,0:T(8,128)S(1)} %get-tuple-element.33.products_ref, bf16[4096,512]{1,0:T(8,128)(2,1)S(1)} %get-tuple-element.24.spread_ref, ...), custom_call_target="tpu_custom_call" | custom-call | flops 5000000000 | bytes 16777216 | tf_op jit(solution)/shard_map/assembled/pallas_call | solution.py:420
  79.1 0.0 collective-permute-done.5.arrived_ref
  79.2 1.3 filtered.1
  80.5 3.6 %all-to-all-start = ((bf16[4,512,128]{2,1,0:T(8,128)(2,1)}), bf16[4,512,128]{2,1,0:T(8,128)(2,1)S(1)}, u32[]{:S(2)}, u32[]{:S(2)}) async-start(bf16[4,512,128]{2,1,0:T(8,128)(2,1)} %bitcast.2), calls=%async_computation | async-start | bytes 1048576 | tf_op jit(solution)/shard_map/all_to_all | solution.py:338
  84.1 10.8 %all-to-all-done = bf16[4,512,128]{2,1,0:T(8,128)(2,1)S(1)} async-done(((bf16[4,512,128]{2,1,0:T(8,128)(2,1)}), bf16[4,512,128]{2,1,0:T(8,128)(2,1)S(1)}, u32[]{:S(2)}, u32[]{:S(2)}) %all-to-all-start) | async-done | bytes 524320 | tf_op jit(solution)/shard_map/all_to_all | solution.py:338
  95.0 0.1 broadcast_in_dim.41
  95.1 8.8 %all_to_all.35.rows_ref = bf16[2,4,512,128]{3,2,1,0:T(8,128)(2,1)S(1)} all-to-all(bf16[2,4,512,128]{3,2,1,0:T(8,128)(2,1)S(1)} %broadcast_in_dim.41), channel_id=1, replica_groups=mesh['dom_0'=4,'dom_1'=4,'dom_2'=2,'band_0'=4,'band_1'=2] {'band_1'}, dimensions={0} | all-to-all | bytes 2097152 | tf_op jit(solution)/shard_map/all_to_all | solution.py:338
  103.9 0.7 gram.1
  104.6 26.1 %all_to_all.36 = bf16[16,144,128]{2,1,0:T(8,128)(2,1)S(1)} all-to-all(bf16[16,144,128]{2,1,0:T(8,128)(2,1)S(1)} %bitcast.14), channel_id=1, replica_groups=mesh['dom_0'=4,'dom_1'=4,'dom_2'=2,'band_0'=4,'band_1'=2] {'dom_0','dom_1'}, dimensions={0} | all-to-all | bytes 1179648 | tf_op jit(solution)/shard_map/all_to_all | solution.py:338
  130.7 0.1 reduce_sum.24
  130.8 13.0 %all_to_all.37 = bf16[8,144,128]{2,1,0:T(8,128)(2,1)S(1)} all-to-all(bf16[8,144,128]{2,1,0:T(8,128)(2,1)S(1)} %broadcast_in_dim.42), channel_id=1, replica_groups=mesh['dom_0'=4,'dom_1'=4,'dom_2'=2,'band_0'=4,'band_1'=2] {'dom_2','band..., dimensions={0} | all-to-all | bytes 589824 | tf_op jit(solution)/shard_map/all_to_all | solution.py:338
  143.9 0.1 broadcast_in_dim.43
  144.0 13.4 %all_to_all.38 = bf16[16,144,128]{2,1,0:T(8,128)(2,1)S(1)} all-to-all(bf16[16,144,128]{2,1,0:T(8,128)(2,1)S(1)} %broadcast_in_dim.43), channel_id=1, replica_groups=mesh['dom_0'=4,'dom_1'=4,'dom_2'=2,'band_0'=4,'band_1'=2] {'dom_0','dom_1'}, dimensions={0} | all-to-all | bytes 1179648 | tf_op jit(solution)/shard_map/all_to_all | solution.py:338
  157.4 0.1 broadcast_in_dim.44
  157.5 9.1 %all_to_all.39 = bf16[2,2304,128]{2,1,0:T(8,128)(2,1)S(1)} all-to-all(bf16[2,2304,128]{2,1,0:T(8,128)(2,1)S(1)} %broadcast_in_dim.44), channel_id=1, replica_groups=mesh['dom_0'=4,'dom_1'=4,'dom_2'=2,'band_0'=4,'band_1'=2] {'band_1'}, dimensions={0} | all-to-all | bytes 2359296 | tf_op jit(solution)/shard_map/all_to_all | solution.py:338
  166.6 5.4 %correction.1 = (bf16[4,512,128]{2,1,0:T(8,128)(2,1)S(1)}, f32[8,128]{1,0:T(8,128)S(1)}) custom-call(s32[1]{0:T(128)} %bitcast.1.core_ref, bf16[36,128,128]{2,1,0:T(8,128)(2,1)S(1)} %bitcast.13, bf16[2,4,512,128]{3,2,1,0:T(8,128)(2,1)S(1)} %all_to_all.35.rows_ref), custom_call_target="tpu_custom_call" | custom-call | flops 4000000000 | bytes 8388608 | tf_op jit(solution)/shard_map/correction/pallas_call | solution.py:457
  171.9 16.7 %all_to_all.40 = bf16[4,512,128]{2,1,0:T(8,128)(2,1)S(1)} all-to-all(bf16[4,512,128]{2,1,0:T(8,128)(2,1)S(1)} %get-tuple-element.39), channel_id=1, replica_groups=mesh['dom_0'=4,'dom_1'=4,'dom_2'=2,'band_0'=4,'band_1'=2] {'band_0'}, dimensions={0} | all-to-all | bytes 1048576 | tf_op jit(solution)/shard_map/all_to_all | solution.py:338
  188.7 1.1 rotated.1
  (13 shorter events, 0.1 us)
Async XLA Ops:
  0.0 1.5 copy-start.2
  1.4 2.3 %copy-start.1 = (s32[8,512]{1,0:T(8,128)S(1)}, s32[8,512]{1,0:T(8,128)}, u32[]{:S(2)}) copy-start(s32[8,512]{1,0:T(8,128)} %index_ref.11) | copy-start | bytes 49156
  2.4 11.4 %collective-permute-start = (bf16[256,128]{1,0:T(8,128)(2,1)S(1)}, bf16[256,128]{1,0:T(8,128)(2,1)S(1)}, u32[]{:S(2)}, u32[]{:S(2)}) collective-permute-start(bf16[256,128]{1,0:T(8,128)(2,1)S(1)} %face_rows.1), channel_id=1, source_target_pairs={{8,0},{16,8},{24,16},{32,24},{40,32},{48,40},{56,48},{64,56},{72,6... | collective-permute-start | bytes 196616 | tf_op jit(solution)/shard_map/ppermute | solution.py:334
  14.0 15.2 %collective-permute-start.1 = (f32[256,128]{1,0:T(8,128)S(1)}, f32[256,128]{1,0:T(8,128)S(1)}, u32[]{:S(2)}, u32[]{:S(2)}) collective-permute-start(f32[256,128]{1,0:T(8,128)S(1)} %returned.3), channel_id=1, source_target_pairs={{0,8},{8,16},{16,24},{24,32},{32,40},{40,48},{48,56},{56,64},{64,7... | collective-permute-start | bytes 393224 | tf_op jit(solution)/shard_map/ppermute | solution.py:334
  23.5 5.8 %copy-start.4 = (f32[2048]{0:T(1024)S(1)}, f32[2048]{0:T(1024)}, u32[]{:S(2)}) copy-start(f32[2048]{0:T(1024)} %param.6) | copy-start | bytes 24580
  23.5 6.1 %copy-start = (bf16[2048,128]{1,0:T(8,128)(2,1)S(1)}, bf16[2048,128]{1,0:T(8,128)(2,1)}, u32[]{:S(2)}) copy-start(bf16[2048,128]{1,0:T(8,128)(2,1)} %previous_ref.1) | copy-start | bytes 1572868
  29.3 3.1 %copy-start.3 = (bf16[8,512,512]{2,1,0:T(8,128)(2,1)S(1)}, bf16[8,512,512]{2,1,0:T(8,128)(2,1)}, u32[]{:S(2)}) copy-start(bf16[8,512,512]{2,1,0:T(8,128)(2,1)} %cells_ref.3) | copy-start | bytes 12582916
  31.1 9.9 %collective-permute-start.2 = (bf16[256,128]{1,0:T(8,128)(2,1)S(1)}, bf16[256,128]{1,0:T(8,128)(2,1)S(1)}, u32[]{:S(2)}, u32[]{:S(2)}) collective-permute-start(bf16[256,128]{1,0:T(8,128)(2,1)S(1)} %get-tuple-element.29), channel_id=1, source_target_pairs={{8,0},{16,8},{24,16},{32,24},{40,32},{48,40},{56,48},{64,56},{72,6... | collective-permute-start | bytes 196616 | tf_op jit(solution)/shard_map/ppermute | solution.py:334
  41.2 14.1 %collective-permute-start.3 = (f32[256,128]{1,0:T(8,128)S(1)}, f32[256,128]{1,0:T(8,128)S(1)}, u32[]{:S(2)}, u32[]{:S(2)}) collective-permute-start(f32[256,128]{1,0:T(8,128)S(1)} %returned.4), channel_id=1, source_target_pairs={{0,8},{8,16},{16,24},{24,32},{32,40},{40,48},{48,56},{56,64},{64,7... | collective-permute-start | bytes 393224 | tf_op jit(solution)/shard_map/ppermute | solution.py:334
  56.8 8.9 %collective-permute-start.4 = (bf16[256,128]{1,0:T(8,128)(2,1)S(1)}, bf16[256,128]{1,0:T(8,128)(2,1)S(1)}, u32[]{:S(2)}, u32[]{:S(2)}) collective-permute-start(bf16[256,128]{1,0:T(8,128)(2,1)S(1)} %get-tuple-element.34), channel_id=1, source_target_pairs={{8,0},{16,8},{24,16},{32,24},{40,32},{48,40},{56,48},{64,56},{72,6... | collective-permute-start | bytes 196616 | tf_op jit(solution)/shard_map/ppermute | solution.py:334
  66.0 13.2 %collective-permute-start.5 = (f32[256,128]{1,0:T(8,128)S(1)}, f32[256,128]{1,0:T(8,128)S(1)}, u32[]{:S(2)}, u32[]{:S(2)}) collective-permute-start(f32[256,128]{1,0:T(8,128)S(1)} %returned.5), channel_id=1, source_target_pairs={{0,8},{8,16},{16,24},{24,32},{32,40},{40,48},{48,56},{56,64},{64,7... | collective-permute-start | bytes 393224 | tf_op jit(solution)/shard_map/ppermute | solution.py:334
  80.5 14.5 %all-to-all-start = ((bf16[4,512,128]{2,1,0:T(8,128)(2,1)}), bf16[4,512,128]{2,1,0:T(8,128)(2,1)S(1)}, u32[]{:S(2)}, u32[]{:S(2)}) async-start(bf16[4,512,128]{2,1,0:T(8,128)(2,1)} %bitcast.2), calls=%async_computation | async-start | bytes 1048576 | tf_op jit(solution)/shard_map/all_to_all | solution.py:338

commit v8 on v7

--- a/solution.py
+++ b/solution.py
@@ -274,7 +274,7 @@
         pl.when(core_ref[0] == core)(functools.partial(blocks, core * half))
 
 
-def correct_body(nodes, core_ref, blocks_ref, rows_ref, change_ref, scale_ref, excess, first, second):
+def correct_body(nodes, core_ref, blocks_ref, rows_ref, change_ref, scale_ref, excess, power, change):
     cores, chips, own, width = rows_ref.shape
     groups = chips * cores
     states = groups * width
@@ -299,29 +299,20 @@
     scale = 1.0 / jnp.sqrt(trace / (states * nodes))
     scale_ref[...] = jnp.broadcast_to(scale, scale_ref.shape)
 
-    def at_core(rows):
-        starts = [pl.multiple_of((cores * p + core_ref[0]) * width, width) for p in range(chips)]
-        return jnp.concatenate([excess[rows, pl.ds(s, width)] for s in starts], 1)
-
-    tall = states // 4
-    parts = [slice(i * tall, (i + 1) * tall) for i in range(4)]
-    for rows in parts:
-        second[rows, :] = at_core(rows)
-    for rows in parts:
-        square = dot(excess[rows, :], second[...])
-        first[rows, :] = (0.0625 * square - 0.3125 * second[rows, :].astype(F32)).astype(BF16)
-    for rows in parts:
-        cube = dot(excess[rows, :], first[...]) + 0.375 * at_core(rows).astype(F32)
-        second[rows, :] = cube.astype(BF16)
-    for rows in parts:
-        added = dot(excess[rows, :], second[...]) - 0.5 * at_core(rows).astype(F32)
-        first[rows, :] = (added * scale).astype(BF16)
-    for p in range(own // width):
-        some = slice(p * width, (p + 1) * width)
-        every = jnp.concatenate([rows_ref[g % cores, g // cores, some, :] for g in range(groups)], 1)
-        change = dot(every, first[...]).astype(BF16)
-        for q in range(chips):
-            change_ref[q, some, :] = change[:, q * width : (q + 1) * width]
+    count = change_ref.shape[1]
+    some = pl.ds(pl.multiple_of(core_ref[0] * count, count), count)
+    for g in range(groups):
+        power[:, g * width : (g + 1) * width] = rows_ref[g % cores, g // cores, some, :]
+    for factor in (-0.5, 0.375, -0.3125, 0.0625):
+        product = dot(power[...], excess[...])
+        power[...] = product.astype(BF16)
+        if factor == -0.5:
+            change[...] = factor * product
+        else:
+            change[...] += factor * product
+    for g in range(groups):
+        part = change[:, g * width : (g + 1) * width]
+        change_ref[g] = (part * scale).astype(BF16)
 
 
 def finish_body(filtered_ref, change_ref, scale_ref, rotated_ref):
@@ -456,15 +447,15 @@
     states = bands * width
     change, scale = call(
         functools.partial(correct_body, own * domains), "correction", [IN_SMEM, IN_VMEM, IN_VMEM],
-        [shape(mine.shape, BF16), shape((8, width), F32)],
+        [shape((bands, own // bands, width), BF16), shape((8, width), F32)],
         [
             pltpu.VMEM((states, states), BF16),
-            pltpu.VMEM((states, chips * width), BF16),
-            pltpu.VMEM((states, chips * width), BF16),
+            pltpu.VMEM((own // bands, states), BF16),
+            pltpu.VMEM((own // bands, states), F32),
         ],
         4 * 10**9, 8 * 2**20,
     )(core, gram.reshape(pairs, width, width), both)
-    change = exchanged(change, CHIP).reshape(own, width)
+    change = exchanged(change, BAND).reshape(own, width)
     return call(finish_body, "rotated", [IN_VMEM] * 3, wide, [], 10**6, 3 * 2**20)(
         filtered, change, scale
     )

time: 190 us -> 188 us (0.989)
  Pallas kernels: 51.7 us -> 49.1 us
    pallas_call x1, Pallas kernels: 5.35 us -> 2.8 us  [on_device(): call(functools.partial(correct_body, own * domains), 'correction', [IN_SM...]
  transfers between devices with their start and end apart: 7 -> 7, of which waited for: 4 -> 4; matrix products, arithmetic and copies ran while one was open for 0% -> 0% of each run, Pallas kernels for 20% -> 21%
where the time goes in v8:
time: 188 us; the launch traced here: 187 us
  blocking collectives  87.4 us (46%)
  Pallas kernels  49.1 us (26%)
  starting transfers between devices  32.8 us (17%)
  waiting for transfers between devices  15.1 us (8%)
    all_to_all x6, blocking collectives, exchanged(): return lax.all_to_all(pieces, axes, split_axis=0, concat_axis=0, tiled=True)  87.4 us
    ppermute x6, starting transfers between devices, passed_along(): lax.ppermute(value, DOM, [(source, source + steps) for source in range(in...  29.2 us
    pallas_call x3, Pallas kernels, on_device(): summed = assemble(connectivity, links, products, spread, received)  17.1 us
    pallas_call x2, Pallas kernels, on_device(): products, sent = local(connectivity, links, column, scaled, cell_matrices)  12.6 us
    all_to_all x1, waiting for transfers between devices, exchanged(): return lax.all_to_all(pieces, axes, split_axis=0, concat_axis=0, tiled=True)  10.8 us
    pallas_call x1, Pallas kernels, on_device(): opening(connectivity, links, column, scaled, cell_matrices)  8.9 us
    ppermute x6, waiting for transfers between devices, passed_along(): lax.ppermute(value, DOM, [(source, source + steps) for source in range(in...  4.31 us
  transfers between devices with their start and end apart: 7, of which 4 were waited for; matrix products, arithmetic and copies ran while one was open for 0% of the time, Pallas kernels for 21%

profile of v8, /device:TPU:1, one launch (start us, length us, event | category | flops | bytes accessed | tf_op | source)
XLA Modules:
  0.0 187.5 jit_solution(1774499417028748707)
XLA Ops:
  0.0 1.4 multiply_convert_fusion
  1.4 0.0 copy-start.1
  1.4 0.1 pad_convert_fusion.scaled_ref
  1.5 0.9 face_rows.1
  2.4 1.3 collective-permute-start
  3.8 0.3 broadcast_in_dim.40.column_ref
  4.1 8.9 %opening_products.1 = (f32[4096,128]{1,0:T(8,128)S(1)}, bf16[4096,512]{1,0:T(8,128)(2,1)S(1)}, bf16[256,512]{1,0:T(8,128)(2,1)S(1)}, f32[256,128]{1,0:T(8,128)S(1)}) custom-call(s32[8,512]{1,0:T(8,128)S(1)} %copy-done.1, s32[8,4096]{1,0:T(8,128)S(1)} %broadcast_in_dim.38.links_ref, s32[2048,128]{1,0:T(8,128)S(1)} %broadcast_in_dim.40.column_ref, ...), custom_call_target="tpu_custom_call" | custom-call | flops 8000000000 | bytes 16777216 | tf_op jit(solution)/shard_map/opening_products/pallas_call | solution.py:405
  13.0 0.8 collective-permute-done.rows_ref
  13.8 0.2 returned.3
  14.0 9.5 %collective-permute-start.1 = (f32[256,128]{1,0:T(8,128)S(1)}, f32[256,128]{1,0:T(8,128)S(1)}, u32[]{:S(2)}, u32[]{:S(2)}) collective-permute-start(f32[256,128]{1,0:T(8,128)S(1)} %returned.3), channel_id=1, source_target_pairs={{0,8},{8,16},{16,24},{24,32},{32,40},{40,48},{48,56},{56,64},{64,7... | collective-permute-start | bytes 393224 | tf_op jit(solution)/shard_map/ppermute | solution.py:325
  23.5 0.0 copy-start.4
  23.5 0.0 copy-start
  23.5 5.7 %assembled.3.summed_ref = f32[2048,128]{1,0:T(8,128)S(1)} custom-call(s32[8,512]{1,0:T(8,128)S(1)} %copy-done.1, s32[8,4096]{1,0:T(8,128)S(1)} %broadcast_in_dim.38.links_ref, f32[4096,128]{1,0:T(8,128)S(1)} %get-tuple-element.23.products_ref, bf16[4096,512]{1,0:T(8,128)(2,1)S(1)} %get-tuple-element.24.spread_ref, ...), custom_call_target="tpu_custom_call" | custom-call | flops 5000000000 | bytes 16777216 | tf_op jit(solution)/shard_map/assembled/pallas_call | solution.py:411
  29.3 0.0 collective-permute-done.1.arrived_ref
  29.3 0.0 copy-start.3
  29.3 0.3 mul.8.mass_ref
  29.6 1.5 first_step.1
  31.1 1.3 collective-permute-start.2
  32.4 6.3 %local_products.2 = (f32[4096,128]{1,0:T(8,128)S(1)}, f32[256,128]{1,0:T(8,128)S(1)}) custom-call(s32[8,512]{1,0:T(8,128)S(1)} %copy-done.1, s32[8,4096]{1,0:T(8,128)S(1)} %broadcast_in_dim.38.links_ref, s32[2048,128]{1,0:T(8,128)S(1)} %broadcast_in_dim.40.column_ref, f32[2304,128]{1,0:T(8,128)S(1)} %get-tuple-element.27.scaled_ref, ...), custom_call_target="tpu_custom_call" | custom-call | flops 5000000000 | bytes 16777216 | tf_op jit(solution)/shard_map/local_products/pallas_call | solution.py:409
  38.7 2.2 %collective-permute-done.2.rows_ref = bf16[256,128]{1,0:T(8,128)(2,1)S(1)} collective-permute-done((bf16[256,128]{1,0:T(8,128)(2,1)S(1)}, bf16[256,128]{1,0:T(8,128)(2,1)S(1)}, u32[]{:S(2)}, u32[]{:S(2)}) %collective-permute-start.2) | collective-permute-done | bytes 65568 | tf_op jit(solution)/shard_map/ppermute | solution.py:325
  41.0 0.2 returned.4
  41.2 8.3 %collective-permute-start.3 = (f32[256,128]{1,0:T(8,128)S(1)}, f32[256,128]{1,0:T(8,128)S(1)}, u32[]{:S(2)}, u32[]{:S(2)}) collective-permute-start(f32[256,128]{1,0:T(8,128)S(1)} %returned.4), channel_id=1, source_target_pairs={{0,8},{8,16},{16,24},{24,32},{32,40},{40,48},{48,56},{56,64},{64,7... | collective-permute-start | bytes 393224 | tf_op jit(solution)/shard_map/ppermute | solution.py:325
  49.5 5.7 %assembled.4.summed_ref = f32[2048,128]{1,0:T(8,128)S(1)} custom-call(s32[8,512]{1,0:T(8,128)S(1)} %copy-done.1, s32[8,4096]{1,0:T(8,128)S(1)} %broadcast_in_dim.38.links_ref, f32[4096,128]{1,0:T(8,128)S(1)} %get-tuple-element.28.products_ref, bf16[4096,512]{1,0:T(8,128)(2,1)S(1)} %get-tuple-element.24.spread_ref, ...), custom_call_target="tpu_custom_call" | custom-call | flops 5000000000 | bytes 16777216 | tf_op jit(solution)/shard_map/assembled/pallas_call | solution.py:411
  55.2 0.0 collective-permute-done.3.arrived_ref
  55.2 1.6 next_step.1
  56.8 1.3 collective-permute-start.4
  58.1 6.3 %local_products.3 = (f32[4096,128]{1,0:T(8,128)S(1)}, f32[256,128]{1,0:T(8,128)S(1)}) custom-call(s32[8,512]{1,0:T(8,128)S(1)} %copy-done.1, s32[8,4096]{1,0:T(8,128)S(1)} %broadcast_in_dim.38.links_ref, s32[2048,128]{1,0:T(8,128)S(1)} %broadcast_in_dim.40.column_ref, f32[2304,128]{1,0:T(8,128)S(1)} %get-tuple-element.32.scaled_ref, ...), custom_call_target="tpu_custom_call" | custom-call | flops 5000000000 | bytes 16777216 | tf_op jit(solution)/shard_map/local_products/pallas_call | solution.py:409
  64.4 1.3 collective-permute-done.4.rows_ref
  65.7 0.2 returned.5
  66.0 7.5 %collective-permute-start.5 = (f32[256,128]{1,0:T(8,128)S(1)}, f32[256,128]{1,0:T(8,128)S(1)}, u32[]{:S(2)}, u32[]{:S(2)}) collective-permute-start(f32[256,128]{1,0:T(8,128)S(1)} %returned.5), channel_id=1, source_target_pairs={{0,8},{8,16},{16,24},{24,32},{32,40},{40,48},{48,56},{56,64},{64,7... | collective-permute-start | bytes 393224 | tf_op jit(solution)/shard_map/ppermute | solution.py:325
  73.5 5.7 %assembled.5.summed_ref = f32[2048,128]{1,0:T(8,128)S(1)} custom-call(s32[8,512]{1,0:T(8,128)S(1)} %copy-done.1, s32[8,4096]{1,0:T(8,128)S(1)} %broadcast_in_dim.38.links_ref, f32[4096,128]{1,0:T(8,128)S(1)} %get-tuple-element.33.products_ref, bf16[4096,512]{1,0:T(8,128)(2,1)S(1)} %get-tuple-element.24.spread_ref, ...), custom_call_target="tpu_custom_call" | custom-call | flops 5000000000 | bytes 16777216 | tf_op jit(solution)/shard_map/assembled/pallas_call | solution.py:411
  79.1 0.0 collective-permute-done.5.arrived_ref
  79.1 1.3 filtered.1
  80.5 3.6 %all-to-all-start = ((bf16[4,512,128]{2,1,0:T(8,128)(2,1)}), bf16[4,512,128]{2,1,0:T(8,128)(2,1)S(1)}, u32[]{:S(2)}, u32[]{:S(2)}) async-start(bf16[4,512,128]{2,1,0:T(8,128)(2,1)} %bitcast.2), calls=%async_computation | async-start | bytes 1048576 | tf_op jit(solution)/shard_map/all_to_all | solution.py:329
  84.1 10.8 %all-to-all-done = bf16[4,512,128]{2,1,0:T(8,128)(2,1)S(1)} async-done(((bf16[4,512,128]{2,1,0:T(8,128)(2,1)}), bf16[4,512,128]{2,1,0:T(8,128)(2,1)S(1)}, u32[]{:S(2)}, u32[]{:S(2)}) %all-to-all-start) | async-done | bytes 524320 | tf_op jit(solution)/shard_map/all_to_all | solution.py:329
  95.0 0.1 broadcast_in_dim.41
  95.1 8.8 %all_to_all.35.rows_ref = bf16[2,4,512,128]{3,2,1,0:T(8,128)(2,1)S(1)} all-to-all(bf16[2,4,512,128]{3,2,1,0:T(8,128)(2,1)S(1)} %broadcast_in_dim.41), channel_id=1, replica_groups=mesh['dom_0'=4,'dom_1'=4,'dom_2'=2,'band_0'=4,'band_1'=2] {'band_1'}, dimensions={0} | all-to-all | bytes 2097152 | tf_op jit(solution)/shard_map/all_to_all | solution.py:329
  103.9 0.7 gram.1
  104.6 26.1 %all_to_all.36 = bf16[16,144,128]{2,1,0:T(8,128)(2,1)S(1)} all-to-all(bf16[16,144,128]{2,1,0:T(8,128)(2,1)S(1)} %bitcast.14), channel_id=1, replica_groups=mesh['dom_0'=4,'dom_1'=4,'dom_2'=2,'band_0'=4,'band_1'=2] {'dom_0','dom_1'}, dimensions={0} | all-to-all | bytes 1179648 | tf_op jit(solution)/shard_map/all_to_all | solution.py:329
  130.7 0.1 reduce_sum.24
  130.8 13.0 %all_to_all.37 = bf16[8,144,128]{2,1,0:T(8,128)(2,1)S(1)} all-to-all(bf16[8,144,128]{2,1,0:T(8,128)(2,1)S(1)} %broadcast_in_dim.42), channel_id=1, replica_groups=mesh['dom_0'=4,'dom_1'=4,'dom_2'=2,'band_0'=4,'band_1'=2] {'dom_2','band..., dimensions={0} | all-to-all | bytes 589824 | tf_op jit(solution)/shard_map/all_to_all | solution.py:329
  143.9 0.1 broadcast_in_dim.43
  144.0 13.4 %all_to_all.38 = bf16[16,144,128]{2,1,0:T(8,128)(2,1)S(1)} all-to-all(bf16[16,144,128]{2,1,0:T(8,128)(2,1)S(1)} %broadcast_in_dim.43), channel_id=1, replica_groups=mesh['dom_0'=4,'dom_1'=4,'dom_2'=2,'band_0'=4,'band_1'=2] {'dom_0','dom_1'}, dimensions={0} | all-to-all | bytes 1179648 | tf_op jit(solution)/shard_map/all_to_all | solution.py:329
  157.4 0.1 broadcast_in_dim.44
  157.5 9.1 %all_to_all.39 = bf16[2,2304,128]{2,1,0:T(8,128)(2,1)S(1)} all-to-all(bf16[2,2304,128]{2,1,0:T(8,128)(2,1)S(1)} %broadcast_in_dim.44), channel_id=1, replica_groups=mesh['dom_0'=4,'dom_1'=4,'dom_2'=2,'band_0'=4,'band_1'=2] {'band_1'}, dimensions={0} | all-to-all | bytes 2359296 | tf_op jit(solution)/shard_map/all_to_all | solution.py:329
  166.6 2.8 %correction.1 = (bf16[8,256,128]{2,1,0:T(8,128)(2,1)S(1)}, f32[8,128]{1,0:T(8,128)S(1)}) custom-call(s32[1]{0:T(128)} %bitcast.1.core_ref, bf16[36,128,128]{2,1,0:T(8,128)(2,1)S(1)} %bitcast.13, bf16[2,4,512,128]{3,2,1,0:T(8,128)(2,1)S(1)} %all_to_all.35.rows_ref), custom_call_target="tpu_custom_call" | custom-call | flops 4000000000 | bytes 8388608 | tf_op jit(solution)/shard_map/correction/pallas_call | solution.py:448
  169.4 17.0 %all_to_all.40 = bf16[8,256,128]{2,1,0:T(8,128)(2,1)S(1)} all-to-all(bf16[8,256,128]{2,1,0:T(8,128)(2,1)S(1)} %get-tuple-element.39), channel_id=1, replica_groups=mesh['dom_0'=4,'dom_1'=4,'dom_2'=2,'band_0'=4,'band_1'=2] {'band_0','ban..., dimensions={0} | all-to-all | bytes 1048576 | tf_op jit(solution)/shard_map/all_to_all | solution.py:329
  186.4 1.1 rotated.1
  (13 shorter events, 0.1 us)
Async XLA Ops:
  0.0 1.5 copy-start.2
  1.4 2.3 %copy-start.1 = (s32[8,512]{1,0:T(8,128)S(1)}, s32[8,512]{1,0:T(8,128)}, u32[]{:S(2)}) copy-start(s32[8,512]{1,0:T(8,128)} %index_ref.11) | copy-start | bytes 49156
  2.4 11.4 %collective-permute-start = (bf16[256,128]{1,0:T(8,128)(2,1)S(1)}, bf16[256,128]{1,0:T(8,128)(2,1)S(1)}, u32[]{:S(2)}, u32[]{:S(2)}) collective-permute-start(bf16[256,128]{1,0:T(8,128)(2,1)S(1)} %face_rows.1), channel_id=1, source_target_pairs={{8,0},{16,8},{24,16},{32,24},{40,32},{48,40},{56,48},{64,56},{72,6... | collective-permute-start | bytes 196616 | tf_op jit(solution)/shard_map/ppermute | solution.py:325
  14.0 15.2 %collective-permute-start.1 = (f32[256,128]{1,0:T(8,128)S(1)}, f32[256,128]{1,0:T(8,128)S(1)}, u32[]{:S(2)}, u32[]{:S(2)}) collective-permute-start(f32[256,128]{1,0:T(8,128)S(1)} %returned.3), channel_id=1, source_target_pairs={{0,8},{8,16},{16,24},{24,32},{32,40},{40,48},{48,56},{56,64},{64,7... | collective-permute-start | bytes 393224 | tf_op jit(solution)/shard_map/ppermute | solution.py:325
  23.5 5.8 %copy-start.4 = (f32[2048]{0:T(1024)S(1)}, f32[2048]{0:T(1024)}, u32[]{:S(2)}) copy-start(f32[2048]{0:T(1024)} %param.6) | copy-start | bytes 24580
  23.5 6.1 %copy-start = (bf16[2048,128]{1,0:T(8,128)(2,1)S(1)}, bf16[2048,128]{1,0:T(8,128)(2,1)}, u32[]{:S(2)}) copy-start(bf16[2048,128]{1,0:T(8,128)(2,1)} %previous_ref.1) | copy-start | bytes 1572868
  29.3 3.1 %copy-start.3 = (bf16[8,512,512]{2,1,0:T(8,128)(2,1)S(1)}, bf16[8,512,512]{2,1,0:T(8,128)(2,1)}, u32[]{:S(2)}) copy-start(bf16[8,512,512]{2,1,0:T(8,128)(2,1)} %cells_ref.3) | copy-start | bytes 12582916
  31.1 9.8 %collective-permute-start.2 = (bf16[256,128]{1,0:T(8,128)(2,1)S(1)}, bf16[256,128]{1,0:T(8,128)(2,1)S(1)}, u32[]{:S(2)}, u32[]{:S(2)}) collective-permute-start(bf16[256,128]{1,0:T(8,128)(2,1)S(1)} %get-tuple-element.29), channel_id=1, source_target_pairs={{8,0},{16,8},{24,16},{32,24},{40,32},{48,40},{56,48},{64,56},{72,6... | collective-permute-start | bytes 196616 | tf_op jit(solution)/shard_map/ppermute | solution.py:325
  41.2 14.1 %collective-permute-start.3 = (f32[256,128]{1,0:T(8,128)S(1)}, f32[256,128]{1,0:T(8,128)S(1)}, u32[]{:S(2)}, u32[]{:S(2)}) collective-permute-start(f32[256,128]{1,0:T(8,128)S(1)} %returned.4), channel_id=1, source_target_pairs={{0,8},{8,16},{16,24},{24,32},{32,40},{40,48},{48,56},{56,64},{64,7... | collective-permute-start | bytes 393224 | tf_op jit(solution)/shard_map/ppermute | solution.py:325
  56.8 8.9 %collective-permute-start.4 = (bf16[256,128]{1,0:T(8,128)(2,1)S(1)}, bf16[256,128]{1,0:T(8,128)(2,1)S(1)}, u32[]{:S(2)}, u32[]{:S(2)}) collective-permute-start(bf16[256,128]{1,0:T(8,128)(2,1)S(1)} %get-tuple-element.34), channel_id=1, source_target_pairs={{8,0},{16,8},{24,16},{32,24},{40,32},{48,40},{56,48},{64,56},{72,6... | collective-permute-start | bytes 196616 | tf_op jit(solution)/shard_map/ppermute | solution.py:325
  66.0 13.2 %collective-permute-start.5 = (f32[256,128]{1,0:T(8,128)S(1)}, f32[256,128]{1,0:T(8,128)S(1)}, u32[]{:S(2)}, u32[]{:S(2)}) collective-permute-start(f32[256,128]{1,0:T(8,128)S(1)} %returned.5), channel_id=1, source_target_pairs={{0,8},{8,16},{16,24},{24,32},{32,40},{40,48},{48,56},{56,64},{64,7... | collective-permute-start | bytes 393224 | tf_op jit(solution)/shard_map/ppermute | solution.py:325
  80.5 14.5 %all-to-all-start = ((bf16[4,512,128]{2,1,0:T(8,128)(2,1)}), bf16[4,512,128]{2,1,0:T(8,128)(2,1)S(1)}, u32[]{:S(2)}, u32[]{:S(2)}) async-start(bf16[4,512,128]{2,1,0:T(8,128)(2,1)} %bitcast.2), calls=%async_computation | async-start | bytes 1048576 | tf_op jit(solution)/shard_map/all_to_all | solution.py:329

commit v9 on v8

--- a/solution.py
+++ b/solution.py
@@ -81,7 +81,7 @@
     extent, width = scaled_ref.shape
     copied = cells - column_ref.shape[0] // nodes
     narrow[...] = scaled_ref[...].astype(BF16)
-    steps = 4
+    steps = 2
     some = nodes // steps
     rest = column_ref.shape[0] // steps
 

time: 188 us -> 188 us (level)
  transfers between devices with their start and end apart: 7 -> 7, of which waited for: 4 -> 4; matrix products, arithmetic and copies ran while one was open for 0% -> 0% of each run, Pallas kernels for 21% -> 20%
where the time goes in v9:
time: 188 us
  blocking collectives  87.3 us (46%)
  Pallas kernels  48.9 us (26%)
  starting transfers between devices  33.1 us (18%)
  waiting for transfers between devices  15.2 us (8%)
    all_to_all x6, blocking collectives, exchanged(): return lax.all_to_all(pieces, axes, split_axis=0, concat_axis=0, tiled=True)  87.3 us
    ppermute x6, starting transfers between devices, passed_along(): lax.ppermute(value, DOM, [(source, source + steps) for source in range(in...  29.5 us
    pallas_call x3, Pallas kernels, on_device(): summed = assemble(connectivity, links, products, spread, received)  17.1 us
    pallas_call x2, Pallas kernels, on_device(): products, sent = local(connectivity, links, column, scaled, cell_matrices)  12.5 us
    all_to_all x1, waiting for transfers between devices, exchanged(): return lax.all_to_all(pieces, axes, split_axis=0, concat_axis=0, tiled=True)  10.9 us
    pallas_call x1, Pallas kernels, on_device(): opening(connectivity, links, column, scaled, cell_matrices)  8.82 us
    ppermute x6, waiting for transfers between devices, passed_along(): lax.ppermute(value, DOM, [(source, source + steps) for source in range(in...  4.31 us
  transfers between devices with their start and end apart: 7, of which 4 were waited for; matrix products, arithmetic and copies ran while one was open for 0% of the time, Pallas kernels for 20%

profile of v9, /device:TPU:1, one launch (start us, length us, event | category | flops | bytes accessed | tf_op | source)
XLA Modules:
  0.0 187.5 jit_solution(1975904335481785545)
XLA Ops:
  0.0 1.4 multiply_convert_fusion
  1.4 0.0 copy-start.1
  1.4 0.1 pad_convert_fusion.scaled_ref
  1.5 0.9 face_rows.1
  2.4 1.3 collective-permute-start
  3.8 0.3 broadcast_in_dim.40.column_ref
  4.1 8.8 %opening_products.1 = (f32[4096,128]{1,0:T(8,128)S(1)}, bf16[4096,512]{1,0:T(8,128)(2,1)S(1)}, bf16[256,512]{1,0:T(8,128)(2,1)S(1)}, f32[256,128]{1,0:T(8,128)S(1)}) custom-call(s32[8,512]{1,0:T(8,128)S(1)} %copy-done.1, s32[8,4096]{1,0:T(8,128)S(1)} %broadcast_in_dim.38.links_ref, s32[2048,128]{1,0:T(8,128)S(1)} %broadcast_in_dim.40.column_ref, ...), custom_call_target="tpu_custom_call" | custom-call | flops 8000000000 | bytes 16777216 | tf_op jit(solution)/shard_map/opening_products/pallas_call | solution.py:405
  13.0 0.9 collective-permute-done.rows_ref
  13.8 0.2 returned.3
  14.0 9.4 %collective-permute-start.1 = (f32[256,128]{1,0:T(8,128)S(1)}, f32[256,128]{1,0:T(8,128)S(1)}, u32[]{:S(2)}, u32[]{:S(2)}) collective-permute-start(f32[256,128]{1,0:T(8,128)S(1)} %returned.3), channel_id=1, source_target_pairs={{0,8},{8,16},{16,24},{24,32},{32,40},{40,48},{48,56},{56,64},{64,7... | collective-permute-start | bytes 393224 | tf_op jit(solution)/shard_map/ppermute | solution.py:325
  23.5 0.0 copy-start.4
  23.5 0.0 copy-start
  23.5 5.7 %assembled.3.summed_ref = f32[2048,128]{1,0:T(8,128)S(1)} custom-call(s32[8,512]{1,0:T(8,128)S(1)} %copy-done.1, s32[8,4096]{1,0:T(8,128)S(1)} %broadcast_in_dim.38.links_ref, f32[4096,128]{1,0:T(8,128)S(1)} %get-tuple-element.23.products_ref, bf16[4096,512]{1,0:T(8,128)(2,1)S(1)} %get-tuple-element.24.spread_ref, ...), custom_call_target="tpu_custom_call" | custom-call | flops 5000000000 | bytes 16777216 | tf_op jit(solution)/shard_map/assembled/pallas_call | solution.py:411
  29.2 0.0 collective-permute-done.1.arrived_ref
  29.2 0.0 copy-start.3
  29.2 0.3 mul.8.mass_ref
  29.6 1.5 first_step.1
  31.1 1.5 collective-permute-start.2
  32.6 6.2 %local_products.2 = (f32[4096,128]{1,0:T(8,128)S(1)}, f32[256,128]{1,0:T(8,128)S(1)}) custom-call(s32[8,512]{1,0:T(8,128)S(1)} %copy-done.1, s32[8,4096]{1,0:T(8,128)S(1)} %broadcast_in_dim.38.links_ref, s32[2048,128]{1,0:T(8,128)S(1)} %broadcast_in_dim.40.column_ref, f32[2304,128]{1,0:T(8,128)S(1)} %get-tuple-element.27.scaled_ref, ...), custom_call_target="tpu_custom_call" | custom-call | flops 5000000000 | bytes 16777216 | tf_op jit(solution)/shard_map/local_products/pallas_call | solution.py:409
  38.8 2.1 %collective-permute-done.2.rows_ref = bf16[256,128]{1,0:T(8,128)(2,1)S(1)} collective-permute-done((bf16[256,128]{1,0:T(8,128)(2,1)S(1)}, bf16[256,128]{1,0:T(8,128)(2,1)S(1)}, u32[]{:S(2)}, u32[]{:S(2)}) %collective-permute-start.2) | collective-permute-done | bytes 65568 | tf_op jit(solution)/shard_map/ppermute | solution.py:325
  40.9 0.2 returned.4
  41.1 8.1 %collective-permute-start.3 = (f32[256,128]{1,0:T(8,128)S(1)}, f32[256,128]{1,0:T(8,128)S(1)}, u32[]{:S(2)}, u32[]{:S(2)}) collective-permute-start(f32[256,128]{1,0:T(8,128)S(1)} %returned.4), channel_id=1, source_target_pairs={{0,8},{8,16},{16,24},{24,32},{32,40},{40,48},{48,56},{56,64},{64,7... | collective-permute-start | bytes 393224 | tf_op jit(solution)/shard_map/ppermute | solution.py:325
  49.3 5.7 %assembled.4.summed_ref = f32[2048,128]{1,0:T(8,128)S(1)} custom-call(s32[8,512]{1,0:T(8,128)S(1)} %copy-done.1, s32[8,4096]{1,0:T(8,128)S(1)} %broadcast_in_dim.38.links_ref, f32[4096,128]{1,0:T(8,128)S(1)} %get-tuple-element.28.products_ref, bf16[4096,512]{1,0:T(8,128)(2,1)S(1)} %get-tuple-element.24.spread_ref, ...), custom_call_target="tpu_custom_call" | custom-call | flops 5000000000 | bytes 16777216 | tf_op jit(solution)/shard_map/assembled/pallas_call | solution.py:411
  55.0 0.0 collective-permute-done.3.arrived_ref
  55.0 1.6 next_step.1
  56.6 1.3 collective-permute-start.4
  57.9 6.3 %local_products.3 = (f32[4096,128]{1,0:T(8,128)S(1)}, f32[256,128]{1,0:T(8,128)S(1)}) custom-call(s32[8,512]{1,0:T(8,128)S(1)} %copy-done.1, s32[8,4096]{1,0:T(8,128)S(1)} %broadcast_in_dim.38.links_ref, s32[2048,128]{1,0:T(8,128)S(1)} %broadcast_in_dim.40.column_ref, f32[2304,128]{1,0:T(8,128)S(1)} %get-tuple-element.32.scaled_ref, ...), custom_call_target="tpu_custom_call" | custom-call | flops 5000000000 | bytes 16777216 | tf_op jit(solution)/shard_map/local_products/pallas_call | solution.py:409
  64.1 1.4 collective-permute-done.4.rows_ref
  65.5 0.2 returned.5
  65.7 7.8 %collective-permute-start.5 = (f32[256,128]{1,0:T(8,128)S(1)}, f32[256,128]{1,0:T(8,128)S(1)}, u32[]{:S(2)}, u32[]{:S(2)}) collective-permute-start(f32[256,128]{1,0:T(8,128)S(1)} %returned.5), channel_id=1, source_target_pairs={{0,8},{8,16},{16,24},{24,32},{32,40},{40,48},{48,56},{56,64},{64,7... | collective-permute-start | bytes 393224 | tf_op jit(solution)/shard_map/ppermute | solution.py:325
  73.6 5.7 %assembled.5.summed_ref = f32[2048,128]{1,0:T(8,128)S(1)} custom-call(s32[8,512]{1,0:T(8,128)S(1)} %copy-done.1, s32[8,4096]{1,0:T(8,128)S(1)} %broadcast_in_dim.38.links_ref, f32[4096,128]{1,0:T(8,128)S(1)} %get-tuple-element.33.products_ref, bf16[4096,512]{1,0:T(8,128)(2,1)S(1)} %get-tuple-element.24.spread_ref, ...), custom_call_target="tpu_custom_call" | custom-call | flops 5000000000 | bytes 16777216 | tf_op jit(solution)/shard_map/assembled/pallas_call | solution.py:411
  79.2 0.0 collective-permute-done.5.arrived_ref
  79.2 1.3 filtered.1
  80.6 3.7 %all-to-all-start = ((bf16[4,512,128]{2,1,0:T(8,128)(2,1)}), bf16[4,512,128]{2,1,0:T(8,128)(2,1)S(1)}, u32[]{:S(2)}, u32[]{:S(2)}) async-start(bf16[4,512,128]{2,1,0:T(8,128)(2,1)} %bitcast.2), calls=%async_computation | async-start | bytes 1048576 | tf_op jit(solution)/shard_map/all_to_all | solution.py:329
  84.3 10.9 %all-to-all-done = bf16[4,512,128]{2,1,0:T(8,128)(2,1)S(1)} async-done(((bf16[4,512,128]{2,1,0:T(8,128)(2,1)}), bf16[4,512,128]{2,1,0:T(8,128)(2,1)S(1)}, u32[]{:S(2)}, u32[]{:S(2)}) %all-to-all-start) | async-done | bytes 524320 | tf_op jit(solution)/shard_map/all_to_all | solution.py:329
  95.1 0.1 broadcast_in_dim.41
  95.3 8.8 %all_to_all.35.rows_ref = bf16[2,4,512,128]{3,2,1,0:T(8,128)(2,1)S(1)} all-to-all(bf16[2,4,512,128]{3,2,1,0:T(8,128)(2,1)S(1)} %broadcast_in_dim.41), channel_id=1, replica_groups=mesh['dom_0'=4,'dom_1'=4,'dom_2'=2,'band_0'=4,'band_1'=2] {'band_1'}, dimensions={0} | all-to-all | bytes 2097152 | tf_op jit(solution)/shard_map/all_to_all | solution.py:329
  104.0 0.7 gram.1
  104.8 25.6 %all_to_all.36 = bf16[16,144,128]{2,1,0:T(8,128)(2,1)S(1)} all-to-all(bf16[16,144,128]{2,1,0:T(8,128)(2,1)S(1)} %bitcast.14), channel_id=1, replica_groups=mesh['dom_0'=4,'dom_1'=4,'dom_2'=2,'band_0'=4,'band_1'=2] {'dom_0','dom_1'}, dimensions={0} | all-to-all | bytes 1179648 | tf_op jit(solution)/shard_map/all_to_all | solution.py:329
  130.4 0.1 reduce_sum.24
  130.5 13.4 %all_to_all.37 = bf16[8,144,128]{2,1,0:T(8,128)(2,1)S(1)} all-to-all(bf16[8,144,128]{2,1,0:T(8,128)(2,1)S(1)} %broadcast_in_dim.42), channel_id=1, replica_groups=mesh['dom_0'=4,'dom_1'=4,'dom_2'=2,'band_0'=4,'band_1'=2] {'dom_2','band..., dimensions={0} | all-to-all | bytes 589824 | tf_op jit(solution)/shard_map/all_to_all | solution.py:329
  143.9 0.1 broadcast_in_dim.43
  144.0 13.4 %all_to_all.38 = bf16[16,144,128]{2,1,0:T(8,128)(2,1)S(1)} all-to-all(bf16[16,144,128]{2,1,0:T(8,128)(2,1)S(1)} %broadcast_in_dim.43), channel_id=1, replica_groups=mesh['dom_0'=4,'dom_1'=4,'dom_2'=2,'band_0'=4,'band_1'=2] {'dom_0','dom_1'}, dimensions={0} | all-to-all | bytes 1179648 | tf_op jit(solution)/shard_map/all_to_all | solution.py:329
  157.4 0.1 broadcast_in_dim.44
  157.5 9.0 %all_to_all.39 = bf16[2,2304,128]{2,1,0:T(8,128)(2,1)S(1)} all-to-all(bf16[2,2304,128]{2,1,0:T(8,128)(2,1)S(1)} %broadcast_in_dim.44), channel_id=1, replica_groups=mesh['dom_0'=4,'dom_1'=4,'dom_2'=2,'band_0'=4,'band_1'=2] {'band_1'}, dimensions={0} | all-to-all | bytes 2359296 | tf_op jit(solution)/shard_map/all_to_all | solution.py:329
  166.5 2.8 %correction.1 = (bf16[8,256,128]{2,1,0:T(8,128)(2,1)S(1)}, f32[8,128]{1,0:T(8,128)S(1)}) custom-call(s32[1]{0:T(128)} %bitcast.1.core_ref, bf16[36,128,128]{2,1,0:T(8,128)(2,1)S(1)} %bitcast.13, bf16[2,4,512,128]{3,2,1,0:T(8,128)(2,1)S(1)} %all_to_all.35.rows_ref), custom_call_target="tpu_custom_call" | custom-call | flops 4000000000 | bytes 8388608 | tf_op jit(solution)/shard_map/correction/pallas_call | solution.py:448
  169.3 17.1 %all_to_all.40 = bf16[8,256,128]{2,1,0:T(8,128)(2,1)S(1)} all-to-all(bf16[8,256,128]{2,1,0:T(8,128)(2,1)S(1)} %get-tuple-element.39), channel_id=1, replica_groups=mesh['dom_0'=4,'dom_1'=4,'dom_2'=2,'band_0'=4,'band_1'=2] {'band_0','ban..., dimensions={0} | all-to-all | bytes 1048576 | tf_op jit(solution)/shard_map/all_to_all | solution.py:329
  186.4 1.1 rotated.1
  (13 shorter events, 0.1 us)
Async XLA Ops:
  0.0 1.5 copy-start.2
  1.4 2.3 %copy-start.1 = (s32[8,512]{1,0:T(8,128)S(1)}, s32[8,512]{1,0:T(8,128)}, u32[]{:S(2)}) copy-start(s32[8,512]{1,0:T(8,128)} %index_ref.11) | copy-start | bytes 49156
  2.4 11.4 %collective-permute-start = (bf16[256,128]{1,0:T(8,128)(2,1)S(1)}, bf16[256,128]{1,0:T(8,128)(2,1)S(1)}, u32[]{:S(2)}, u32[]{:S(2)}) collective-permute-start(bf16[256,128]{1,0:T(8,128)(2,1)S(1)} %face_rows.1), channel_id=1, source_target_pairs={{8,0},{16,8},{24,16},{32,24},{40,32},{48,40},{56,48},{64,56},{72,6... | collective-permute-start | bytes 196616 | tf_op jit(solution)/shard_map/ppermute | solution.py:325
  14.0 15.2 %collective-permute-start.1 = (f32[256,128]{1,0:T(8,128)S(1)}, f32[256,128]{1,0:T(8,128)S(1)}, u32[]{:S(2)}, u32[]{:S(2)}) collective-permute-start(f32[256,128]{1,0:T(8,128)S(1)} %returned.3), channel_id=1, source_target_pairs={{0,8},{8,16},{16,24},{24,32},{32,40},{40,48},{48,56},{56,64},{64,7... | collective-permute-start | bytes 393224 | tf_op jit(solution)/shard_map/ppermute | solution.py:325
  23.5 5.8 %copy-start.4 = (f32[2048]{0:T(1024)S(1)}, f32[2048]{0:T(1024)}, u32[]{:S(2)}) copy-start(f32[2048]{0:T(1024)} %param.6) | copy-start | bytes 24580
  23.5 6.1 %copy-start = (bf16[2048,128]{1,0:T(8,128)(2,1)S(1)}, bf16[2048,128]{1,0:T(8,128)(2,1)}, u32[]{:S(2)}) copy-start(bf16[2048,128]{1,0:T(8,128)(2,1)} %previous_ref.1) | copy-start | bytes 1572868
  29.2 3.3 %copy-start.3 = (bf16[8,512,512]{2,1,0:T(8,128)(2,1)S(1)}, bf16[8,512,512]{2,1,0:T(8,128)(2,1)}, u32[]{:S(2)}) copy-start(bf16[8,512,512]{2,1,0:T(8,128)(2,1)} %cells_ref.3) | copy-start | bytes 12582916
  31.1 9.8 %collective-permute-start.2 = (bf16[256,128]{1,0:T(8,128)(2,1)S(1)}, bf16[256,128]{1,0:T(8,128)(2,1)S(1)}, u32[]{:S(2)}, u32[]{:S(2)}) collective-permute-start(bf16[256,128]{1,0:T(8,128)(2,1)S(1)} %get-tuple-element.29), channel_id=1, source_target_pairs={{8,0},{16,8},{24,16},{32,24},{40,32},{48,40},{56,48},{64,56},{72,6... | collective-permute-start | bytes 196616 | tf_op jit(solution)/shard_map/ppermute | solution.py:325
  41.1 13.9 %collective-permute-start.3 = (f32[256,128]{1,0:T(8,128)S(1)}, f32[256,128]{1,0:T(8,128)S(1)}, u32[]{:S(2)}, u32[]{:S(2)}) collective-permute-start(f32[256,128]{1,0:T(8,128)S(1)} %returned.4), channel_id=1, source_target_pairs={{0,8},{8,16},{16,24},{24,32},{32,40},{40,48},{48,56},{56,64},{64,7... | collective-permute-start | bytes 393224 | tf_op jit(solution)/shard_map/ppermute | solution.py:325
  56.6 8.9 %collective-permute-start.4 = (bf16[256,128]{1,0:T(8,128)(2,1)S(1)}, bf16[256,128]{1,0:T(8,128)(2,1)S(1)}, u32[]{:S(2)}, u32[]{:S(2)}) collective-permute-start(bf16[256,128]{1,0:T(8,128)(2,1)S(1)} %get-tuple-element.34), channel_id=1, source_target_pairs={{8,0},{16,8},{24,16},{32,24},{40,32},{48,40},{56,48},{64,56},{72,6... | collective-permute-start | bytes 196616 | tf_op jit(solution)/shard_map/ppermute | solution.py:325
  65.7 13.5 %collective-permute-start.5 = (f32[256,128]{1,0:T(8,128)S(1)}, f32[256,128]{1,0:T(8,128)S(1)}, u32[]{:S(2)}, u32[]{:S(2)}) collective-permute-start(f32[256,128]{1,0:T(8,128)S(1)} %returned.5), channel_id=1, source_target_pairs={{0,8},{8,16},{16,24},{24,32},{32,40},{40,48},{48,56},{56,64},{64,7... | collective-permute-start | bytes 393224 | tf_op jit(solution)/shard_map/ppermute | solution.py:325
  80.6 14.6 %all-to-all-start = ((bf16[4,512,128]{2,1,0:T(8,128)(2,1)}), bf16[4,512,128]{2,1,0:T(8,128)(2,1)S(1)}, u32[]{:S(2)}, u32[]{:S(2)}) async-start(bf16[4,512,128]{2,1,0:T(8,128)(2,1)} %bitcast.2), calls=%async_computation | async-start | bytes 1048576 | tf_op jit(solution)/shard_map/all_to_all | solution.py:329
